TPU v7x, 32 devices: a whole 2x2x4 slice. The times are simulated.
32 devices in a mesh: ctx: 4 (over z), exp: 8 (over y, x, core).
Axes of the slice: x: 2, y: 2, z: 4, core: 2. Of those that a mesh axis runs over, the one named last changes fastest.
Arguments:
- queries: bfloat16 [256, 3072], P('ctx', 'exp'), may hold values from -8 to 8
- keys_values: bfloat16 [2, 256, 512], P(None, 'ctx', 'exp'), may hold values from -8 to 8
- residual: bfloat16 [256, 6144], P(('ctx', 'exp')), may hold values from -12 to 12
- out_weight: bfloat16 [3072, 6144], P('exp', 'ctx'), may hold values from -0.109375 to 0.109375
- norm_gain: float32 [6144], replicated, may hold values from 0.5 to 2
- routes: int32 [256, 4], P(('ctx', 'exp')), may hold values from 0 to 7, as said below
- route_weight: float32 [256, 4], P(('ctx', 'exp')), may hold values from 0.1 to 1
- gate_weight: bfloat16 [8, 6144, 5376], P('exp', None, 'ctx'), may hold values from -0.078125 to 0.078125
- up_weight: bfloat16 [8, 6144, 5376], P('exp', None, 'ctx'), may hold values from -0.078125 to 0.078125
- down_weight: bfloat16 [8, 5376, 6144], P('exp', 'ctx'), may hold values from -0.078125 to 0.078125
Outputs:
- layer_out: bfloat16 [256, 6144], P(('ctx', 'exp'))
Inputs may be any that keep to these rules, and one draw needn't show every extreme that they name: `routes`: each row names 4 different experts. Within each aligned block of 8 rows (the rows of one device) no expert is named by more than 8 rows, and one expert is named by exactly 8 rows in every block.
All inputs are finite; a program needn't handle non-finite values.
Results may differ from a plain program's by a relative error of at most 0.025.
Values may be sent and summed in bfloat16 or wider, within the bound.
No kernel may reach another device: no remote copies, remote signals or barrier semaphores. Data moves between devices by JAX's collectives and lax.ppermute only.
A program may use at most 128 MiB of HBM per device.

v0:
```python
import functools
import math

import jax
import jax.numpy as jnp
from jax import lax
from jax.experimental import pallas as pl
from jax.experimental.pallas import tpu as pltpu
from jax.sharding import PartitionSpec as P

HD = 128
EXTRA = 128
SPLIT = 3
FIRST = 8
MIB = 1024 * 1024
F32 = jnp.float32
BF16 = jnp.bfloat16
WHOLE = pl.BlockSpec(memory_space=pltpu.VMEM)
IN_HBM = pl.BlockSpec(memory_space=pltpu.HBM)


def swap(value, axis, mask):
    return lax.ppermute(value, axis, [(i, i ^ mask) for i in range(lax.axis_size(axis))])


def call(kernel, out_shape, operands, in_specs, scratch=(), limit=16):
    return pl.pallas_call(
        kernel,
        out_shape=out_shape,
        in_specs=in_specs,
        out_specs=jax.tree.map(lambda _: WHOLE, out_shape),
        scratch_shapes=list(scratch),
        compiler_params=pltpu.CompilerParams(vmem_limit_bytes=limit * MIB),
    )(*operands)


def shape(dims, dtype):
    return jax.ShapeDtypeStruct(tuple(dims), dtype)


def attend_kernel(C, E, heads, *refs):
    messages, mates, out_weight, mate_out, own_out, projected = refs[:C], *refs[C:]
    ctx, exp = lax.axis_index("ctx"), lax.axis_index("exp")
    token_rows = mate_out.shape[2]
    rows = E * token_rows
    seq = rows * C
    blocks = [
        m[:E].astype(F32).reshape(rows, m.shape[2]).astype(BF16) for m in messages
    ]
    width = heads * HD
    half = HD // 2
    lower = (exp & 1) == 0

    other_half = mates[...].astype(F32).reshape(seq, HD).astype(BF16)

    def joined(start):
        first = width + start
        own = jnp.concatenate([b[:, first : first + half] for b in blocks], axis=0)
        mate = other_half[:, start : start + half]
        both = jnp.concatenate([own, mate], axis=1)
        other = jnp.concatenate([mate, own], axis=1)
        return jnp.where(lower, both, other)

    keys = joined(0)
    values = joined(half)
    shift = rows.bit_length() - 1
    column = lax.broadcasted_iota(jnp.int32, (rows, seq), 1)
    key_position = ((column >> shift) ^ ctx) * rows + (column & (rows - 1))
    row = lax.broadcasted_iota(jnp.int32, (rows, seq), 0)
    parts = []
    for k in range(C):
        allowed = key_position <= (ctx ^ k) * rows + row
        block_parts = []
        for h in range(heads):
            q = blocks[k][:, h * HD : (h + 1) * HD]
            scores = lax.dot_general(
                q, keys, (((1,), (1,)), ((), ())), preferred_element_type=F32
            ) * (1.0 / math.sqrt(HD))
            scores = jnp.where(allowed, scores, -jnp.inf)
            top = jnp.max(scores, axis=1, keepdims=True)
            weights = jnp.exp(scores - top)
            total = jnp.sum(weights, axis=1, keepdims=True)
            high = weights.astype(BF16)
            low = (weights - high.astype(F32)).astype(BF16)
            summed = jnp.dot(high, values, preferred_element_type=F32) + jnp.dot(
                low, values, preferred_element_type=F32
            )
            block_parts.append((summed / total).astype(BF16))
        parts.append(jnp.concatenate(block_parts, axis=1))
    attended = jnp.concatenate(parts, axis=0)
    projected[...] = jnp.dot(attended, out_weight[...], preferred_element_type=F32)
    for p in range(E):
        for j in range(C):
            start = pl.multiple_of(((ctx ^ j) * E + (exp ^ p)) * token_rows, token_rows)
            piece = projected[pl.ds(start, token_rows), :]
            if p & 1:
                mate_out[p >> 1, j] = piece.astype(BF16)
            else:
                own_out[p >> 1, j] = piece


def mate_sum_kernel(own, received, kept, *sent):
    kept[...] = own[0] + received[0].astype(F32)
    for p, out in enumerate(sent):
        out[...] = (own[p + 1] + received[p + 1].astype(F32)).astype(BF16)


def message_kernel(C, E, queries_in, own_in, residual_in, *refs):
    messages = refs[:C]
    queries, own, residual, sems = refs[C:]
    pairs = [(queries_in, queries), (own_in, own), (residual_in, residual)]
    loads = [pltpu.make_async_copy(a, b, sems.at[i]) for i, (a, b) in enumerate(pairs)]
    for load in loads:
        load.start()
    for load in loads:
        load.wait()
    token_rows, wide = messages[0].shape[1:]
    cols = residual.shape[1] // C
    parts = [queries[...], own[0], own[1]]
    bundle = jnp.concatenate([part.astype(F32) for part in parts], axis=1)
    bundle = bundle.reshape(E, token_rows, wide).astype(BF16)
    ctx = lax.axis_index("ctx")
    for k, out in enumerate(messages):
        out[:E] = bundle
        first = (ctx ^ k) * cols
        for i in range(out.shape[0] - E):
            width = min(wide, cols - i * wide)
            at = pl.ds(pl.multiple_of(first + i * wide, 128), width)
            out[E + i, :, :width] = residual[:, at]


def keep_kernel(after, out_weight, gain, weight_out, gain_out):
    weight_out[...] = out_weight[...]
    gain_out[...] = gain[...]


def halves_kernel(C, E, *refs):
    for k in range(C):
        refs[-1][k] = refs[k][:E, :, refs[k].shape[2] - HD :]


def split_terms(value):
    terms = []
    for _ in range(SPLIT):
        term = value.astype(BF16).astype(F32)
        terms.append(term)
        value = value - term
    return terms


def plane_sum_kernel(C, E, count, *refs):
    own, received, messages = refs[0], refs[1 : 1 + count], refs[1 + count : 1 + count + C]
    extra, out = refs[1 + count + C :]
    cols = own.shape[2]
    wide = messages[0].shape[2]
    lane = lax.broadcasted_iota(jnp.int32, (own.shape[1], EXTRA), 1)
    for k in range(C):
        j = lax.axis_index("ctx") ^ k
        pieces = [
            messages[k][E + i, :, : min(wide, cols - i * wide)].astype(F32)
            for i in range(messages[k].shape[0] - E)
        ]
        total = own[j] + jnp.concatenate(pieces, axis=1)
        for piece in received:
            total = total + piece[j].astype(F32)
        mean = jnp.sum(total, axis=1, keepdims=True) * (1.0 / cols)
        centered = total - mean
        squares = jnp.sum(centered * centered, axis=1, keepdims=True)
        out[j, :, :cols] = centered.astype(BF16)
        tail = jnp.zeros(lane.shape, F32) if k else extra[...].astype(F32)
        for i, term in enumerate(split_terms(mean) + split_terms(squares)):
            tail = jnp.where(lane == i, term, tail)
        out[j, :, cols:] = tail.astype(BF16)


def pack_kernel(plan, *refs):
    ins, outs = refs[: -len(plan)], refs[-len(plan) :]
    for out, sources in zip(outs, plan):
        for i, (at, place) in enumerate(sources):
            value = ins[at][...] if place is None else ins[at][place]
            if len(sources) == 1:
                out[...] = value
            else:
                out[i] = value


def pack(plan, arrays, tail, after=()):
    return call(
        functools.partial(pack_kernel, plan),
        [shape(tail if len(p) == 1 else (len(p), *tail), BF16) for p in plan],
        [*arrays, *after],
        [WHOLE] * (len(arrays) + len(after)),
    )


def spread_over_plane(arrays, sources, orders, chips, after):
    tail = arrays[0].shape[-3:]
    holds = [{0: source} for source in sources]
    arrays = list(arrays)
    for step in range(len(orders[0])):
        plan = [[hold[p] for p in sorted(hold)] for hold in holds]
        if step == 0 and len(arrays) == 2:
            sends = arrays[:]
        else:
            sends = pack(plan, arrays, tail, after)
            after = []
        for hold, order, send in zip(holds, orders, sends):
            at = len(arrays)
            arrays.append(swap(send, "exp", 1 << order[step]))
            far = 1 << (order[step] - 1)
            for i, p in enumerate(sorted(hold)):
                hold[p | far] = (at, None if step == 0 else i)
    (packed,) = pack([[hold[p] for hold in holds for p in range(chips)]], arrays, tail)
    return packed, sends


def expert_kernel(C, E, per_block, width, columns, *refs):
    groups = C // 2
    packed = refs[: 2 * groups]
    gain, gate, up, down = refs[2 * groups : 2 * groups + 4]
    outs = refs[2 * groups + 4 : 4 * groups + 4]
    hidden = refs[4 * groups + 4]
    gate_sum, up_sum, activated, piece, shift, spread, scale = refs[4 * groups + 5 : -5]
    gate_slots, up_slots, down_slots, up_sems, down_sems = refs[-5:]
    step = pl.program_id(0)
    ctx, exp = lax.axis_index("ctx"), lax.axis_index("exp")
    chips = E // 2
    token_rows = packed[0].shape[2]
    cols = packed[0].shape[3] - EXTRA
    half_rows = chips * C * token_rows
    features = hidden.shape[1]
    up_steps = C * per_block
    down_steps = features // columns
    ahead, down_ahead = gate_slots.shape[0], down_slots.shape[0]

    def up_copies(i, slot):
        at = pl.ds(pl.multiple_of(i * width, 128), width)
        return [
            pltpu.make_async_copy(gate.at[0, :, at], gate_slots.at[slot], up_sems.at[0, slot]),
            pltpu.make_async_copy(up.at[0, :, at], up_slots.at[slot], up_sems.at[1, slot]),
        ]

    def down_copy(i, slot):
        at = pl.ds(pl.multiple_of(i * columns, 128), columns)
        return pltpu.make_async_copy(down.at[0, :, at], down_slots.at[slot], down_sems.at[slot])

    @pl.when(step == 0)
    def _():
        for i in range(ahead):
            for copy in up_copies(i, i):
                copy.start()

    @pl.when(step < up_steps)
    def _():
        for copy in up_copies(step, step % ahead):
            copy.wait()

    @pl.when(step >= up_steps)
    def _():
        done = step - up_steps
        down_copy(done, done % down_ahead).wait()

    def read(g, s, at):
        parts = [
            packed[side * groups + g][pl.ds(s * chips, chips), :, :, at] for side in range(2)
        ]
        parts = [part.astype(F32).reshape(half_rows, part.shape[-1]) for part in parts]
        return jnp.concatenate(parts, axis=0)

    @pl.when(step == 0)
    def _():
        tails = [read(k // 2, k % 2, slice(cols, cols + EXTRA)) for k in range(C)]
        lane = lax.broadcasted_iota(jnp.int32, tails[0].shape, 1)

        def pick(tail, wanted):
            return jnp.sum(jnp.where(wanted, tail, 0.0), axis=1, keepdims=True)

        means = [pick(tail, lane < SPLIT) for tail in tails]
        squares = [pick(tail, (lane >= SPLIT) & (lane < 2 * SPLIT)) for tail in tails]
        mean = sum(means) * (1.0 / C)
        deviation = sum(squares) + cols * sum((m - mean) * (m - mean) for m in means)
        spread[...] = lax.rsqrt(deviation * (1.0 / features) + 1e-05)
        for k in range(C):
            shift[k, 0] = means[k]
            shift[k, 1] = means[k] - mean
        first = lane - FIRST
        wanted = (first >= 0) & ((first & (E - 1)) == exp) & (first < SPLIT * E)
        scale[...] = sum(pick(tail, wanted) for tail in tails)

    for g in range(groups):
        block_at = step // per_block
        k = block_at ^ ctx

        @pl.when((step < up_steps) & (k // 2 == g))
        def _():
            part = step % per_block
            s = k % 2
            at = pl.ds(pl.multiple_of(part * width, 128), width)
            place_at = pl.multiple_of(block_at * cols + part * width, 128)
            centered = read(g, s, at)
            value = (centered + shift[k, 1]) * spread[...] * gain[:, pl.ds(place_at, width)]
            block = value.astype(BF16)
            own = packed[g][s * chips, ctx, :, at].astype(F32)
            own_mean = shift[k, 0, pl.ds(pl.multiple_of(ctx * token_rows, token_rows), token_rows)]
            hidden[:, pl.ds(place_at, width)] = own + own_mean
            turned_dot = functools.partial(
                lax.dot_general,
                dimension_numbers=(((1,), (1,)), ((), ())),
                preferred_element_type=F32,
            )

            @pl.when(step == 0)
            def _():
                gate_sum[...] = turned_dot(block, gate_slots[step % ahead])
                up_sum[...] = turned_dot(block, up_slots[step % ahead])

            @pl.when(step > 0)
            def _():
                gate_sum[...] += turned_dot(block, gate_slots[step % ahead])
                up_sum[...] += turned_dot(block, up_slots[step % ahead])

    @pl.when(step + ahead < up_steps)
    def _():
        for copy in up_copies(step + ahead, step % ahead):
            copy.start()

    first = step + ahead - up_steps

    @pl.when((first >= 0) & (first < down_ahead))
    def _():
        down_copy(first, first).start()

    @pl.when(step == up_steps)
    def _():
        value = gate_sum[...]
        value = value / (1.0 + jnp.exp(-value)) * up_sum[...]
        activated[...] = value.astype(BF16)

    @pl.when(step >= up_steps)
    def _():
        done = step - up_steps
        block = down_slots[done % down_ahead]
        piece[...] = jnp.dot(activated[...], block, preferred_element_type=F32) * scale[...]

        @pl.when(done + down_ahead < down_steps)
        def _():
            down_copy(done + down_ahead, done % down_ahead).start()

        for g in range(groups):
            for side in range(2):
                for s in range(2):
                    for p in range(chips):
                        row = ((side * chips + p) * C + (ctx ^ (2 * g + s))) * token_rows
                        at = pl.ds(pl.multiple_of(row, token_rows), token_rows)
                        outs[side * groups + g][s * chips + p] = piece[at, :].astype(BF16)


def largest_part(size, most, unit):
    return max(c for c in range(unit, most + 1, unit) if size % c == 0)


def run_experts(packed, gain, gate_weight, up_weight, down_weight, C, E):
    count = len(packed)
    pieces, _, token_rows, wide = packed[0].shape
    cols = wide - EXTRA
    features = cols * C
    units = gate_weight.shape[2]
    total = C * E * token_rows
    small = total <= 256
    width = largest_part(cols, 768 if small else 384, 128)
    columns = largest_part(features, 1024 if small else 384, 128)
    per_block = cols // width
    up_steps = C * per_block
    down_steps = features // columns

    def column_block(i):
        return (0, 0, jnp.maximum(i - up_steps, 0))

    def whole(*dims):
        return pl.BlockSpec(dims, lambda i: (0,) * len(dims), pipeline_mode=pl.Buffered(1))

    ahead = 4 if small else 2
    down_ahead = 3 if small else 2
    *outs, hidden = pl.pallas_call(
        functools.partial(expert_kernel, C, E, per_block, width, columns),
        out_shape=[shape((pieces, token_rows, features), BF16) for _ in packed]
        + [shape((token_rows, features), F32)],
        grid=(up_steps + down_steps,),
        in_specs=[whole(*packed[0].shape) for _ in packed]
        + [whole(1, features), IN_HBM, IN_HBM, IN_HBM],
        out_specs=[pl.BlockSpec((pieces, token_rows, columns), column_block) for _ in packed]
        + [pl.BlockSpec((token_rows, features), lambda i: (0, 0))],
        scratch_shapes=[
            pltpu.VMEM((total, units), F32),
            pltpu.VMEM((total, units), F32),
            pltpu.VMEM((total, units), BF16),
            pltpu.VMEM((total, columns), F32),
            pltpu.VMEM((C, 2, total, 1), F32),
            pltpu.VMEM((total, 1), F32),
            pltpu.VMEM((total, 1), F32),
            pltpu.VMEM((ahead, units, width), BF16),
            pltpu.VMEM((ahead, units, width), BF16),
            pltpu.VMEM((down_ahead, units, columns), BF16),
            pltpu.SemaphoreType.DMA((2, ahead)),
            pltpu.SemaphoreType.DMA((down_ahead,)),
        ],
        compiler_params=pltpu.CompilerParams(
            vmem_limit_bytes=(42 if small else 58) * MIB,
            dimension_semantics=("arbitrary",),
        ),
        cost_estimate=pl.CostEstimate(
            flops=6 * total * features * units,
            bytes_accessed=6 * features * units + 4 * total * features,
            transcendentals=total * units,
        ),
    )(
        *packed,
        gain,
        jnp.swapaxes(gate_weight, 1, 2),
        jnp.swapaxes(up_weight, 1, 2),
        down_weight,
    )
    return outs, hidden


def fold_kernel(plan, *refs):
    ins, outs = refs[: -len(plan)], refs[-len(plan) :]
    for out, places in zip(outs, plan):
        for i, parts in enumerate(places):
            out[i] = sum(ins[at][place].astype(F32) for at, place in parts).astype(BF16)


def fold(plan, operands):
    tail = operands[0].shape[1:]
    return call(
        functools.partial(fold_kernel, plan),
        [shape((len(places), *tail), BF16) for places in plan],
        operands,
        [WHOLE] * len(operands),
    )


def sum_over_plane(own, received, orders):
    chips = own.shape[0] // 2
    operands = [own, received]
    holds = [
        {p: [(0, s * chips + p), (1, s * chips + p)] for p in range(chips)}
        for s in range(len(orders))
    ]
    for step in range(len(orders[0])):
        far = [1 << (order[step] - 1) for order in orders]
        sent = [[p for p in sorted(hold) if p & f] for hold, f in zip(holds, far)]
        kept = [[p for p in sorted(hold) if not p & f] for hold, f in zip(holds, far)]
        plan = [[hold[p] for p in ps] for hold, ps in zip(holds * 2, sent + kept)]
        *sends, keep0, keep1 = fold(plan, operands)
        got = [swap(value, "exp", 1 << order[step]) for value, order in zip(sends, orders)]
        operands = [keep0, got[0], keep1, got[1]]
        holds = [
            {p: [(2 * s, i), (2 * s + 1, i)] for i, p in enumerate(kept[s])}
            for s in range(len(orders))
        ]
    return fold([[hold[0]] for hold in holds], operands)


def on_device(
    queries,
    keys_values,
    residual,
    out_weight,
    norm_gain,
    routes,
    route_weight,
    gate_weight,
    up_weight,
    down_weight,
):
    C = lax.axis_size("ctx")
    E = lax.axis_size("exp")
    chips = E // 2
    chip_bits = list(range(1, E.bit_length() - 1))
    heads = queries.shape[1] // HD
    seq = queries.shape[0] * C
    token_rows, features = residual.shape
    cols = out_weight.shape[1]
    wide = queries.shape[1] + HD
    slots = E + -(-cols // wide)
    sent = call(
        functools.partial(message_kernel, C, E),
        [shape((slots, token_rows, wide), BF16)] * C,
        [queries, keys_values, residual],
        [IN_HBM] * 3,
        [
            pltpu.VMEM(queries.shape, BF16),
            pltpu.VMEM(keys_values.shape, BF16),
            pltpu.VMEM(residual.shape, BF16),
            pltpu.SemaphoreType.DMA((3,)),
        ],
        limit=60,
    )
    messages = [swap(piece, "ctx", k) if k else piece for k, piece in enumerate(sent)]
    weight, gain = call(
        keep_kernel,
        [shape(out_weight.shape, BF16), shape((1, features), F32)],
        [sent[0], out_weight, norm_gain.reshape(1, -1)],
        [WHOLE] * 3,
    )
    (halves,) = call(
        functools.partial(halves_kernel, C, E),
        [shape((C, E, token_rows, HD), BF16)],
        [*messages, weight, gain],
        [WHOLE] * (C + 2),
    )

    experts = jnp.arange(E, dtype=jnp.int32)
    left = jnp.sum(jnp.where(routes[:, :, None] == experts, route_weight[:, :, None], 0.0), axis=1)
    terms = []
    for _ in range(SPLIT):
        term = lax.reduce_precision(left, 8, 7)
        terms.append(term.astype(BF16))
        left = left - term
    extra = jnp.pad(
        jnp.concatenate(terms, axis=1), ((0, 0), (FIRST, EXTRA - FIRST - SPLIT * E))
    )

    mate_part, own_part = call(
        functools.partial(attend_kernel, C, E, heads),
        [
            shape((chips, C, token_rows, cols), BF16),
            shape((chips, C, token_rows, cols), F32),
        ],
        [*messages, swap(halves, "exp", 1), weight],
        [WHOLE] * (C + 2),
        [pltpu.VMEM((seq, cols), F32)],
        limit=16 if seq <= 256 else 56,
    )

    kept, *sent = call(
        mate_sum_kernel,
        [shape((C, token_rows, cols), F32)] + [shape((C, token_rows, cols), BF16)] * (chips - 1),
        [own_part, swap(mate_part, "exp", 1)],
        [WHOLE, WHOLE],
    )
    received = [swap(piece, "exp", (p + 1) << 1) for p, piece in enumerate(sent)]
    (rows,) = call(
        functools.partial(plane_sum_kernel, C, E, chips - 1),
        [shape((C, token_rows, cols + EXTRA), BF16)],
        [kept, *received, *messages, extra],
        [WHOLE] * (chips + C + 1),
    )

    orders = (chip_bits[::-1], chip_bits)
    near = [rows, swap(rows, "ctx", 1)]
    (pair,) = pack([[(0, None), (1, None)]], near, rows.shape)
    pairs = [pair]
    for bit in range(1, C.bit_length() - 1):
        pairs += [swap(value, "ctx", 1 << bit) for value in pairs]
    group, sends = spread_over_plane(near, [(0, None), (1, None)], orders, chips, [])
    packed = [group]
    for value in pairs[1:]:
        group, sends = spread_over_plane([value], [(0, 0), (0, 1)], orders, chips, sends)
        packed.append(group)
    packed += [swap(group, "exp", 1) for group in packed]

    outs, hidden = run_experts(packed, gain, gate_weight, up_weight, down_weight, C, E)

    count = C // 2
    shards = [None] * C
    for g in reversed(range(count)):
        received = swap(outs[count + g], "exp", 1)
        shards[2 * g : 2 * g + 2] = sum_over_plane(outs[g], received, orders[::-1])
    total = hidden
    for k, shard in enumerate(shards):
        total = total + (swap(shard, "ctx", k) if k else shard)[0].astype(F32)
    return total.astype(BF16)


def solution(mesh):
    in_specs = (
        P("ctx", "exp"),
        P(None, "ctx", "exp"),
        P(("ctx", "exp"), None),
        P("exp", "ctx"),
        P(),
        P(("ctx", "exp"), None),
        P(("ctx", "exp"), None),
        P("exp", None, "ctx"),
        P("exp", None, "ctx"),
        P("exp", "ctx", None),
    )
    out_specs = P(("ctx", "exp"), None)
    return jax.shard_map(
        on_device, mesh=mesh, in_specs=in_specs, out_specs=out_specs, check_vma=False
    )
```

profile of v0, /device:TPU:0, one launch (start us, length us, event | category | flops | bytes accessed | tf_op | source)
XLA Modules:
  0.0 115.2 jit_solution(10570992827976175979)
XLA Ops:
  0.0 1.8 %shard_map.100 = (bf16[11,8,512]{2,1,0:T(8,128)(2,1)}, bf16[11,8,512]{2,1,0:T(8,128)(2,1)}, bf16[11,8,512]{2,1,0:T(8,128)(2,1)}, bf16[11,8,512]{2,1,0:T(8,128)(2,1)}) custom-call(bf16[64,384]{1,0:T(8,128)(2,1)} %queries_in.1, bf16[2,64,64]{2,1,0:T(8,128)(2,1)} %own_in.1, bf16[8,6144]{1,0:T(8,128)(2,1)} %residual_in.1), custom_call_target="tpu_custom_call" | custom-call | tf_op jit(solution)/shard_map/pallas_call | solution.py:27
  1.8 3.1 %collective-permute-start = (bf16[11,8,512]{2,1,0:T(8,128)(2,1)}, bf16[11,8,512]{2,1,0:T(8,128)(2,1)S(1)}, u32[]{:S(2)}, u32[]{:S(2)}) collective-permute-start(bf16[11,8,512]{2,1,0:T(8,128)(2,1)} %get-tuple-element.49), channel_id=1, source_target_pairs={{0,8},{8,0},{16,24},{24,16},{1,9},{9,1},{17,25},{25,17},{2,10},{10... | collective-permute-start | bytes 270344 | tf_op jit(solution)/shard_map/ppermute | solution.py:23
  4.9 2.6 %collective-permute-start.1 = (bf16[11,8,512]{2,1,0:T(8,128)(2,1)}, bf16[11,8,512]{2,1,0:T(8,128)(2,1)S(1)}, u32[]{:S(2)}, u32[]{:S(2)}) collective-permute-start(bf16[11,8,512]{2,1,0:T(8,128)(2,1)} %get-tuple-element.50), channel_id=1, source_target_pairs={{0,16},{8,24},{16,0},{24,8},{1,17},{9,25},{17,1},{25,9},{2,18},{10... | collective-permute-start | bytes 270344 | tf_op jit(solution)/shard_map/ppermute | solution.py:23
  8.4 1.3 %copy-done.2 = bf16[384,1536]{1,0:T(8,128)(2,1)S(1)} copy-done((bf16[384,1536]{1,0:T(8,128)(2,1)S(1)}, bf16[384,1536]{1,0:T(8,128)(2,1)}, u32[]{:S(2)}) %copy-start.2) | copy-done | bytes 1179672
  10.4 4.4 %collective-permute-done.1.refs_2_.refs_6_ = bf16[11,8,512]{2,1,0:T(8,128)(2,1)S(1)} collective-permute-done((bf16[11,8,512]{2,1,0:T(8,128)(2,1)}, bf16[11,8,512]{2,1,0:T(8,128)(2,1)S(1)}, u32[]{:S(2)}, u32[]{:S(2)}) %collective-permute-start.1) | collective-permute-done | bytes 90144 | tf_op jit(solution)/shard_map/ppermute | solution.py:23
  16.2 1.4 %shard_map.103 = (bf16[4,4,8,1536]{3,2,1,0:T(8,128)(2,1)S(1)}, f32[4,4,8,1536]{3,2,1,0:T(8,128)S(1)}) custom-call(bf16[11,8,512]{2,1,0:T(8,128)(2,1)S(1)} %copy-done, bf16[11,8,512]{2,1,0:T(8,128)(2,1)S(1)} %collective-permute-done.refs_1_.refs_5_, bf16[11,8,512]{2,1,0:T(8,128)(2,1)S(1)} %collective-permute-done.1.refs_2_.refs_6_, ...), custom_call_target="tpu_custom_call" | custom-call | tf_op jit(solution)/shard_map/pallas_call | solution.py:27
  19.5 1.6 %collective-permute-start.5 = (bf16[4,8,1536]{2,1,0:T(8,128)(2,1)S(1)}, bf16[4,8,1536]{2,1,0:T(8,128)(2,1)S(1)}, u32[]{:S(2)}, u32[]{:S(2)}) collective-permute-start(bf16[4,8,1536]{2,1,0:T(8,128)(2,1)S(1)} %get-tuple-element.57), channel_id=1, source_target_pairs={{0,2},{1,3},{2,0},{3,1},{4,6},{5,7},{6,4},{7,5},{8,10},{9,11},{10,... | collective-permute-start | bytes 294920 | tf_op jit(solution)/shard_map/ppermute | solution.py:23
  21.1 1.5 %collective-permute-start.6 = (bf16[4,8,1536]{2,1,0:T(8,128)(2,1)S(1)}, bf16[4,8,1536]{2,1,0:T(8,128)(2,1)S(1)}, u32[]{:S(2)}, u32[]{:S(2)}) collective-permute-start(bf16[4,8,1536]{2,1,0:T(8,128)(2,1)S(1)} %get-tuple-element.58), channel_id=1, source_target_pairs={{0,4},{1,5},{2,6},{3,7},{4,0},{5,1},{6,2},{7,3},{8,12},{9,13},{10,... | collective-permute-start | bytes 294920 | tf_op jit(solution)/shard_map/ppermute | solution.py:23
  23.1 1.3 %collective-permute-done.5.refs_1_ = bf16[4,8,1536]{2,1,0:T(8,128)(2,1)S(1)} collective-permute-done((bf16[4,8,1536]{2,1,0:T(8,128)(2,1)S(1)}, bf16[4,8,1536]{2,1,0:T(8,128)(2,1)S(1)}, u32[]{:S(2)}, u32[]{:S(2)}) %collective-permute-start.5) | collective-permute-done | bytes 98336 | tf_op jit(solution)/shard_map/ppermute | solution.py:23
  24.4 2.4 %collective-permute-done.6.refs_2_ = bf16[4,8,1536]{2,1,0:T(8,128)(2,1)S(1)} collective-permute-done((bf16[4,8,1536]{2,1,0:T(8,128)(2,1)S(1)}, bf16[4,8,1536]{2,1,0:T(8,128)(2,1)S(1)}, u32[]{:S(2)}, u32[]{:S(2)}) %collective-permute-start.6) | collective-permute-done | bytes 98336 | tf_op jit(solution)/shard_map/ppermute | solution.py:23
  26.8 1.3 %collective-permute-done.7.refs_3_ = bf16[4,8,1536]{2,1,0:T(8,128)(2,1)S(1)} collective-permute-done((bf16[4,8,1536]{2,1,0:T(8,128)(2,1)S(1)}, bf16[4,8,1536]{2,1,0:T(8,128)(2,1)S(1)}, u32[]{:S(2)}, u32[]{:S(2)}) %collective-permute-start.7) | collective-permute-done | bytes 98336 | tf_op jit(solution)/shard_map/ppermute | solution.py:23
  29.2 1.6 %collective-permute-start.8 = (bf16[4,8,1664]{2,1,0:T(8,128)(2,1)S(1)}, bf16[4,8,1664]{2,1,0:T(8,128)(2,1)S(1)}, u32[]{:S(2)}, u32[]{:S(2)}) collective-permute-start(bf16[4,8,1664]{2,1,0:T(8,128)(2,1)S(1)} %shard_map.105.refs_0_), channel_id=1, source_target_pairs={{0,8},{8,0},{16,24},{24,16},{1,9},{9,1},{17,25},{25,17},{2,10},{10... | collective-permute-start | bytes 319496 | tf_op jit(solution)/shard_map/ppermute | solution.py:23
  30.8 3.2 %collective-permute-done.8.refs_1_ = bf16[4,8,1664]{2,1,0:T(8,128)(2,1)S(1)} collective-permute-done((bf16[4,8,1664]{2,1,0:T(8,128)(2,1)S(1)}, bf16[4,8,1664]{2,1,0:T(8,128)(2,1)S(1)}, u32[]{:S(2)}, u32[]{:S(2)}) %collective-permute-start.8) | collective-permute-done | bytes 106528 | tf_op jit(solution)/shard_map/ppermute | solution.py:23
  34.0 2.7 %collective-permute-start.13 = (bf16[2,4,8,1664]{3,2,1,0:T(8,128)(2,1)S(1)}, bf16[2,4,8,1664]{3,2,1,0:T(8,128)(2,1)S(1)}, u32[]{:S(2)}, u32[]{:S(2)}) collective-permute-start(bf16[2,4,8,1664]{3,2,1,0:T(8,128)(2,1)S(1)} %shard_map.108), channel_id=1, source_target_pairs={{0,16},{8,24},{16,0},{24,8},{1,17},{9,25},{17,1},{25,9},{2,18},{10... | collective-permute-start | bytes 638984 | tf_op jit(solution)/shard_map/ppermute | solution.py:23
  36.7 1.9 %collective-permute-start.9 = (bf16[4,8,1664]{2,1,0:T(8,128)(2,1)S(1)}, bf16[4,8,1664]{2,1,0:T(8,128)(2,1)S(1)}, u32[]{:S(2)}, u32[]{:S(2)}) collective-permute-start(bf16[4,8,1664]{2,1,0:T(8,128)(2,1)S(1)} %shard_map.105.refs_0_), channel_id=1, source_target_pairs={{0,4},{1,5},{2,6},{3,7},{4,0},{5,1},{6,2},{7,3},{8,12},{9,13},{10,... | collective-permute-start | bytes 319496 | tf_op jit(solution)/shard_map/ppermute | solution.py:23
  38.6 2.8 %collective-permute-done.9.refs_2_ = bf16[4,8,1664]{2,1,0:T(8,128)(2,1)S(1)} collective-permute-done((bf16[4,8,1664]{2,1,0:T(8,128)(2,1)S(1)}, bf16[4,8,1664]{2,1,0:T(8,128)(2,1)S(1)}, u32[]{:S(2)}, u32[]{:S(2)}) %collective-permute-start.9) | collective-permute-done | bytes 106528 | tf_op jit(solution)/shard_map/ppermute | solution.py:23
  41.4 1.9 %collective-permute-done.10.refs_3_ = bf16[4,8,1664]{2,1,0:T(8,128)(2,1)S(1)} collective-permute-done((bf16[4,8,1664]{2,1,0:T(8,128)(2,1)S(1)}, bf16[4,8,1664]{2,1,0:T(8,128)(2,1)S(1)}, u32[]{:S(2)}, u32[]{:S(2)}) %collective-permute-start.10) | collective-permute-done | bytes 106528 | tf_op jit(solution)/shard_map/ppermute | solution.py:23
  44.8 1.6 %collective-permute-start.15 = (bf16[4,8,1664]{2,1,0:T(8,128)(2,1)S(1)}, bf16[4,8,1664]{2,1,0:T(8,128)(2,1)S(1)}, u32[]{:S(2)}, u32[]{:S(2)}) collective-permute-start(bf16[4,8,1664]{2,1,0:T(8,128)(2,1)S(1)} %get-tuple-element.63), channel_id=1, source_target_pairs={{0,2},{1,3},{2,0},{3,1},{4,6},{5,7},{6,4},{7,5},{8,10},{9,11},{10,... | collective-permute-start | bytes 319496 | tf_op jit(solution)/shard_map/ppermute | solution.py:23
  46.9 1.3 %collective-permute-start.12 = (bf16[2,4,8,1664]{3,2,1,0:T(8,128)(2,1)S(1)}, bf16[2,4,8,1664]{3,2,1,0:T(8,128)(2,1)S(1)}, u32[]{:S(2)}, u32[]{:S(2)}) collective-permute-start(bf16[2,4,8,1664]{3,2,1,0:T(8,128)(2,1)S(1)} %get-tuple-element.61.refs_2_), channel_id=1, source_target_pairs={{0,4},{1,5},{2,6},{3,7},{4,0},{5,1},{6,2},{7,3},{8,12},{9,13},{10,... | collective-permute-start | bytes 638984 | tf_op jit(solution)/shard_map/ppermute | solution.py:23
  48.1 1.8 %collective-permute-done.14.refs_1_ = bf16[4,8,1664]{2,1,0:T(8,128)(2,1)S(1)} collective-permute-done((bf16[4,8,1664]{2,1,0:T(8,128)(2,1)S(1)}, bf16[4,8,1664]{2,1,0:T(8,128)(2,1)S(1)}, u32[]{:S(2)}, u32[]{:S(2)}) %collective-permute-start.14) | collective-permute-done | bytes 106528 | tf_op jit(solution)/shard_map/ppermute | solution.py:23
  50.7 1.7 %collective-permute-start.16 = (bf16[2,4,8,1664]{3,2,1,0:T(8,128)(2,1)S(1)}, bf16[2,4,8,1664]{3,2,1,0:T(8,128)(2,1)S(1)}, u32[]{:S(2)}, u32[]{:S(2)}) collective-permute-start(bf16[2,4,8,1664]{3,2,1,0:T(8,128)(2,1)S(1)} %get-tuple-element.64), channel_id=1, source_target_pairs={{0,2},{1,3},{2,0},{3,1},{4,6},{5,7},{6,4},{7,5},{8,10},{9,11},{10,... | collective-permute-start | bytes 638984 | tf_op jit(solution)/shard_map/ppermute | solution.py:23
  52.4 1.5 %collective-permute-start.17 = (bf16[2,4,8,1664]{3,2,1,0:T(8,128)(2,1)S(1)}, bf16[2,4,8,1664]{3,2,1,0:T(8,128)(2,1)S(1)}, u32[]{:S(2)}, u32[]{:S(2)}) collective-permute-start(bf16[2,4,8,1664]{3,2,1,0:T(8,128)(2,1)S(1)} %get-tuple-element.65), channel_id=1, source_target_pairs={{0,4},{1,5},{2,6},{3,7},{4,0},{5,1},{6,2},{7,3},{8,12},{9,13},{10,... | collective-permute-start | bytes 638984 | tf_op jit(solution)/shard_map/ppermute | solution.py:23
  53.9 1.3 %collective-permute-done.11.refs_4_ = bf16[2,4,8,1664]{3,2,1,0:T(8,128)(2,1)S(1)} collective-permute-done((bf16[2,4,8,1664]{3,2,1,0:T(8,128)(2,1)S(1)}, bf16[2,4,8,1664]{3,2,1,0:T(8,128)(2,1)S(1)}, u32[]{:S(2)}, u32[]{:S(2)}) %collective-permute-start.11) | collective-permute-done | bytes 213024 | tf_op jit(solution)/shard_map/ppermute | solution.py:23
  55.4 2.3 %collective-permute-done.16.refs_3_ = bf16[2,4,8,1664]{3,2,1,0:T(8,128)(2,1)S(1)} collective-permute-done((bf16[2,4,8,1664]{3,2,1,0:T(8,128)(2,1)S(1)}, bf16[2,4,8,1664]{3,2,1,0:T(8,128)(2,1)S(1)}, u32[]{:S(2)}, u32[]{:S(2)}) %collective-permute-start.16) | collective-permute-done | bytes 213024 | tf_op jit(solution)/shard_map/ppermute | solution.py:23
  58.4 2.4 %collective-permute-done.19.refs_3_ = bf16[8,4,8,1664]{3,2,1,0:T(8,128)(2,1)S(1)} collective-permute-done((bf16[8,4,8,1664]{3,2,1,0:T(8,128)(2,1)S(1)}, bf16[8,4,8,1664]{3,2,1,0:T(8,128)(2,1)S(1)}, u32[]{:S(2)}, u32[]{:S(2)}) %collective-permute-start.19) | collective-permute-done | bytes 852000 | tf_op jit(solution)/shard_map/ppermute | solution.py:23
  60.8 24.3 %shard_map.112 = (bf16[8,8,6144]{2,1,0:T(8,128)(2,1)S(1)}, bf16[8,8,6144]{2,1,0:T(8,128)(2,1)S(1)}, bf16[8,8,6144]{2,1,0:T(8,128)(2,1)S(1)}, bf16[8,8,6144]{2,1,0:T(8,128)(2,1)S(1)}, f32[8,6144]{1,0:T(8,128)S(1)}) custom-call(bf16[8,4,8,1664]{3,2,1,0:T(8,128)(2,1)S(1)} %shard_map.107.refs_0_, bf16[8,4,8,1664]{3,2,1,0:T(8,128)(2,1)S(1)} %shard_map.111.refs_1_, ...), custom_call_target="tpu_custom_call" | custom-call | flops 12683575296 | bytes 55836672 | tf_op jit(solution)/shard_map/pallas_call | solution.py:384
  85.7 1.8 %collective-permute-done.20.refs_1_ = bf16[8,8,6144]{2,1,0:T(8,128)(2,1)S(1)} collective-permute-done((bf16[8,8,6144]{2,1,0:T(8,128)(2,1)S(1)}, bf16[8,8,6144]{2,1,0:T(8,128)(2,1)S(1)}, u32[]{:S(2)}, u32[]{:S(2)}) %collective-permute-start.20) | collective-permute-done | bytes 786464 | tf_op jit(solution)/shard_map/ppermute | solution.py:23
  92.0 3.4 %collective-permute-done.21.refs_1_ = bf16[2,8,6144]{2,1,0:T(8,128)(2,1)S(1)} collective-permute-done((bf16[2,8,6144]{2,1,0:T(8,128)(2,1)S(1)}, bf16[2,8,6144]{2,1,0:T(8,128)(2,1)S(1)}, u32[]{:S(2)}, u32[]{:S(2)}) %collective-permute-start.21) | collective-permute-done | bytes 196640 | tf_op jit(solution)/shard_map/ppermute | solution.py:23
  99.4 1.4 %collective-permute-done.28.refs_3_ = bf16[2,8,6144]{2,1,0:T(8,128)(2,1)S(1)} collective-permute-done((bf16[2,8,6144]{2,1,0:T(8,128)(2,1)S(1)}, bf16[2,8,6144]{2,1,0:T(8,128)(2,1)S(1)}, u32[]{:S(2)}, u32[]{:S(2)}) %collective-permute-start.28) | collective-permute-done | bytes 196640 | tf_op jit(solution)/shard_map/ppermute | solution.py:23
  103.5 2.1 %collective-permute-done.29.refs_1_ = bf16[1,8,6144]{2,1,0:T(8,128)(2,1)S(1)} collective-permute-done((bf16[1,8,6144]{2,1,0:T(8,128)(2,1)S(1)}, bf16[1,8,6144]{2,1,0:T(8,128)(2,1)S(1)}, u32[]{:S(2)}, u32[]{:S(2)}) %collective-permute-start.29) | collective-permute-done | bytes 98336 | tf_op jit(solution)/shard_map/ppermute | solution.py:23
  106.9 2.7 %collective-permute-start.32 = (bf16[1,8,6144]{2,1,0:T(8,128)(2,1)S(1)}, bf16[1,8,6144]{2,1,0:T(8,128)(2,1)S(1)}, u32[]{:S(2)}, u32[]{:S(2)}) collective-permute-start(bf16[1,8,6144]{2,1,0:T(8,128)(2,1)S(1)} %get-tuple-element.90), channel_id=1, source_target_pairs={{0,24},{8,16},{16,8},{24,0},{1,25},{9,17},{17,9},{25,1},{2,26},{10... | collective-permute-start | bytes 294920 | tf_op jit(solution)/shard_map/ppermute | solution.py:23
  109.6 4.9 %collective-permute-done.31 = bf16[1,8,6144]{2,1,0:T(8,128)(2,1)S(1)} collective-permute-done((bf16[1,8,6144]{2,1,0:T(8,128)(2,1)S(1)}, bf16[1,8,6144]{2,1,0:T(8,128)(2,1)S(1)}, u32[]{:S(2)}, u32[]{:S(2)}) %collective-permute-start.31) | collective-permute-done | bytes 98336 | tf_op jit(solution)/shard_map/ppermute | solution.py:23
  (65 shorter events, 23.9 us)
Async XLA Ops:
  1.8 8.7 %collective-permute-start = (bf16[11,8,512]{2,1,0:T(8,128)(2,1)}, bf16[11,8,512]{2,1,0:T(8,128)(2,1)S(1)}, u32[]{:S(2)}, u32[]{:S(2)}) collective-permute-start(bf16[11,8,512]{2,1,0:T(8,128)(2,1)} %get-tuple-element.49), channel_id=1, source_target_pairs={{0,8},{8,0},{16,24},{24,16},{1,9},{9,1},{17,25},{25,17},{2,10},{10... | collective-permute-start | bytes 270344 | tf_op jit(solution)/shard_map/ppermute | solution.py:23
  4.9 10.0 %collective-permute-start.1 = (bf16[11,8,512]{2,1,0:T(8,128)(2,1)}, bf16[11,8,512]{2,1,0:T(8,128)(2,1)S(1)}, u32[]{:S(2)}, u32[]{:S(2)}) collective-permute-start(bf16[11,8,512]{2,1,0:T(8,128)(2,1)} %get-tuple-element.50), channel_id=1, source_target_pairs={{0,16},{8,24},{16,0},{24,8},{1,17},{9,25},{17,1},{25,9},{2,18},{10... | collective-permute-start | bytes 270344 | tf_op jit(solution)/shard_map/ppermute | solution.py:23
  7.5 7.4 %collective-permute-start.2 = (bf16[11,8,512]{2,1,0:T(8,128)(2,1)}, bf16[11,8,512]{2,1,0:T(8,128)(2,1)S(1)}, u32[]{:S(2)}, u32[]{:S(2)}) collective-permute-start(bf16[11,8,512]{2,1,0:T(8,128)(2,1)} %get-tuple-element.51), channel_id=1, source_target_pairs={{0,24},{8,16},{16,8},{24,0},{1,25},{9,17},{17,9},{25,1},{2,26},{10... | collective-permute-start | bytes 270344 | tf_op jit(solution)/shard_map/ppermute | solution.py:23
  17.6 1.8 %collective-permute-start.4 = (bf16[4,4,8,1536]{3,2,1,0:T(8,128)(2,1)S(1)}, bf16[4,4,8,1536]{3,2,1,0:T(8,128)(2,1)S(1)}, u32[]{:S(2)}, u32[]{:S(2)}) collective-permute-start(bf16[4,4,8,1536]{3,2,1,0:T(8,128)(2,1)S(1)} %get-tuple-element.55), channel_id=1, source_target_pairs={{0,1},{1,0},{2,3},{3,2},{4,5},{5,4},{6,7},{7,6},{8,9},{9,8},{10,11... | collective-permute-start | bytes 1179656 | tf_op jit(solution)/shard_map/ppermute | solution.py:23
  19.5 4.9 %collective-permute-start.5 = (bf16[4,8,1536]{2,1,0:T(8,128)(2,1)S(1)}, bf16[4,8,1536]{2,1,0:T(8,128)(2,1)S(1)}, u32[]{:S(2)}, u32[]{:S(2)}) collective-permute-start(bf16[4,8,1536]{2,1,0:T(8,128)(2,1)S(1)} %get-tuple-element.57), channel_id=1, source_target_pairs={{0,2},{1,3},{2,0},{3,1},{4,6},{5,7},{6,4},{7,5},{8,10},{9,11},{10,... | collective-permute-start | bytes 294920 | tf_op jit(solution)/shard_map/ppermute | solution.py:23
  21.1 5.8 %collective-permute-start.6 = (bf16[4,8,1536]{2,1,0:T(8,128)(2,1)S(1)}, bf16[4,8,1536]{2,1,0:T(8,128)(2,1)S(1)}, u32[]{:S(2)}, u32[]{:S(2)}) collective-permute-start(bf16[4,8,1536]{2,1,0:T(8,128)(2,1)S(1)} %get-tuple-element.58), channel_id=1, source_target_pairs={{0,4},{1,5},{2,6},{3,7},{4,0},{5,1},{6,2},{7,3},{8,12},{9,13},{10,... | collective-permute-start | bytes 294920 | tf_op jit(solution)/shard_map/ppermute | solution.py:23
  22.6 5.5 %collective-permute-start.7 = (bf16[4,8,1536]{2,1,0:T(8,128)(2,1)S(1)}, bf16[4,8,1536]{2,1,0:T(8,128)(2,1)S(1)}, u32[]{:S(2)}, u32[]{:S(2)}) collective-permute-start(bf16[4,8,1536]{2,1,0:T(8,128)(2,1)S(1)} %get-tuple-element.59), channel_id=1, source_target_pairs={{0,6},{1,7},{2,4},{3,5},{4,2},{5,3},{6,0},{7,1},{8,14},{9,15},{10,... | collective-permute-start | bytes 294920 | tf_op jit(solution)/shard_map/ppermute | solution.py:23
  29.2 4.8 %collective-permute-start.8 = (bf16[4,8,1664]{2,1,0:T(8,128)(2,1)S(1)}, bf16[4,8,1664]{2,1,0:T(8,128)(2,1)S(1)}, u32[]{:S(2)}, u32[]{:S(2)}) collective-permute-start(bf16[4,8,1664]{2,1,0:T(8,128)(2,1)S(1)} %shard_map.105.refs_0_), channel_id=1, source_target_pairs={{0,8},{8,0},{16,24},{24,16},{1,9},{9,1},{17,25},{25,17},{2,10},{10... | collective-permute-start | bytes 319496 | tf_op jit(solution)/shard_map/ppermute | solution.py:23
  34.0 10.0 %collective-permute-start.13 = (bf16[2,4,8,1664]{3,2,1,0:T(8,128)(2,1)S(1)}, bf16[2,4,8,1664]{3,2,1,0:T(8,128)(2,1)S(1)}, u32[]{:S(2)}, u32[]{:S(2)}) collective-permute-start(bf16[2,4,8,1664]{3,2,1,0:T(8,128)(2,1)S(1)} %shard_map.108), channel_id=1, source_target_pairs={{0,16},{8,24},{16,0},{24,8},{1,17},{9,25},{17,1},{25,9},{2,18},{10... | collective-permute-start | bytes 638984 | tf_op jit(solution)/shard_map/ppermute | solution.py:23
  36.7 4.7 %collective-permute-start.9 = (bf16[4,8,1664]{2,1,0:T(8,128)(2,1)S(1)}, bf16[4,8,1664]{2,1,0:T(8,128)(2,1)S(1)}, u32[]{:S(2)}, u32[]{:S(2)}) collective-permute-start(bf16[4,8,1664]{2,1,0:T(8,128)(2,1)S(1)} %shard_map.105.refs_0_), channel_id=1, source_target_pairs={{0,4},{1,5},{2,6},{3,7},{4,0},{5,1},{6,2},{7,3},{8,12},{9,13},{10,... | collective-permute-start | bytes 319496 | tf_op jit(solution)/shard_map/ppermute | solution.py:23
  38.6 4.7 %collective-permute-start.10 = (bf16[4,8,1664]{2,1,0:T(8,128)(2,1)S(1)}, bf16[4,8,1664]{2,1,0:T(8,128)(2,1)S(1)}, u32[]{:S(2)}, u32[]{:S(2)}) collective-permute-start(bf16[4,8,1664]{2,1,0:T(8,128)(2,1)S(1)} %collective-permute-done.8.refs_1_), channel_id=1, source_target_pairs={{0,2},{1,3},{2,0},{3,1},{4,6},{5,7},{6,4},{7,5},{8,10},{9,11},{10,... | collective-permute-start | bytes 319496 | tf_op jit(solution)/shard_map/ppermute | solution.py:23
  44.0 5.9 %collective-permute-start.14 = (bf16[4,8,1664]{2,1,0:T(8,128)(2,1)S(1)}, bf16[4,8,1664]{2,1,0:T(8,128)(2,1)S(1)}, u32[]{:S(2)}, u32[]{:S(2)}) collective-permute-start(bf16[4,8,1664]{2,1,0:T(8,128)(2,1)S(1)} %get-tuple-element.62), channel_id=1, source_target_pairs={{0,4},{1,5},{2,6},{3,7},{4,0},{5,1},{6,2},{7,3},{8,12},{9,13},{10,... | collective-permute-start | bytes 319496 | tf_op jit(solution)/shard_map/ppermute | solution.py:23
  44.8 5.8 %collective-permute-start.15 = (bf16[4,8,1664]{2,1,0:T(8,128)(2,1)S(1)}, bf16[4,8,1664]{2,1,0:T(8,128)(2,1)S(1)}, u32[]{:S(2)}, u32[]{:S(2)}) collective-permute-start(bf16[4,8,1664]{2,1,0:T(8,128)(2,1)S(1)} %get-tuple-element.63), channel_id=1, source_target_pairs={{0,2},{1,3},{2,0},{3,1},{4,6},{5,7},{6,4},{7,5},{8,10},{9,11},{10,... | collective-permute-start | bytes 319496 | tf_op jit(solution)/shard_map/ppermute | solution.py:23
  46.4 8.8 %collective-permute-start.11 = (bf16[2,4,8,1664]{3,2,1,0:T(8,128)(2,1)S(1)}, bf16[2,4,8,1664]{3,2,1,0:T(8,128)(2,1)S(1)}, u32[]{:S(2)}, u32[]{:S(2)}) collective-permute-start(bf16[2,4,8,1664]{3,2,1,0:T(8,128)(2,1)S(1)} %get-tuple-element.60.refs_1_), channel_id=1, source_target_pairs={{0,2},{1,3},{2,0},{3,1},{4,6},{5,7},{6,4},{7,5},{8,10},{9,11},{10,... | collective-permute-start | bytes 638984 | tf_op jit(solution)/shard_map/ppermute | solution.py:23
  46.9 8.4 %collective-permute-start.12 = (bf16[2,4,8,1664]{3,2,1,0:T(8,128)(2,1)S(1)}, bf16[2,4,8,1664]{3,2,1,0:T(8,128)(2,1)S(1)}, u32[]{:S(2)}, u32[]{:S(2)}) collective-permute-start(bf16[2,4,8,1664]{3,2,1,0:T(8,128)(2,1)S(1)} %get-tuple-element.61.refs_2_), channel_id=1, source_target_pairs={{0,4},{1,5},{2,6},{3,7},{4,0},{5,1},{6,2},{7,3},{8,12},{9,13},{10,... | collective-permute-start | bytes 638984 | tf_op jit(solution)/shard_map/ppermute | solution.py:23
  50.7 7.0 %collective-permute-start.16 = (bf16[2,4,8,1664]{3,2,1,0:T(8,128)(2,1)S(1)}, bf16[2,4,8,1664]{3,2,1,0:T(8,128)(2,1)S(1)}, u32[]{:S(2)}, u32[]{:S(2)}) collective-permute-start(bf16[2,4,8,1664]{3,2,1,0:T(8,128)(2,1)S(1)} %get-tuple-element.64), channel_id=1, source_target_pairs={{0,2},{1,3},{2,0},{3,1},{4,6},{5,7},{6,4},{7,5},{8,10},{9,11},{10,... | collective-permute-start | bytes 638984 | tf_op jit(solution)/shard_map/ppermute | solution.py:23
  52.4 5.8 %collective-permute-start.17 = (bf16[2,4,8,1664]{3,2,1,0:T(8,128)(2,1)S(1)}, bf16[2,4,8,1664]{3,2,1,0:T(8,128)(2,1)S(1)}, u32[]{:S(2)}, u32[]{:S(2)}) collective-permute-start(bf16[2,4,8,1664]{3,2,1,0:T(8,128)(2,1)S(1)} %get-tuple-element.65), channel_id=1, source_target_pairs={{0,4},{1,5},{2,6},{3,7},{4,0},{5,1},{6,2},{7,3},{8,12},{9,13},{10,... | collective-permute-start | bytes 638984 | tf_op jit(solution)/shard_map/ppermute | solution.py:23
  55.3 3.1 %collective-permute-start.18 = (bf16[8,4,8,1664]{3,2,1,0:T(8,128)(2,1)S(1)}, bf16[8,4,8,1664]{3,2,1,0:T(8,128)(2,1)S(1)}, u32[]{:S(2)}, u32[]{:S(2)}) collective-permute-start(bf16[8,4,8,1664]{3,2,1,0:T(8,128)(2,1)S(1)} %shard_map.107.refs_0_), channel_id=1, source_target_pairs={{0,1},{1,0},{2,3},{3,2},{4,5},{5,4},{6,7},{7,6},{8,9},{9,8},{10,11... | collective-permute-start | bytes 2555912 | tf_op jit(solution)/shard_map/ppermute | solution.py:23
  58.3 2.4 %collective-permute-start.19 = (bf16[8,4,8,1664]{3,2,1,0:T(8,128)(2,1)S(1)}, bf16[8,4,8,1664]{3,2,1,0:T(8,128)(2,1)S(1)}, u32[]{:S(2)}, u32[]{:S(2)}) collective-permute-start(bf16[8,4,8,1664]{3,2,1,0:T(8,128)(2,1)S(1)} %shard_map.111.refs_1_), channel_id=1, source_target_pairs={{0,1},{1,0},{2,3},{3,2},{4,5},{5,4},{6,7},{7,6},{8,9},{9,8},{10,11... | collective-permute-start | bytes 2555912 | tf_op jit(solution)/shard_map/ppermute | solution.py:23
  85.1 2.4 %collective-permute-start.20 = (bf16[8,8,6144]{2,1,0:T(8,128)(2,1)S(1)}, bf16[8,8,6144]{2,1,0:T(8,128)(2,1)S(1)}, u32[]{:S(2)}, u32[]{:S(2)}) collective-permute-start(bf16[8,8,6144]{2,1,0:T(8,128)(2,1)S(1)} %get-tuple-element.68), channel_id=1, source_target_pairs={{0,1},{1,0},{2,3},{3,2},{4,5},{5,4},{6,7},{7,6},{8,9},{9,8},{10,11... | collective-permute-start | bytes 2359304 | tf_op jit(solution)/shard_map/ppermute | solution.py:23
  85.3 4.8 %collective-permute-start.26 = (bf16[8,8,6144]{2,1,0:T(8,128)(2,1)S(1)}, bf16[8,8,6144]{2,1,0:T(8,128)(2,1)S(1)}, u32[]{:S(2)}, u32[]{:S(2)}) collective-permute-start(bf16[8,8,6144]{2,1,0:T(8,128)(2,1)S(1)} %get-tuple-element.80), channel_id=1, source_target_pairs={{0,1},{1,0},{2,3},{3,2},{4,5},{5,4},{6,7},{7,6},{8,9},{9,8},{10,11... | collective-permute-start | bytes 2359304 | tf_op jit(solution)/shard_map/ppermute | solution.py:23
  87.6 7.8 %collective-permute-start.21 = (bf16[2,8,6144]{2,1,0:T(8,128)(2,1)S(1)}, bf16[2,8,6144]{2,1,0:T(8,128)(2,1)S(1)}, u32[]{:S(2)}, u32[]{:S(2)}) collective-permute-start(bf16[2,8,6144]{2,1,0:T(8,128)(2,1)S(1)} %get-tuple-element.70), channel_id=1, source_target_pairs={{0,2},{1,3},{2,0},{3,1},{4,6},{5,7},{6,4},{7,5},{8,10},{9,11},{10,... | collective-permute-start | bytes 589832 | tf_op jit(solution)/shard_map/ppermute | solution.py:23
  88.9 7.8 %collective-permute-start.22 = (bf16[2,8,6144]{2,1,0:T(8,128)(2,1)S(1)}, bf16[2,8,6144]{2,1,0:T(8,128)(2,1)S(1)}, u32[]{:S(2)}, u32[]{:S(2)}) collective-permute-start(bf16[2,8,6144]{2,1,0:T(8,128)(2,1)S(1)} %get-tuple-element.72), channel_id=1, source_target_pairs={{0,4},{1,5},{2,6},{3,7},{4,0},{5,1},{6,2},{7,3},{8,12},{9,13},{10,... | collective-permute-start | bytes 589832 | tf_op jit(solution)/shard_map/ppermute | solution.py:23
  90.2 9.2 %collective-permute-start.27 = (bf16[2,8,6144]{2,1,0:T(8,128)(2,1)S(1)}, bf16[2,8,6144]{2,1,0:T(8,128)(2,1)S(1)}, u32[]{:S(2)}, u32[]{:S(2)}) collective-permute-start(bf16[2,8,6144]{2,1,0:T(8,128)(2,1)S(1)} %get-tuple-element.82), channel_id=1, source_target_pairs={{0,2},{1,3},{2,0},{3,1},{4,6},{5,7},{6,4},{7,5},{8,10},{9,11},{10,... | collective-permute-start | bytes 589832 | tf_op jit(solution)/shard_map/ppermute | solution.py:23
  91.5 9.3 %collective-permute-start.28 = (bf16[2,8,6144]{2,1,0:T(8,128)(2,1)S(1)}, bf16[2,8,6144]{2,1,0:T(8,128)(2,1)S(1)}, u32[]{:S(2)}, u32[]{:S(2)}) collective-permute-start(bf16[2,8,6144]{2,1,0:T(8,128)(2,1)S(1)} %get-tuple-element.84), channel_id=1, source_target_pairs={{0,4},{1,5},{2,6},{3,7},{4,0},{5,1},{6,2},{7,3},{8,12},{9,13},{10,... | collective-permute-start | bytes 589832 | tf_op jit(solution)/shard_map/ppermute | solution.py:23
  96.7 6.6 %collective-permute-start.23 = (bf16[1,8,6144]{2,1,0:T(8,128)(2,1)S(1)}, bf16[1,8,6144]{2,1,0:T(8,128)(2,1)S(1)}, u32[]{:S(2)}, u32[]{:S(2)}) collective-permute-start(bf16[1,8,6144]{2,1,0:T(8,128)(2,1)S(1)} %get-tuple-element.74), channel_id=1, source_target_pairs={{0,4},{1,5},{2,6},{3,7},{4,0},{5,1},{6,2},{7,3},{8,12},{9,13},{10,... | collective-permute-start | bytes 294920 | tf_op jit(solution)/shard_map/ppermute | solution.py:23
  98.0 5.3 %collective-permute-start.24 = (bf16[1,8,6144]{2,1,0:T(8,128)(2,1)S(1)}, bf16[1,8,6144]{2,1,0:T(8,128)(2,1)S(1)}, u32[]{:S(2)}, u32[]{:S(2)}) collective-permute-start(bf16[1,8,6144]{2,1,0:T(8,128)(2,1)S(1)} %get-tuple-element.76), channel_id=1, source_target_pairs={{0,2},{1,3},{2,0},{3,1},{4,6},{5,7},{6,4},{7,5},{8,10},{9,11},{10,... | collective-permute-start | bytes 294920 | tf_op jit(solution)/shard_map/ppermute | solution.py:23
  100.9 4.7 %collective-permute-start.29 = (bf16[1,8,6144]{2,1,0:T(8,128)(2,1)S(1)}, bf16[1,8,6144]{2,1,0:T(8,128)(2,1)S(1)}, u32[]{:S(2)}, u32[]{:S(2)}) collective-permute-start(bf16[1,8,6144]{2,1,0:T(8,128)(2,1)S(1)} %get-tuple-element.86), channel_id=1, source_target_pairs={{0,4},{1,5},{2,6},{3,7},{4,0},{5,1},{6,2},{7,3},{8,12},{9,13},{10,... | collective-permute-start | bytes 294920 | tf_op jit(solution)/shard_map/ppermute | solution.py:23
  102.2 4.6 %collective-permute-start.30 = (bf16[1,8,6144]{2,1,0:T(8,128)(2,1)S(1)}, bf16[1,8,6144]{2,1,0:T(8,128)(2,1)S(1)}, u32[]{:S(2)}, u32[]{:S(2)}) collective-permute-start(bf16[1,8,6144]{2,1,0:T(8,128)(2,1)S(1)} %get-tuple-element.88), channel_id=1, source_target_pairs={{0,2},{1,3},{2,0},{3,1},{4,6},{5,7},{6,4},{7,5},{8,10},{9,11},{10,... | collective-permute-start | bytes 294920 | tf_op jit(solution)/shard_map/ppermute | solution.py:23
  103.4 6.2 %collective-permute-start.25 = (bf16[1,8,6144]{2,1,0:T(8,128)(2,1)S(1)}, bf16[1,8,6144]{2,1,0:T(8,128)(2,1)S(1)}, u32[]{:S(2)}, u32[]{:S(2)}) collective-permute-start(bf16[1,8,6144]{2,1,0:T(8,128)(2,1)S(1)} %get-tuple-element.78), channel_id=1, source_target_pairs={{0,8},{8,0},{16,24},{24,16},{1,9},{9,1},{17,25},{25,17},{2,10},{10... | collective-permute-start | bytes 294920 | tf_op jit(solution)/shard_map/ppermute | solution.py:23
  106.8 7.6 %collective-permute-start.31 = (bf16[1,8,6144]{2,1,0:T(8,128)(2,1)S(1)}, bf16[1,8,6144]{2,1,0:T(8,128)(2,1)S(1)}, u32[]{:S(2)}, u32[]{:S(2)}) collective-permute-start(bf16[1,8,6144]{2,1,0:T(8,128)(2,1)S(1)} %get-tuple-element.89), channel_id=1, source_target_pairs={{0,16},{8,24},{16,0},{24,8},{1,17},{9,25},{17,1},{25,9},{2,18},{10... | collective-permute-start | bytes 294920 | tf_op jit(solution)/shard_map/ppermute | solution.py:23
  106.9 7.6 %collective-permute-start.32 = (bf16[1,8,6144]{2,1,0:T(8,128)(2,1)S(1)}, bf16[1,8,6144]{2,1,0:T(8,128)(2,1)S(1)}, u32[]{:S(2)}, u32[]{:S(2)}) collective-permute-start(bf16[1,8,6144]{2,1,0:T(8,128)(2,1)S(1)} %get-tuple-element.90), channel_id=1, source_target_pairs={{0,24},{8,16},{16,8},{24,0},{1,25},{9,17},{17,9},{25,1},{2,26},{10... | collective-permute-start | bytes 294920 | tf_op jit(solution)/shard_map/ppermute | solution.py:23
  (5 other events, 5.1 us)
where the time goes:
time: 116 us; the launch traced here: 115 us
  waiting for transfers between devices  45.2 us (39%)
  starting transfers between devices  35.7 us (31%)
  Pallas kernels  28.7 us (25%)
  local copies, waits for them, and re-layouts  3.79 us (3%)
  other arithmetic  1.57 us (1%)
    ppermute x33, waiting for transfers between devices, swap(): lax.ppermute(value, axis, [(i, i ^ mask) for i in range(lax.axis_size(axi...  45.2 us
    ppermute x33, starting transfers between devices, swap(): lax.ppermute(value, axis, [(i, i ^ mask) for i in range(lax.axis_size(axi...  35.7 us
    pallas_call x1, Pallas kernels, run_experts(): pl.pallas_call(functools.partial(expert_kernel, C, E, per_block, width, c...  24.3 us
    pallas_call x18, Pallas kernels, call(): pl.pallas_call(kernel, out_shape=out_shape, in_specs=in_specs, out_specs=...  4.43 us
    unnamed x8, local copies, waits for them, and re-layouts  3.79 us
  transfers between devices with their start and end apart: 33, of which 24 were waited for; matrix products, arithmetic and copies ran while one was open for 1% of the time, Pallas kernels for 1%

commit v1 on v0

--- a/solution.py
+++ b/solution.py
@@ -135,8 +135,10 @@
 
 
 def halves_kernel(C, E, *refs):
+    halves, residual = refs[-2:]
     for k in range(C):
-        refs[-1][k] = refs[k][:E, :, refs[k].shape[2] - HD :]
+        halves[k] = refs[k][:E, :, refs[k].shape[2] - HD :]
+    residual[...] = refs[0][E:]
 
 
 def split_terms(value):
@@ -156,9 +158,10 @@
     lane = lax.broadcasted_iota(jnp.int32, (own.shape[1], EXTRA), 1)
     for k in range(C):
         j = lax.axis_index("ctx") ^ k
+        start = E if k else 0
         pieces = [
-            messages[k][E + i, :, : min(wide, cols - i * wide)].astype(F32)
-            for i in range(messages[k].shape[0] - E)
+            messages[k][start + i, :, : min(wide, cols - i * wide)].astype(F32)
+            for i in range(messages[k].shape[0] - start)
         ]
         total = own[j] + jnp.concatenate(pieces, axis=1)
         for piece in received:
@@ -193,7 +196,7 @@
     )
 
 
-def spread_over_plane(arrays, sources, orders, chips, after):
+def spread_over_plane(arrays, sources, orders, chips, afters, last=lambda sends: []):
     tail = arrays[0].shape[-3:]
     holds = [{0: source} for source in sources]
     arrays = list(arrays)
@@ -202,27 +205,57 @@
         if step == 0 and len(arrays) == 2:
             sends = arrays[:]
         else:
-            sends = pack(plan, arrays, tail, after)
-            after = []
+            sends = pack(plan, arrays, tail, afters[step])
         for hold, order, send in zip(holds, orders, sends):
             at = len(arrays)
             arrays.append(swap(send, "exp", 1 << order[step]))
             far = 1 << (order[step] - 1)
             for i, p in enumerate(sorted(hold)):
                 hold[p | far] = (at, None if step == 0 else i)
-    (packed,) = pack([[hold[p] for hold in holds for p in range(chips)]], arrays, tail)
+    plan = [[hold[p] for hold in holds for p in range(chips)]]
+    (packed,) = pack(plan, arrays, tail, last(sends))
     return packed, sends
 
 
-def expert_kernel(C, E, per_block, width, columns, *refs):
+def load_kernel(blocks, *refs):
+    token, sems = refs[-2:]
+    outs = refs[-2 - len(blocks) : -2]
+    copies = []
+    for i, (out, (which, j)) in enumerate(zip(outs, blocks)):
+        cols = out.shape[1]
+        source = refs[which].at[0, :, j * cols : (j + 1) * cols]
+        copies.append(pltpu.make_async_copy(source, out, sems.at[i]))
+    for copy in copies:
+        copy.start()
+    for copy in copies:
+        copy.wait()
+    token[...] = jnp.zeros_like(token)
+
+
+def load_blocks(weights, blocks, cols, after, limit):
+    units = weights[0].shape[1]
+    *loaded, token = pl.pallas_call(
+        functools.partial(load_kernel, blocks),
+        out_shape=[shape((units, cols), BF16) for _ in blocks] + [shape((8, 128), F32)],
+        in_specs=[IN_HBM, IN_HBM, WHOLE],
+        out_specs=[WHOLE] * (len(blocks) + 1),
+        scratch_shapes=[pltpu.SemaphoreType.DMA((len(blocks),))],
+        compiler_params=pltpu.CompilerParams(vmem_limit_bytes=limit * MIB),
+        cost_estimate=pl.CostEstimate(
+            flops=0, bytes_accessed=4 * units * cols * len(blocks), transcendentals=0
+        ),
+    )(*weights, after)
+    return loaded, token
+
+
+def expert_kernel(C, E, per_block, width, columns, held, *refs):
     groups = C // 2
-    packed = refs[: 2 * groups]
-    gain, gate, up, down = refs[2 * groups : 2 * groups + 4]
-    outs = refs[2 * groups + 4 : 4 * groups + 4]
-    hidden = refs[4 * groups + 4]
-    gate_sum, up_sum, activated, piece, shift, spread, scale = refs[4 * groups + 5 : -5]
-    gate_slots, up_slots, down_slots, up_sems, down_sems = refs[-5:]
-    step = pl.program_id(0)
+    packed, refs = refs[: 2 * groups], refs[2 * groups :]
+    gate_held, up_held, refs = refs[:held], refs[held : 2 * held], refs[2 * held :]
+    gain, gate, up, down = refs[:4]
+    outs, hidden, refs = refs[4 : 2 * groups + 4], refs[2 * groups + 4], refs[2 * groups + 5 :]
+    gate_sum, up_sum, activated, piece, block, shift, spread, scale = refs[:8]
+    gate_slots, up_slots, down_slots, up_sems, down_sems = refs[8:]
     ctx, exp = lax.axis_index("ctx"), lax.axis_index("exp")
     chips = E // 2
     token_rows = packed[0].shape[2]
@@ -230,6 +263,7 @@
     half_rows = chips * C * token_rows
     features = hidden.shape[1]
     up_steps = C * per_block
+    first = held * per_block
     down_steps = features // columns
     ahead, down_ahead = gate_slots.shape[0], down_slots.shape[0]
 
@@ -244,21 +278,9 @@
         at = pl.ds(pl.multiple_of(i * columns, 128), columns)
         return pltpu.make_async_copy(down.at[0, :, at], down_slots.at[slot], down_sems.at[slot])
 
-    @pl.when(step == 0)
-    def _():
-        for i in range(ahead):
-            for copy in up_copies(i, i):
-                copy.start()
-
-    @pl.when(step < up_steps)
-    def _():
-        for copy in up_copies(step, step % ahead):
-            copy.wait()
-
-    @pl.when(step >= up_steps)
-    def _():
-        done = step - up_steps
-        down_copy(done, done % down_ahead).wait()
+    for i in range(ahead):
+        for copy in up_copies(first + i, i):
+            copy.start()
 
     def read(g, s, at):
         parts = [
@@ -267,134 +289,132 @@
         parts = [part.astype(F32).reshape(half_rows, part.shape[-1]) for part in parts]
         return jnp.concatenate(parts, axis=0)
 
-    @pl.when(step == 0)
-    def _():
-        tails = [read(k // 2, k % 2, slice(cols, cols + EXTRA)) for k in range(C)]
-        lane = lax.broadcasted_iota(jnp.int32, tails[0].shape, 1)
-
-        def pick(tail, wanted):
-            return jnp.sum(jnp.where(wanted, tail, 0.0), axis=1, keepdims=True)
-
-        means = [pick(tail, lane < SPLIT) for tail in tails]
-        squares = [pick(tail, (lane >= SPLIT) & (lane < 2 * SPLIT)) for tail in tails]
-        mean = sum(means) * (1.0 / C)
-        deviation = sum(squares) + cols * sum((m - mean) * (m - mean) for m in means)
-        spread[...] = lax.rsqrt(deviation * (1.0 / features) + 1e-05)
-        for k in range(C):
-            shift[k, 0] = means[k]
-            shift[k, 1] = means[k] - mean
-        first = lane - FIRST
-        wanted = (first >= 0) & ((first & (E - 1)) == exp) & (first < SPLIT * E)
-        scale[...] = sum(pick(tail, wanted) for tail in tails)
-
-    for g in range(groups):
-        block_at = step // per_block
-        k = block_at ^ ctx
-
-        @pl.when((step < up_steps) & (k // 2 == g))
+    tails = [read(k % groups, k // groups, slice(cols, cols + EXTRA)) for k in range(C)]
+    lane = lax.broadcasted_iota(jnp.int32, tails[0].shape, 1)
+
+    def pick(tail, wanted):
+        return jnp.sum(jnp.where(wanted, tail, 0.0), axis=1, keepdims=True)
+
+    means = [pick(tail, lane < SPLIT) for tail in tails]
+    squares = [pick(tail, (lane >= SPLIT) & (lane < 2 * SPLIT)) for tail in tails]
+    mean = sum(means) * (1.0 / C)
+    deviation = sum(squares) + cols * sum((m - mean) * (m - mean) for m in means)
+    spread[...] = lax.rsqrt(deviation * (1.0 / features) + 1e-05)
+    for k in range(C):
+        shift[k, 0] = means[k]
+        shift[k, 1] = means[k] - mean
+    term = lane - FIRST
+    wanted = (term >= 0) & ((term & (E - 1)) == exp) & (term < SPLIT * E)
+    scale[...] = sum(pick(tail, wanted) for tail in tails)
+
+    def normalise(j, part):
+        k = j ^ ctx
+        at = pl.ds(pl.multiple_of(part * width, 128), width)
+        place = pl.multiple_of(j * cols + part * width, 128)
+        for g in range(groups):
+
+            @pl.when(k % groups == g)
+            def _():
+                s = k // groups
+                value = (read(g, s, at) + shift[k, 1]) * spread[...]
+                block[...] = (value * gain[:, pl.ds(place, width)]).astype(BF16)
+                own = packed[g][s * chips, ctx, :, at].astype(F32)
+                rows = pl.ds(pl.multiple_of(ctx * token_rows, token_rows), token_rows)
+                hidden[:, pl.ds(place, width)] = own + shift[k, 0, rows]
+
+    turned_dot = functools.partial(
+        lax.dot_general,
+        dimension_numbers=(((1,), (1,)), ((), ())),
+        preferred_element_type=F32,
+    )
+    if held == 0:
+        gate_sum[...] = jnp.zeros_like(gate_sum)
+        up_sum[...] = jnp.zeros_like(up_sum)
+        for i in range(down_ahead):
+            down_copy(i, i).start()
+    for i in range(first):
+        j, part = i // per_block, i % per_block
+        normalise(j, part)
+        at = slice(part * width, (part + 1) * width)
+        gate_part = turned_dot(block[...], gate_held[j][:, at])
+        gate_sum[...] = gate_part if i == 0 else gate_sum[...] + gate_part
+        up_part = turned_dot(block[...], up_held[j][:, at])
+        up_sum[...] = up_part if i == 0 else up_sum[...] + up_part
+        if i == first // 2:
+            for d in range(down_ahead):
+                down_copy(d, d).start()
+
+    @pl.loop(first, up_steps)
+    def _(i):
+        slot = (i - first) % ahead
+        normalise(i // per_block, i % per_block)
+        for copy in up_copies(i, slot):
+            copy.wait()
+        gate_sum[...] += turned_dot(block[...], gate_slots[slot])
+        up_sum[...] += turned_dot(block[...], up_slots[slot])
+
+        @pl.when(i + ahead < up_steps)
         def _():
-            part = step % per_block
-            s = k % 2
-            at = pl.ds(pl.multiple_of(part * width, 128), width)
-            place_at = pl.multiple_of(block_at * cols + part * width, 128)
-            centered = read(g, s, at)
-            value = (centered + shift[k, 1]) * spread[...] * gain[:, pl.ds(place_at, width)]
-            block = value.astype(BF16)
-            own = packed[g][s * chips, ctx, :, at].astype(F32)
-            own_mean = shift[k, 0, pl.ds(pl.multiple_of(ctx * token_rows, token_rows), token_rows)]
-            hidden[:, pl.ds(place_at, width)] = own + own_mean
-            turned_dot = functools.partial(
-                lax.dot_general,
-                dimension_numbers=(((1,), (1,)), ((), ())),
-                preferred_element_type=F32,
-            )
-
-            @pl.when(step == 0)
-            def _():
-                gate_sum[...] = turned_dot(block, gate_slots[step % ahead])
-                up_sum[...] = turned_dot(block, up_slots[step % ahead])
-
-            @pl.when(step > 0)
-            def _():
-                gate_sum[...] += turned_dot(block, gate_slots[step % ahead])
-                up_sum[...] += turned_dot(block, up_slots[step % ahead])
-
-    @pl.when(step + ahead < up_steps)
-    def _():
-        for copy in up_copies(step + ahead, step % ahead):
-            copy.start()
-
-    first = step + ahead - up_steps
-
-    @pl.when((first >= 0) & (first < down_ahead))
-    def _():
-        down_copy(first, first).start()
-
-    @pl.when(step == up_steps)
-    def _():
-        value = gate_sum[...]
-        value = value / (1.0 + jnp.exp(-value)) * up_sum[...]
-        activated[...] = value.astype(BF16)
-
-    @pl.when(step >= up_steps)
-    def _():
-        done = step - up_steps
-        block = down_slots[done % down_ahead]
-        piece[...] = jnp.dot(activated[...], block, preferred_element_type=F32) * scale[...]
-
-        @pl.when(done + down_ahead < down_steps)
+            for copy in up_copies(i + ahead, slot):
+                copy.start()
+
+    value = gate_sum[...]
+    value = value / (1.0 + jnp.exp(-value)) * up_sum[...]
+    activated[...] = value.astype(BF16)
+
+    @pl.loop(0, down_steps)
+    def _(i):
+        slot = i % down_ahead
+        down_copy(i, slot).wait()
+        value = jnp.dot(activated[...], down_slots[slot], preferred_element_type=F32)
+        piece[...] = value * scale[...]
+
+        @pl.when(i + down_ahead < down_steps)
         def _():
-            down_copy(done + down_ahead, done % down_ahead).start()
-
+            down_copy(i + down_ahead, slot).start()
+
+        place = pl.ds(pl.multiple_of(i * columns, 128), columns)
         for g in range(groups):
             for side in range(2):
                 for s in range(2):
                     for p in range(chips):
-                        row = ((side * chips + p) * C + (ctx ^ (2 * g + s))) * token_rows
+                        k = s * groups + g
+                        row = ((side * chips + p) * C + (ctx ^ k)) * token_rows
                         at = pl.ds(pl.multiple_of(row, token_rows), token_rows)
-                        outs[side * groups + g][s * chips + p] = piece[at, :].astype(BF16)
+                        out = outs[side * groups + g]
+                        out[s * chips + p, :, place] = piece[at, :].astype(BF16)
 
 
 def largest_part(size, most, unit):
     return max(c for c in range(unit, most + 1, unit) if size % c == 0)
 
 
-def run_experts(packed, gain, gate_weight, up_weight, down_weight, C, E):
+def run_experts(packed, gate_held, up_held, gain, weights, down_weight, C, E):
     count = len(packed)
     pieces, _, token_rows, wide = packed[0].shape
     cols = wide - EXTRA
     features = cols * C
-    units = gate_weight.shape[2]
+    units = weights[0].shape[1]
     total = C * E * token_rows
-    small = total <= 256
-    width = largest_part(cols, 768 if small else 384, 128)
-    columns = largest_part(features, 1024 if small else 384, 128)
+    held = len(gate_held)
+    width = largest_part(cols, 768 if held else 384, 128)
+    columns = largest_part(features, 768 if held else 384, 128)
     per_block = cols // width
-    up_steps = C * per_block
-    down_steps = features // columns
-
-    def column_block(i):
-        return (0, 0, jnp.maximum(i - up_steps, 0))
-
-    def whole(*dims):
-        return pl.BlockSpec(dims, lambda i: (0,) * len(dims), pipeline_mode=pl.Buffered(1))
-
-    ahead = 4 if small else 2
-    down_ahead = 3 if small else 2
+    ahead = 3 if held else 2
+    down_ahead = 3 if held else 2
+    operands = [*packed, *gate_held, *up_held, gain]
     *outs, hidden = pl.pallas_call(
-        functools.partial(expert_kernel, C, E, per_block, width, columns),
+        functools.partial(expert_kernel, C, E, per_block, width, columns, held),
         out_shape=[shape((pieces, token_rows, features), BF16) for _ in packed]
         + [shape((token_rows, features), F32)],
-        grid=(up_steps + down_steps,),
-        in_specs=[whole(*packed[0].shape) for _ in packed]
-        + [whole(1, features), IN_HBM, IN_HBM, IN_HBM],
-        out_specs=[pl.BlockSpec((pieces, token_rows, columns), column_block) for _ in packed]
-        + [pl.BlockSpec((token_rows, features), lambda i: (0, 0))],
+        in_specs=[WHOLE] * len(operands) + [IN_HBM] * 3,
+        out_specs=[WHOLE] * (count + 1),
         scratch_shapes=[
             pltpu.VMEM((total, units), F32),
             pltpu.VMEM((total, units), F32),
             pltpu.VMEM((total, units), BF16),
             pltpu.VMEM((total, columns), F32),
+            pltpu.VMEM((total, width), BF16),
             pltpu.VMEM((C, 2, total, 1), F32),
             pltpu.VMEM((total, 1), F32),
             pltpu.VMEM((total, 1), F32),
@@ -404,22 +424,13 @@
             pltpu.SemaphoreType.DMA((2, ahead)),
             pltpu.SemaphoreType.DMA((down_ahead,)),
         ],
-        compiler_params=pltpu.CompilerParams(
-            vmem_limit_bytes=(42 if small else 58) * MIB,
-            dimension_semantics=("arbitrary",),
-        ),
+        compiler_params=pltpu.CompilerParams(vmem_limit_bytes=(35 if held else 58) * MIB),
         cost_estimate=pl.CostEstimate(
             flops=6 * total * features * units,
             bytes_accessed=6 * features * units + 4 * total * features,
             transcendentals=total * units,
         ),
-    )(
-        *packed,
-        gain,
-        jnp.swapaxes(gate_weight, 1, 2),
-        jnp.swapaxes(up_weight, 1, 2),
-        down_weight,
-    )
+    )(*operands, *weights, down_weight)
     return outs, hidden
 
 
@@ -440,7 +451,7 @@
     )
 
 
-def sum_over_plane(own, received, orders):
+def sum_over_plane(own, received, orders, added, apart):
     chips = own.shape[0] // 2
     operands = [own, received]
     holds = [
@@ -459,7 +470,8 @@
             {p: [(2 * s, i), (2 * s + 1, i)] for i, p in enumerate(kept[s])}
             for s in range(len(orders))
         ]
-    return fold([[hold[0]] for hold in holds], operands)
+    parts = [hold[0] + [(4 + i, s) for i in range(len(added))] for s, hold in enumerate(holds)]
+    return fold([[part] for part in parts] if apart else [parts], operands + added)
 
 
 def on_device(
@@ -504,9 +516,12 @@
         [sent[0], out_weight, norm_gain.reshape(1, -1)],
         [WHOLE] * 3,
     )
-    (halves,) = call(
+    halves, own_residual = call(
         functools.partial(halves_kernel, C, E),
-        [shape((C, E, token_rows, HD), BF16)],
+        [
+            shape((C, E, token_rows, HD), BF16),
+            shape((slots - E, token_rows, wide), BF16),
+        ],
         [*messages, weight, gain],
         [WHOLE] * (C + 2),
     )
@@ -544,33 +559,54 @@
     (rows,) = call(
         functools.partial(plane_sum_kernel, C, E, chips - 1),
         [shape((C, token_rows, cols + EXTRA), BF16)],
-        [kept, *received, *messages, extra],
+        [kept, *received, own_residual, *messages[1:], extra],
         [WHOLE] * (chips + C + 1),
     )
 
+    weights = [jnp.swapaxes(gate_weight, 1, 2), jnp.swapaxes(up_weight, 1, 2)]
+    hold = C * E * token_rows <= 256 and C == 4 and len(chip_bits) == 2
+    loaded = []
+
+    def load(which, after):
+        if not hold:
+            return []
+        blocks, token = load_blocks(weights, [(which, 0)], cols, after, 44)
+        loaded.extend(blocks)
+        return [token]
+
     orders = (chip_bits[::-1], chip_bits)
-    near = [rows, swap(rows, "ctx", 1)]
+    near = [rows, swap(rows, "ctx", C // 2)]
     (pair,) = pack([[(0, None), (1, None)]], near, rows.shape)
     pairs = [pair]
-    for bit in range(1, C.bit_length() - 1):
+    for bit in range(C.bit_length() - 2):
         pairs += [swap(value, "ctx", 1 << bit) for value in pairs]
-    group, sends = spread_over_plane(near, [(0, None), (1, None)], orders, chips, [])
+    afters = [[]] * len(chip_bits)
+    group, sends = spread_over_plane(near, [(0, None), (1, None)], orders, chips, afters)
     packed = [group]
+    token = load(0, sends[0])
     for value in pairs[1:]:
-        group, sends = spread_over_plane([value], [(0, 0), (0, 1)], orders, chips, sends)
+        afters = [sends] + [token] * (len(chip_bits) - 1)
+        last = (lambda sent: load(1, sent[0])) if hold else (lambda sent: [])
+        group, sends = spread_over_plane(
+            [value], [(0, 0), (0, 1)], orders, chips, afters, last
+        )
         packed.append(group)
     packed += [swap(group, "exp", 1) for group in packed]
 
-    outs, hidden = run_experts(packed, gain, gate_weight, up_weight, down_weight, C, E)
+    outs, hidden = run_experts(
+        packed, loaded[0::2], loaded[1::2], gain, weights, down_weight, C, E
+    )
 
     count = C // 2
-    shards = [None] * C
+    added = [[] for _ in range(count)]
     for g in reversed(range(count)):
         received = swap(outs[count + g], "exp", 1)
-        shards[2 * g : 2 * g + 2] = sum_over_plane(outs[g], received, orders[::-1])
-    total = hidden
-    for k, shard in enumerate(shards):
-        total = total + (swap(shard, "ctx", k) if k else shard)[0].astype(F32)
+        values = sum_over_plane(outs[g], received, orders[::-1], added[g], g == 0)
+        if g:
+            top = 1 << (g.bit_length() - 1)
+            added[g ^ top].append(swap(values[0], "ctx", top))
+    kept, sent = values
+    total = hidden + kept[0].astype(F32) + swap(sent, "ctx", C // 2)[0].astype(F32)
     return total.astype(BF16)
 
 

time: 116 us -> 112 us (0.966)
  starting transfers between devices: 35.7 us -> 33.8 us
  waiting for transfers between devices: 45.2 us -> 44 us
    pallas_call x0 -> x2, Pallas kernels: none -> 4.35 us  [load_blocks(): pl.pallas_call(functools.partial(load_kernel, blocks), out_shape=[shape((...]
    pallas_call x1, Pallas kernels: 24.3 us -> 20.7 us  [run_experts(): pl.pallas_call(functools.partial(expert_kernel, C, E, per_block, width, c...]
    ppermute x33 -> x32, starting transfers between devices: 35.7 us -> 33.8 us  [swap(): lax.ppermute(value, axis, [(i, i ^ mask) for i in range(lax.axis_size(axi...]
    ppermute x33 -> x32, waiting for transfers between devices: 45.2 us -> 44 us  [swap(): lax.ppermute(value, axis, [(i, i ^ mask) for i in range(lax.axis_size(axi...]
    unnamed x8 -> x10, local copies, waits for them, and re-layouts: 3.79 us -> 2.9 us
  transfers between devices with their start and end apart: 33 -> 32, of which waited for: 24 -> 20; matrix products, arithmetic and copies ran while one was open for 1% -> 0% of each run, Pallas kernels for 1% -> 5%
where the time goes in v1:
time: 112 us; the launch traced here: 111 us
  waiting for transfers between devices  44 us (39%)
  starting transfers between devices  33.8 us (30%)
  Pallas kernels  29.6 us (26%)
  local copies, waits for them, and re-layouts  2.9 us (3%)
    ppermute x32, waiting for transfers between devices, swap(): lax.ppermute(value, axis, [(i, i ^ mask) for i in range(lax.axis_size(axi...  44 us
    ppermute x32, starting transfers between devices, swap(): lax.ppermute(value, axis, [(i, i ^ mask) for i in range(lax.axis_size(axi...  33.8 us
    pallas_call x1, Pallas kernels, run_experts(): pl.pallas_call(functools.partial(expert_kernel, C, E, per_block, width, c...  20.7 us
    pallas_call x18, Pallas kernels, call(): pl.pallas_call(kernel, out_shape=out_shape, in_specs=in_specs, out_specs=...  4.5 us
    pallas_call x2, Pallas kernels, load_blocks(): pl.pallas_call(functools.partial(load_kernel, blocks), out_shape=[shape((...  4.35 us
    unnamed x10, local copies, waits for them, and re-layouts  2.9 us
  transfers between devices with their start and end apart: 32, of which 20 were waited for; matrix products, arithmetic and copies ran while one was open for 0% of the time, Pallas kernels for 5%

profile of v1, /device:TPU:0, one launch (start us, length us, event | category | flops | bytes accessed | tf_op | source)
XLA Modules:
  0.0 111.4 jit_solution(17175186938377265089)
XLA Ops:
  0.0 1.8 %shard_map.100 = (bf16[11,8,512]{2,1,0:T(8,128)(2,1)}, bf16[11,8,512]{2,1,0:T(8,128)(2,1)}, bf16[11,8,512]{2,1,0:T(8,128)(2,1)}, bf16[11,8,512]{2,1,0:T(8,128)(2,1)}) custom-call(bf16[64,384]{1,0:T(8,128)(2,1)} %queries_in.1, bf16[2,64,64]{2,1,0:T(8,128)(2,1)} %own_in.1, bf16[8,6144]{1,0:T(8,128)(2,1)} %residual_in.1), custom_call_target="tpu_custom_call" | custom-call | tf_op jit(solution)/shard_map/pallas_call | solution.py:27
  1.8 3.1 %collective-permute-start = (bf16[11,8,512]{2,1,0:T(8,128)(2,1)}, bf16[11,8,512]{2,1,0:T(8,128)(2,1)S(1)}, u32[]{:S(2)}, u32[]{:S(2)}) collective-permute-start(bf16[11,8,512]{2,1,0:T(8,128)(2,1)} %get-tuple-element.53), channel_id=1, source_target_pairs={{0,8},{8,0},{16,24},{24,16},{1,9},{9,1},{17,25},{25,17},{2,10},{10... | collective-permute-start | bytes 270344 | tf_op jit(solution)/shard_map/ppermute | solution.py:23
  4.9 2.6 %collective-permute-start.1 = (bf16[11,8,512]{2,1,0:T(8,128)(2,1)}, bf16[11,8,512]{2,1,0:T(8,128)(2,1)S(1)}, u32[]{:S(2)}, u32[]{:S(2)}) collective-permute-start(bf16[11,8,512]{2,1,0:T(8,128)(2,1)} %get-tuple-element.54), channel_id=1, source_target_pairs={{0,16},{8,24},{16,0},{24,8},{1,17},{9,25},{17,1},{25,9},{2,18},{10... | collective-permute-start | bytes 270344 | tf_op jit(solution)/shard_map/ppermute | solution.py:23
  10.5 4.4 %collective-permute-done.1.refs_2_.refs_6_ = bf16[11,8,512]{2,1,0:T(8,128)(2,1)S(1)} collective-permute-done((bf16[11,8,512]{2,1,0:T(8,128)(2,1)}, bf16[11,8,512]{2,1,0:T(8,128)(2,1)S(1)}, u32[]{:S(2)}, u32[]{:S(2)}) %collective-permute-start.1) | collective-permute-done | bytes 90144 | tf_op jit(solution)/shard_map/ppermute | solution.py:23
  16.3 1.4 %shard_map.103 = (bf16[4,4,8,1536]{3,2,1,0:T(8,128)(2,1)S(1)}, f32[4,4,8,1536]{3,2,1,0:T(8,128)S(1)}) custom-call(bf16[11,8,512]{2,1,0:T(8,128)(2,1)S(1)} %copy-done.1, bf16[11,8,512]{2,1,0:T(8,128)(2,1)S(1)} %collective-permute-done.refs_1_.refs_5_, bf16[11,8,512]{2,1,0:T(8,128)(2,1)S(1)} %collective-permute-done.1.refs_2_.refs_6_, ...), custom_call_target="tpu_custom_call" | custom-call | tf_op jit(solution)/shard_map/pallas_call | solution.py:27
  18.0 1.5 %collective-permute-done.4.received = bf16[4,4,8,1536]{3,2,1,0:T(8,128)(2,1)S(1)} collective-permute-done((bf16[4,4,8,1536]{3,2,1,0:T(8,128)(2,1)S(1)}, bf16[4,4,8,1536]{3,2,1,0:T(8,128)(2,1)S(1)}, u32[]{:S(2)}, u32[]{:S(2)}) %collective-permute-start.4) | collective-permute-done | bytes 393248 | tf_op jit(solution)/shard_map/ppermute | solution.py:23
  19.5 1.6 %collective-permute-start.5 = (bf16[4,8,1536]{2,1,0:T(8,128)(2,1)S(1)}, bf16[4,8,1536]{2,1,0:T(8,128)(2,1)S(1)}, u32[]{:S(2)}, u32[]{:S(2)}) collective-permute-start(bf16[4,8,1536]{2,1,0:T(8,128)(2,1)S(1)} %get-tuple-element.62), channel_id=1, source_target_pairs={{0,2},{1,3},{2,0},{3,1},{4,6},{5,7},{6,4},{7,5},{8,10},{9,11},{10,... | collective-permute-start | bytes 294920 | tf_op jit(solution)/shard_map/ppermute | solution.py:23
  21.1 1.5 %collective-permute-start.6 = (bf16[4,8,1536]{2,1,0:T(8,128)(2,1)S(1)}, bf16[4,8,1536]{2,1,0:T(8,128)(2,1)S(1)}, u32[]{:S(2)}, u32[]{:S(2)}) collective-permute-start(bf16[4,8,1536]{2,1,0:T(8,128)(2,1)S(1)} %get-tuple-element.63), channel_id=1, source_target_pairs={{0,4},{1,5},{2,6},{3,7},{4,0},{5,1},{6,2},{7,3},{8,12},{9,13},{10,... | collective-permute-start | bytes 294920 | tf_op jit(solution)/shard_map/ppermute | solution.py:23
  23.2 1.3 %collective-permute-done.5.refs_1_ = bf16[4,8,1536]{2,1,0:T(8,128)(2,1)S(1)} collective-permute-done((bf16[4,8,1536]{2,1,0:T(8,128)(2,1)S(1)}, bf16[4,8,1536]{2,1,0:T(8,128)(2,1)S(1)}, u32[]{:S(2)}, u32[]{:S(2)}) %collective-permute-start.5) | collective-permute-done | bytes 98336 | tf_op jit(solution)/shard_map/ppermute | solution.py:23
  24.5 2.4 %collective-permute-done.6.refs_2_ = bf16[4,8,1536]{2,1,0:T(8,128)(2,1)S(1)} collective-permute-done((bf16[4,8,1536]{2,1,0:T(8,128)(2,1)S(1)}, bf16[4,8,1536]{2,1,0:T(8,128)(2,1)S(1)}, u32[]{:S(2)}, u32[]{:S(2)}) %collective-permute-start.6) | collective-permute-done | bytes 98336 | tf_op jit(solution)/shard_map/ppermute | solution.py:23
  28.4 2.6 %collective-permute-start.8 = (bf16[4,8,1664]{2,1,0:T(8,128)(2,1)S(1)}, bf16[4,8,1664]{2,1,0:T(8,128)(2,1)S(1)}, u32[]{:S(2)}, u32[]{:S(2)}) collective-permute-start(bf16[4,8,1664]{2,1,0:T(8,128)(2,1)S(1)} %shard_map.105.refs_0_), channel_id=1, source_target_pairs={{0,16},{8,24},{16,0},{24,8},{1,17},{9,25},{17,1},{25,9},{2,18},{10... | collective-permute-start | bytes 319496 | tf_op jit(solution)/shard_map/ppermute | solution.py:23
  31.0 4.2 %collective-permute-done.8.refs_1_ = bf16[4,8,1664]{2,1,0:T(8,128)(2,1)S(1)} collective-permute-done((bf16[4,8,1664]{2,1,0:T(8,128)(2,1)S(1)}, bf16[4,8,1664]{2,1,0:T(8,128)(2,1)S(1)}, u32[]{:S(2)}, u32[]{:S(2)}) %collective-permute-start.8) | collective-permute-done | bytes 106528 | tf_op jit(solution)/shard_map/ppermute | solution.py:23
  37.5 3.5 %collective-permute-done.9.refs_2_ = bf16[4,8,1664]{2,1,0:T(8,128)(2,1)S(1)} collective-permute-done((bf16[4,8,1664]{2,1,0:T(8,128)(2,1)S(1)}, bf16[4,8,1664]{2,1,0:T(8,128)(2,1)S(1)}, u32[]{:S(2)}, u32[]{:S(2)}) %collective-permute-start.9) | collective-permute-done | bytes 106528 | tf_op jit(solution)/shard_map/ppermute | solution.py:23
  41.0 1.5 %collective-permute-done.10.refs_3_ = bf16[4,8,1664]{2,1,0:T(8,128)(2,1)S(1)} collective-permute-done((bf16[4,8,1664]{2,1,0:T(8,128)(2,1)S(1)}, bf16[4,8,1664]{2,1,0:T(8,128)(2,1)S(1)}, u32[]{:S(2)}, u32[]{:S(2)}) %collective-permute-start.10) | collective-permute-done | bytes 106528 | tf_op jit(solution)/shard_map/ppermute | solution.py:23
  44.8 1.9 %collective-permute-start.11 = (bf16[2,4,8,1664]{3,2,1,0:T(8,128)(2,1)S(1)}, bf16[2,4,8,1664]{3,2,1,0:T(8,128)(2,1)S(1)}, u32[]{:S(2)}, u32[]{:S(2)}) collective-permute-start(bf16[2,4,8,1664]{3,2,1,0:T(8,128)(2,1)S(1)} %get-tuple-element.66.refs_1_.refs_2_), channel_id=1, source_target_pairs={{0,2},{1,3},{2,0},{3,1},{4,6},{5,7},{6,4},{7,5},{8,10},{9,11},{10,... | collective-permute-start | bytes 638984 | tf_op jit(solution)/shard_map/ppermute | solution.py:23
  46.7 2.2 %shard_map.110 = (bf16[1344,1536]{1,0:T(8,128)(2,1)S(1)}, f32[8,128]{1,0:T(8,128)S(1)}) custom-call(bf16[1,1344,6144]{2,1,0:T(8,128)(2,1)} %bitcast.10, bf16[1,1344,6144]{2,1,0:T(8,128)(2,1)} %bitcast.13, bf16[2,4,8,1664]{3,2,1,0:T(8,128)(2,1)S(1)} %get-tuple-element.66.refs_1_.refs_2_), custom_call_target="tpu_custom_call" | custom-call | bytes 8257536 | tf_op jit(solution)/shard_map/pallas_call | solution.py:237
  49.0 1.7 %collective-permute-start.17 = (bf16[2,4,8,1664]{3,2,1,0:T(8,128)(2,1)S(1)}, bf16[2,4,8,1664]{3,2,1,0:T(8,128)(2,1)S(1)}, u32[]{:S(2)}, u32[]{:S(2)}) collective-permute-start(bf16[2,4,8,1664]{3,2,1,0:T(8,128)(2,1)S(1)} %get-tuple-element.72), channel_id=1, source_target_pairs={{0,4},{1,5},{2,6},{3,7},{4,0},{5,1},{6,2},{7,3},{8,12},{9,13},{10,... | collective-permute-start | bytes 638984 | tf_op jit(solution)/shard_map/ppermute | solution.py:23
  50.6 2.2 %shard_map.112 = (bf16[1344,1536]{1,0:T(8,128)(2,1)S(1)}, f32[8,128]{1,0:T(8,128)S(1)}) custom-call(bf16[1,1344,6144]{2,1,0:T(8,128)(2,1)} %bitcast.11, bf16[1,1344,6144]{2,1,0:T(8,128)(2,1)} %bitcast.14, bf16[2,4,8,1664]{3,2,1,0:T(8,128)(2,1)S(1)} %get-tuple-element.71.refs_2_), custom_call_target="tpu_custom_call" | custom-call | bytes 8257536 | tf_op jit(solution)/shard_map/pallas_call | solution.py:237
  53.0 1.9 %collective-permute-done.17.refs_4_ = bf16[2,4,8,1664]{3,2,1,0:T(8,128)(2,1)S(1)} collective-permute-done((bf16[2,4,8,1664]{3,2,1,0:T(8,128)(2,1)S(1)}, bf16[2,4,8,1664]{3,2,1,0:T(8,128)(2,1)S(1)}, u32[]{:S(2)}, u32[]{:S(2)}) %collective-permute-start.17) | collective-permute-done | bytes 213024 | tf_op jit(solution)/shard_map/ppermute | solution.py:23
  54.9 1.6 %collective-permute-done.16.refs_3_ = bf16[2,4,8,1664]{3,2,1,0:T(8,128)(2,1)S(1)} collective-permute-done((bf16[2,4,8,1664]{3,2,1,0:T(8,128)(2,1)S(1)}, bf16[2,4,8,1664]{3,2,1,0:T(8,128)(2,1)S(1)}, u32[]{:S(2)}, u32[]{:S(2)}) %collective-permute-start.16) | collective-permute-done | bytes 213024 | tf_op jit(solution)/shard_map/ppermute | solution.py:23
  56.6 2.4 %collective-permute-done.19.refs_3_ = bf16[8,4,8,1664]{3,2,1,0:T(8,128)(2,1)S(1)} collective-permute-done((bf16[8,4,8,1664]{3,2,1,0:T(8,128)(2,1)S(1)}, bf16[8,4,8,1664]{3,2,1,0:T(8,128)(2,1)S(1)}, u32[]{:S(2)}, u32[]{:S(2)}) %collective-permute-start.19) | collective-permute-done | bytes 852000 | tf_op jit(solution)/shard_map/ppermute | solution.py:23
  59.0 20.7 %shard_map.114 = (bf16[8,8,6144]{2,1,0:T(8,128)(2,1)S(1)}, bf16[8,8,6144]{2,1,0:T(8,128)(2,1)S(1)}, bf16[8,8,6144]{2,1,0:T(8,128)(2,1)S(1)}, bf16[8,8,6144]{2,1,0:T(8,128)(2,1)S(1)}, f32[8,6144]{1,0:T(8,128)S(1)}) custom-call(bf16[8,4,8,1664]{3,2,1,0:T(8,128)(2,1)S(1)} %shard_map.107.refs_0_, bf16[8,4,8,1664]{3,2,1,0:T(8,128)(2,1)S(1)} %shard_map.113.refs_1_, ...), custom_call_target="tpu_custom_call" | custom-call | flops 12683575296 | bytes 55836672 | tf_op jit(solution)/shard_map/pallas_call | solution.py:406
  80.3 1.8 %collective-permute-done.25.refs_1_ = bf16[8,8,6144]{2,1,0:T(8,128)(2,1)S(1)} collective-permute-done((bf16[8,8,6144]{2,1,0:T(8,128)(2,1)S(1)}, bf16[8,8,6144]{2,1,0:T(8,128)(2,1)S(1)}, u32[]{:S(2)}, u32[]{:S(2)}) %collective-permute-start.25) | collective-permute-done | bytes 786464 | tf_op jit(solution)/shard_map/ppermute | solution.py:23
  83.4 1.7 %collective-permute-start.21 = (bf16[2,8,6144]{2,1,0:T(8,128)(2,1)S(1)}, bf16[2,8,6144]{2,1,0:T(8,128)(2,1)S(1)}, u32[]{:S(2)}, u32[]{:S(2)}) collective-permute-start(bf16[2,8,6144]{2,1,0:T(8,128)(2,1)S(1)} %get-tuple-element.80), channel_id=1, source_target_pairs={{0,2},{1,3},{2,0},{3,1},{4,6},{5,7},{6,4},{7,5},{8,10},{9,11},{10,... | collective-permute-start | bytes 589832 | tf_op jit(solution)/shard_map/ppermute | solution.py:23
  85.0 1.6 %collective-permute-start.22 = (bf16[2,8,6144]{2,1,0:T(8,128)(2,1)S(1)}, bf16[2,8,6144]{2,1,0:T(8,128)(2,1)S(1)}, u32[]{:S(2)}, u32[]{:S(2)}) collective-permute-start(bf16[2,8,6144]{2,1,0:T(8,128)(2,1)S(1)} %get-tuple-element.82), channel_id=1, source_target_pairs={{0,4},{1,5},{2,6},{3,7},{4,0},{5,1},{6,2},{7,3},{8,12},{9,13},{10,... | collective-permute-start | bytes 589832 | tf_op jit(solution)/shard_map/ppermute | solution.py:23
  86.6 3.4 %collective-permute-done.26.refs_1_ = bf16[2,8,6144]{2,1,0:T(8,128)(2,1)S(1)} collective-permute-done((bf16[2,8,6144]{2,1,0:T(8,128)(2,1)S(1)}, bf16[2,8,6144]{2,1,0:T(8,128)(2,1)S(1)}, u32[]{:S(2)}, u32[]{:S(2)}) %collective-permute-start.26) | collective-permute-done | bytes 196640 | tf_op jit(solution)/shard_map/ppermute | solution.py:23
  91.1 1.6 %collective-permute-start.29 = (bf16[1,8,6144]{2,1,0:T(8,128)(2,1)S(1)}, bf16[1,8,6144]{2,1,0:T(8,128)(2,1)S(1)}, u32[]{:S(2)}, u32[]{:S(2)}) collective-permute-start(bf16[1,8,6144]{2,1,0:T(8,128)(2,1)S(1)} %get-tuple-element.96), channel_id=1, source_target_pairs={{0,2},{1,3},{2,0},{3,1},{4,6},{5,7},{6,4},{7,5},{8,10},{9,11},{10,... | collective-permute-start | bytes 294920 | tf_op jit(solution)/shard_map/ppermute | solution.py:23
  92.7 2.9 %collective-permute-done.28.refs_1_ = bf16[1,8,6144]{2,1,0:T(8,128)(2,1)S(1)} collective-permute-done((bf16[1,8,6144]{2,1,0:T(8,128)(2,1)S(1)}, bf16[1,8,6144]{2,1,0:T(8,128)(2,1)S(1)}, u32[]{:S(2)}, u32[]{:S(2)}) %collective-permute-start.28) | collective-permute-done | bytes 98336 | tf_op jit(solution)/shard_map/ppermute | solution.py:23
  95.8 3.1 %collective-permute-start.30 = (bf16[2,8,6144]{2,1,0:T(8,128)(2,1)S(1)}, bf16[2,8,6144]{2,1,0:T(8,128)(2,1)S(1)}, u32[]{:S(2)}, u32[]{:S(2)}) collective-permute-start(bf16[2,8,6144]{2,1,0:T(8,128)(2,1)S(1)} %shard_map.119), channel_id=1, source_target_pairs={{0,8},{8,0},{16,24},{24,16},{1,9},{9,1},{17,25},{25,17},{2,10},{10... | collective-permute-start | bytes 589832 | tf_op jit(solution)/shard_map/ppermute | solution.py:23
  100.6 3.0 %collective-permute-done.23.refs_1_ = bf16[1,8,6144]{2,1,0:T(8,128)(2,1)S(1)} collective-permute-done((bf16[1,8,6144]{2,1,0:T(8,128)(2,1)S(1)}, bf16[1,8,6144]{2,1,0:T(8,128)(2,1)S(1)}, u32[]{:S(2)}, u32[]{:S(2)}) %collective-permute-start.23) | collective-permute-done | bytes 98336 | tf_op jit(solution)/shard_map/ppermute | solution.py:23
  104.2 1.5 %collective-permute-start.31 = (bf16[1,8,6144]{2,1,0:T(8,128)(2,1)S(1)}, bf16[1,8,6144]{2,1,0:T(8,128)(2,1)S(1)}, u32[]{:S(2)}, u32[]{:S(2)}) collective-permute-start(bf16[1,8,6144]{2,1,0:T(8,128)(2,1)S(1)} %get-tuple-element.98), channel_id=1, source_target_pairs={{0,16},{8,24},{16,0},{24,8},{1,17},{9,25},{17,1},{25,9},{2,18},{10... | collective-permute-start | bytes 294920 | tf_op jit(solution)/shard_map/ppermute | solution.py:23
  105.7 4.9 %collective-permute-done.31 = bf16[1,8,6144]{2,1,0:T(8,128)(2,1)S(1)} collective-permute-done((bf16[1,8,6144]{2,1,0:T(8,128)(2,1)S(1)}, bf16[1,8,6144]{2,1,0:T(8,128)(2,1)S(1)}, u32[]{:S(2)}, u32[]{:S(2)}) %collective-permute-start.31) | collective-permute-done | bytes 98336 | tf_op jit(solution)/shard_map/ppermute | solution.py:23
  (67 shorter events, 17.7 us)
Async XLA Ops:
  1.8 8.7 %collective-permute-start = (bf16[11,8,512]{2,1,0:T(8,128)(2,1)}, bf16[11,8,512]{2,1,0:T(8,128)(2,1)S(1)}, u32[]{:S(2)}, u32[]{:S(2)}) collective-permute-start(bf16[11,8,512]{2,1,0:T(8,128)(2,1)} %get-tuple-element.53), channel_id=1, source_target_pairs={{0,8},{8,0},{16,24},{24,16},{1,9},{9,1},{17,25},{25,17},{2,10},{10... | collective-permute-start | bytes 270344 | tf_op jit(solution)/shard_map/ppermute | solution.py:23
  4.9 10.0 %collective-permute-start.1 = (bf16[11,8,512]{2,1,0:T(8,128)(2,1)}, bf16[11,8,512]{2,1,0:T(8,128)(2,1)S(1)}, u32[]{:S(2)}, u32[]{:S(2)}) collective-permute-start(bf16[11,8,512]{2,1,0:T(8,128)(2,1)} %get-tuple-element.54), channel_id=1, source_target_pairs={{0,16},{8,24},{16,0},{24,8},{1,17},{9,25},{17,1},{25,9},{2,18},{10... | collective-permute-start | bytes 270344 | tf_op jit(solution)/shard_map/ppermute | solution.py:23
  7.5 7.4 %collective-permute-start.2 = (bf16[11,8,512]{2,1,0:T(8,128)(2,1)}, bf16[11,8,512]{2,1,0:T(8,128)(2,1)S(1)}, u32[]{:S(2)}, u32[]{:S(2)}) collective-permute-start(bf16[11,8,512]{2,1,0:T(8,128)(2,1)} %get-tuple-element.55), channel_id=1, source_target_pairs={{0,24},{8,16},{16,8},{24,0},{1,25},{9,17},{17,9},{25,1},{2,26},{10... | collective-permute-start | bytes 270344 | tf_op jit(solution)/shard_map/ppermute | solution.py:23
  14.9 1.3 %collective-permute-start.3 = (bf16[4,8,8,128]{3,2,1,0:T(8,128)(2,1)S(1)}, bf16[4,8,8,128]{3,2,1,0:T(8,128)(2,1)S(1)}, u32[]{:S(2)}, u32[]{:S(2)}) collective-permute-start(bf16[4,8,8,128]{3,2,1,0:T(8,128)(2,1)S(1)} %get-tuple-element.58), channel_id=1, source_target_pairs={{0,1},{1,0},{2,3},{3,2},{4,5},{5,4},{6,7},{7,6},{8,9},{9,8},{10,11... | collective-permute-start | bytes 196616 | tf_op jit(solution)/shard_map/ppermute | solution.py:23
  17.7 1.8 %collective-permute-start.4 = (bf16[4,4,8,1536]{3,2,1,0:T(8,128)(2,1)S(1)}, bf16[4,4,8,1536]{3,2,1,0:T(8,128)(2,1)S(1)}, u32[]{:S(2)}, u32[]{:S(2)}) collective-permute-start(bf16[4,4,8,1536]{3,2,1,0:T(8,128)(2,1)S(1)} %get-tuple-element.60), channel_id=1, source_target_pairs={{0,1},{1,0},{2,3},{3,2},{4,5},{5,4},{6,7},{7,6},{8,9},{9,8},{10,11... | collective-permute-start | bytes 1179656 | tf_op jit(solution)/shard_map/ppermute | solution.py:23
  19.5 4.9 %collective-permute-start.5 = (bf16[4,8,1536]{2,1,0:T(8,128)(2,1)S(1)}, bf16[4,8,1536]{2,1,0:T(8,128)(2,1)S(1)}, u32[]{:S(2)}, u32[]{:S(2)}) collective-permute-start(bf16[4,8,1536]{2,1,0:T(8,128)(2,1)S(1)} %get-tuple-element.62), channel_id=1, source_target_pairs={{0,2},{1,3},{2,0},{3,1},{4,6},{5,7},{6,4},{7,5},{8,10},{9,11},{10,... | collective-permute-start | bytes 294920 | tf_op jit(solution)/shard_map/ppermute | solution.py:23
  21.1 5.8 %collective-permute-start.6 = (bf16[4,8,1536]{2,1,0:T(8,128)(2,1)S(1)}, bf16[4,8,1536]{2,1,0:T(8,128)(2,1)S(1)}, u32[]{:S(2)}, u32[]{:S(2)}) collective-permute-start(bf16[4,8,1536]{2,1,0:T(8,128)(2,1)S(1)} %get-tuple-element.63), channel_id=1, source_target_pairs={{0,4},{1,5},{2,6},{3,7},{4,0},{5,1},{6,2},{7,3},{8,12},{9,13},{10,... | collective-permute-start | bytes 294920 | tf_op jit(solution)/shard_map/ppermute | solution.py:23
  22.6 5.5 %collective-permute-start.7 = (bf16[4,8,1536]{2,1,0:T(8,128)(2,1)S(1)}, bf16[4,8,1536]{2,1,0:T(8,128)(2,1)S(1)}, u32[]{:S(2)}, u32[]{:S(2)}) collective-permute-start(bf16[4,8,1536]{2,1,0:T(8,128)(2,1)S(1)} %get-tuple-element.64), channel_id=1, source_target_pairs={{0,6},{1,7},{2,4},{3,5},{4,2},{5,3},{6,0},{7,1},{8,14},{9,15},{10,... | collective-permute-start | bytes 294920 | tf_op jit(solution)/shard_map/ppermute | solution.py:23
  28.4 6.8 %collective-permute-start.8 = (bf16[4,8,1664]{2,1,0:T(8,128)(2,1)S(1)}, bf16[4,8,1664]{2,1,0:T(8,128)(2,1)S(1)}, u32[]{:S(2)}, u32[]{:S(2)}) collective-permute-start(bf16[4,8,1664]{2,1,0:T(8,128)(2,1)S(1)} %shard_map.105.refs_0_), channel_id=1, source_target_pairs={{0,16},{8,24},{16,0},{24,8},{1,17},{9,25},{17,1},{25,9},{2,18},{10... | collective-permute-start | bytes 319496 | tf_op jit(solution)/shard_map/ppermute | solution.py:23
  35.2 7.4 %collective-permute-start.13 = (bf16[2,4,8,1664]{3,2,1,0:T(8,128)(2,1)S(1)}, bf16[2,4,8,1664]{3,2,1,0:T(8,128)(2,1)S(1)}, u32[]{:S(2)}, u32[]{:S(2)}) collective-permute-start(bf16[2,4,8,1664]{3,2,1,0:T(8,128)(2,1)S(1)} %shard_map.108), channel_id=1, source_target_pairs={{0,8},{8,0},{16,24},{24,16},{1,9},{9,1},{17,25},{25,17},{2,10},{10... | collective-permute-start | bytes 638984 | tf_op jit(solution)/shard_map/ppermute | solution.py:23
  35.8 5.2 %collective-permute-start.9 = (bf16[4,8,1664]{2,1,0:T(8,128)(2,1)S(1)}, bf16[4,8,1664]{2,1,0:T(8,128)(2,1)S(1)}, u32[]{:S(2)}, u32[]{:S(2)}) collective-permute-start(bf16[4,8,1664]{2,1,0:T(8,128)(2,1)S(1)} %shard_map.105.refs_0_), channel_id=1, source_target_pairs={{0,4},{1,5},{2,6},{3,7},{4,0},{5,1},{6,2},{7,3},{8,12},{9,13},{10,... | collective-permute-start | bytes 319496 | tf_op jit(solution)/shard_map/ppermute | solution.py:23
  37.0 5.6 %collective-permute-start.10 = (bf16[4,8,1664]{2,1,0:T(8,128)(2,1)S(1)}, bf16[4,8,1664]{2,1,0:T(8,128)(2,1)S(1)}, u32[]{:S(2)}, u32[]{:S(2)}) collective-permute-start(bf16[4,8,1664]{2,1,0:T(8,128)(2,1)S(1)} %collective-permute-done.8.refs_1_), channel_id=1, source_target_pairs={{0,2},{1,3},{2,0},{3,1},{4,6},{5,7},{6,4},{7,5},{8,10},{9,11},{10,... | collective-permute-start | bytes 319496 | tf_op jit(solution)/shard_map/ppermute | solution.py:23
  42.6 6.3 %collective-permute-start.14 = (bf16[4,8,1664]{2,1,0:T(8,128)(2,1)S(1)}, bf16[4,8,1664]{2,1,0:T(8,128)(2,1)S(1)}, u32[]{:S(2)}, u32[]{:S(2)}) collective-permute-start(bf16[4,8,1664]{2,1,0:T(8,128)(2,1)S(1)} %get-tuple-element.68), channel_id=1, source_target_pairs={{0,4},{1,5},{2,6},{3,7},{4,0},{5,1},{6,2},{7,3},{8,12},{9,13},{10,... | collective-permute-start | bytes 319496 | tf_op jit(solution)/shard_map/ppermute | solution.py:23
  43.0 5.9 %collective-permute-start.15 = (bf16[4,8,1664]{2,1,0:T(8,128)(2,1)S(1)}, bf16[4,8,1664]{2,1,0:T(8,128)(2,1)S(1)}, u32[]{:S(2)}, u32[]{:S(2)}) collective-permute-start(bf16[4,8,1664]{2,1,0:T(8,128)(2,1)S(1)} %get-tuple-element.69), channel_id=1, source_target_pairs={{0,2},{1,3},{2,0},{3,1},{4,6},{5,7},{6,4},{7,5},{8,10},{9,11},{10,... | collective-permute-start | bytes 319496 | tf_op jit(solution)/shard_map/ppermute | solution.py:23
  43.8 9.0 %collective-permute-start.12 = (bf16[2,4,8,1664]{3,2,1,0:T(8,128)(2,1)S(1)}, bf16[2,4,8,1664]{3,2,1,0:T(8,128)(2,1)S(1)}, u32[]{:S(2)}, u32[]{:S(2)}) collective-permute-start(bf16[2,4,8,1664]{3,2,1,0:T(8,128)(2,1)S(1)} %get-tuple-element.67.refs_2_), channel_id=1, source_target_pairs={{0,4},{1,5},{2,6},{3,7},{4,0},{5,1},{6,2},{7,3},{8,12},{9,13},{10,... | collective-permute-start | bytes 638984 | tf_op jit(solution)/shard_map/ppermute | solution.py:23
  44.8 8.0 %collective-permute-start.11 = (bf16[2,4,8,1664]{3,2,1,0:T(8,128)(2,1)S(1)}, bf16[2,4,8,1664]{3,2,1,0:T(8,128)(2,1)S(1)}, u32[]{:S(2)}, u32[]{:S(2)}) collective-permute-start(bf16[2,4,8,1664]{3,2,1,0:T(8,128)(2,1)S(1)} %get-tuple-element.66.refs_1_.refs_2_), channel_id=1, source_target_pairs={{0,2},{1,3},{2,0},{3,1},{4,6},{5,7},{6,4},{7,5},{8,10},{9,11},{10,... | collective-permute-start | bytes 638984 | tf_op jit(solution)/shard_map/ppermute | solution.py:23
  49.0 5.9 %collective-permute-start.17 = (bf16[2,4,8,1664]{3,2,1,0:T(8,128)(2,1)S(1)}, bf16[2,4,8,1664]{3,2,1,0:T(8,128)(2,1)S(1)}, u32[]{:S(2)}, u32[]{:S(2)}) collective-permute-start(bf16[2,4,8,1664]{3,2,1,0:T(8,128)(2,1)S(1)} %get-tuple-element.72), channel_id=1, source_target_pairs={{0,4},{1,5},{2,6},{3,7},{4,0},{5,1},{6,2},{7,3},{8,12},{9,13},{10,... | collective-permute-start | bytes 638984 | tf_op jit(solution)/shard_map/ppermute | solution.py:23
  50.6 5.8 %collective-permute-start.16 = (bf16[2,4,8,1664]{3,2,1,0:T(8,128)(2,1)S(1)}, bf16[2,4,8,1664]{3,2,1,0:T(8,128)(2,1)S(1)}, u32[]{:S(2)}, u32[]{:S(2)}) collective-permute-start(bf16[2,4,8,1664]{3,2,1,0:T(8,128)(2,1)S(1)} %get-tuple-element.71.refs_2_), channel_id=1, source_target_pairs={{0,2},{1,3},{2,0},{3,1},{4,6},{5,7},{6,4},{7,5},{8,10},{9,11},{10,... | collective-permute-start | bytes 638984 | tf_op jit(solution)/shard_map/ppermute | solution.py:23
  52.9 3.7 %collective-permute-start.18 = (bf16[8,4,8,1664]{3,2,1,0:T(8,128)(2,1)S(1)}, bf16[8,4,8,1664]{3,2,1,0:T(8,128)(2,1)S(1)}, u32[]{:S(2)}, u32[]{:S(2)}) collective-permute-start(bf16[8,4,8,1664]{3,2,1,0:T(8,128)(2,1)S(1)} %shard_map.107.refs_0_), channel_id=1, source_target_pairs={{0,1},{1,0},{2,3},{3,2},{4,5},{5,4},{6,7},{7,6},{8,9},{9,8},{10,11... | collective-permute-start | bytes 2555912 | tf_op jit(solution)/shard_map/ppermute | solution.py:23
  56.5 2.4 %collective-permute-start.19 = (bf16[8,4,8,1664]{3,2,1,0:T(8,128)(2,1)S(1)}, bf16[8,4,8,1664]{3,2,1,0:T(8,128)(2,1)S(1)}, u32[]{:S(2)}, u32[]{:S(2)}) collective-permute-start(bf16[8,4,8,1664]{3,2,1,0:T(8,128)(2,1)S(1)} %shard_map.113.refs_1_), channel_id=1, source_target_pairs={{0,1},{1,0},{2,3},{3,2},{4,5},{5,4},{6,7},{7,6},{8,9},{9,8},{10,11... | collective-permute-start | bytes 2555912 | tf_op jit(solution)/shard_map/ppermute | solution.py:23
  79.7 2.4 %collective-permute-start.25 = (bf16[8,8,6144]{2,1,0:T(8,128)(2,1)S(1)}, bf16[8,8,6144]{2,1,0:T(8,128)(2,1)S(1)}, u32[]{:S(2)}, u32[]{:S(2)}) collective-permute-start(bf16[8,8,6144]{2,1,0:T(8,128)(2,1)S(1)} %get-tuple-element.88), channel_id=1, source_target_pairs={{0,1},{1,0},{2,3},{3,2},{4,5},{5,4},{6,7},{7,6},{8,9},{9,8},{10,11... | collective-permute-start | bytes 2359304 | tf_op jit(solution)/shard_map/ppermute | solution.py:23
  79.9 3.3 %collective-permute-start.20 = (bf16[8,8,6144]{2,1,0:T(8,128)(2,1)S(1)}, bf16[8,8,6144]{2,1,0:T(8,128)(2,1)S(1)}, u32[]{:S(2)}, u32[]{:S(2)}) collective-permute-start(bf16[8,8,6144]{2,1,0:T(8,128)(2,1)S(1)} %get-tuple-element.78), channel_id=1, source_target_pairs={{0,1},{1,0},{2,3},{3,2},{4,5},{5,4},{6,7},{7,6},{8,9},{9,8},{10,11... | collective-permute-start | bytes 2359304 | tf_op jit(solution)/shard_map/ppermute | solution.py:23
  82.3 7.8 %collective-permute-start.26 = (bf16[2,8,6144]{2,1,0:T(8,128)(2,1)S(1)}, bf16[2,8,6144]{2,1,0:T(8,128)(2,1)S(1)}, u32[]{:S(2)}, u32[]{:S(2)}) collective-permute-start(bf16[2,8,6144]{2,1,0:T(8,128)(2,1)S(1)} %get-tuple-element.90), channel_id=1, source_target_pairs={{0,2},{1,3},{2,0},{3,1},{4,6},{5,7},{6,4},{7,5},{8,10},{9,11},{10,... | collective-permute-start | bytes 589832 | tf_op jit(solution)/shard_map/ppermute | solution.py:23
  82.3 7.8 %collective-permute-start.27 = (bf16[2,8,6144]{2,1,0:T(8,128)(2,1)S(1)}, bf16[2,8,6144]{2,1,0:T(8,128)(2,1)S(1)}, u32[]{:S(2)}, u32[]{:S(2)}) collective-permute-start(bf16[2,8,6144]{2,1,0:T(8,128)(2,1)S(1)} %get-tuple-element.92), channel_id=1, source_target_pairs={{0,4},{1,5},{2,6},{3,7},{4,0},{5,1},{6,2},{7,3},{8,12},{9,13},{10,... | collective-permute-start | bytes 589832 | tf_op jit(solution)/shard_map/ppermute | solution.py:23
  83.4 15.5 %collective-permute-start.21 = (bf16[2,8,6144]{2,1,0:T(8,128)(2,1)S(1)}, bf16[2,8,6144]{2,1,0:T(8,128)(2,1)S(1)}, u32[]{:S(2)}, u32[]{:S(2)}) collective-permute-start(bf16[2,8,6144]{2,1,0:T(8,128)(2,1)S(1)} %get-tuple-element.80), channel_id=1, source_target_pairs={{0,2},{1,3},{2,0},{3,1},{4,6},{5,7},{6,4},{7,5},{8,10},{9,11},{10,... | collective-permute-start | bytes 589832 | tf_op jit(solution)/shard_map/ppermute | solution.py:23
  85.0 13.8 %collective-permute-start.22 = (bf16[2,8,6144]{2,1,0:T(8,128)(2,1)S(1)}, bf16[2,8,6144]{2,1,0:T(8,128)(2,1)S(1)}, u32[]{:S(2)}, u32[]{:S(2)}) collective-permute-start(bf16[2,8,6144]{2,1,0:T(8,128)(2,1)S(1)} %get-tuple-element.82), channel_id=1, source_target_pairs={{0,4},{1,5},{2,6},{3,7},{4,0},{5,1},{6,2},{7,3},{8,12},{9,13},{10,... | collective-permute-start | bytes 589832 | tf_op jit(solution)/shard_map/ppermute | solution.py:23
  90.2 5.4 %collective-permute-start.28 = (bf16[1,8,6144]{2,1,0:T(8,128)(2,1)S(1)}, bf16[1,8,6144]{2,1,0:T(8,128)(2,1)S(1)}, u32[]{:S(2)}, u32[]{:S(2)}) collective-permute-start(bf16[1,8,6144]{2,1,0:T(8,128)(2,1)S(1)} %get-tuple-element.94), channel_id=1, source_target_pairs={{0,4},{1,5},{2,6},{3,7},{4,0},{5,1},{6,2},{7,3},{8,12},{9,13},{10,... | collective-permute-start | bytes 294920 | tf_op jit(solution)/shard_map/ppermute | solution.py:23
  91.1 4.6 %collective-permute-start.29 = (bf16[1,8,6144]{2,1,0:T(8,128)(2,1)S(1)}, bf16[1,8,6144]{2,1,0:T(8,128)(2,1)S(1)}, u32[]{:S(2)}, u32[]{:S(2)}) collective-permute-start(bf16[1,8,6144]{2,1,0:T(8,128)(2,1)S(1)} %get-tuple-element.96), channel_id=1, source_target_pairs={{0,2},{1,3},{2,0},{3,1},{4,6},{5,7},{6,4},{7,5},{8,10},{9,11},{10,... | collective-permute-start | bytes 294920 | tf_op jit(solution)/shard_map/ppermute | solution.py:23
  95.8 8.4 %collective-permute-start.30 = (bf16[2,8,6144]{2,1,0:T(8,128)(2,1)S(1)}, bf16[2,8,6144]{2,1,0:T(8,128)(2,1)S(1)}, u32[]{:S(2)}, u32[]{:S(2)}) collective-permute-start(bf16[2,8,6144]{2,1,0:T(8,128)(2,1)S(1)} %shard_map.119), channel_id=1, source_target_pairs={{0,8},{8,0},{16,24},{24,16},{1,9},{9,1},{17,25},{25,17},{2,10},{10... | collective-permute-start | bytes 589832 | tf_op jit(solution)/shard_map/ppermute | solution.py:23
  99.0 4.7 %collective-permute-start.23 = (bf16[1,8,6144]{2,1,0:T(8,128)(2,1)S(1)}, bf16[1,8,6144]{2,1,0:T(8,128)(2,1)S(1)}, u32[]{:S(2)}, u32[]{:S(2)}) collective-permute-start(bf16[1,8,6144]{2,1,0:T(8,128)(2,1)S(1)} %get-tuple-element.84), channel_id=1, source_target_pairs={{0,4},{1,5},{2,6},{3,7},{4,0},{5,1},{6,2},{7,3},{8,12},{9,13},{10,... | collective-permute-start | bytes 294920 | tf_op jit(solution)/shard_map/ppermute | solution.py:23
  99.5 4.6 %collective-permute-start.24 = (bf16[1,8,6144]{2,1,0:T(8,128)(2,1)S(1)}, bf16[1,8,6144]{2,1,0:T(8,128)(2,1)S(1)}, u32[]{:S(2)}, u32[]{:S(2)}) collective-permute-start(bf16[1,8,6144]{2,1,0:T(8,128)(2,1)S(1)} %get-tuple-element.86), channel_id=1, source_target_pairs={{0,2},{1,3},{2,0},{3,1},{4,6},{5,7},{6,4},{7,5},{8,10},{9,11},{10,... | collective-permute-start | bytes 294920 | tf_op jit(solution)/shard_map/ppermute | solution.py:23
  104.2 6.4 %collective-permute-start.31 = (bf16[1,8,6144]{2,1,0:T(8,128)(2,1)S(1)}, bf16[1,8,6144]{2,1,0:T(8,128)(2,1)S(1)}, u32[]{:S(2)}, u32[]{:S(2)}) collective-permute-start(bf16[1,8,6144]{2,1,0:T(8,128)(2,1)S(1)} %get-tuple-element.98), channel_id=1, source_target_pairs={{0,16},{8,24},{16,0},{24,8},{1,17},{9,25},{17,1},{25,9},{2,18},{10... | collective-permute-start | bytes 294920 | tf_op jit(solution)/shard_map/ppermute | solution.py:23
  (5 other events, 38.7 us)

commit v2 on v1

--- a/solution.py
+++ b/solution.py
@@ -248,46 +248,51 @@
     return loaded, token
 
 
-def expert_kernel(C, E, per_block, width, columns, held, *refs):
+def expert_kernel(C, E, per_block, width, columns, held_counts, *refs):
     groups = C // 2
     packed, refs = refs[: 2 * groups], refs[2 * groups :]
-    gate_held, up_held, refs = refs[:held], refs[held : 2 * held], refs[2 * held :]
-    gain, gate, up, down = refs[:4]
+    gate_count, held = held_counts[0], sum(held_counts)
+    helds, refs = (refs[:gate_count], refs[gate_count:held]), refs[held:]
+    gain, *streamed, down = refs[:4]
     outs, hidden, refs = refs[4 : 2 * groups + 4], refs[2 * groups + 4], refs[2 * groups + 5 :]
-    gate_sum, up_sum, activated, piece, block, shift, spread, scale = refs[:8]
-    gate_slots, up_slots, down_slots, up_sems, down_sems = refs[8:]
+    *sums, activated, block, shift, spread, scale = refs[:7]
+    *slots, down_slots, gate_sems, up_sems, down_sems = refs[7:]
+    sems = (gate_sems, up_sems)
     ctx, exp = lax.axis_index("ctx"), lax.axis_index("exp")
     chips = E // 2
     token_rows = packed[0].shape[2]
     cols = packed[0].shape[3] - EXTRA
-    half_rows = chips * C * token_rows
+    group_rows = 2 * chips * token_rows
     features = hidden.shape[1]
     up_steps = C * per_block
-    first = held * per_block
+    firsts = [count * per_block for count in held_counts]
+    first = max(firsts)
     down_steps = features // columns
-    ahead, down_ahead = gate_slots.shape[0], down_slots.shape[0]
-
-    def up_copies(i, slot):
+    aheads, down_ahead = [ref.shape[0] for ref in slots], down_slots.shape[0]
+
+    def up_copy(n, i, slot):
         at = pl.ds(pl.multiple_of(i * width, 128), width)
-        return [
-            pltpu.make_async_copy(gate.at[0, :, at], gate_slots.at[slot], up_sems.at[0, slot]),
-            pltpu.make_async_copy(up.at[0, :, at], up_slots.at[slot], up_sems.at[1, slot]),
-        ]
+        return pltpu.make_async_copy(
+            streamed[n].at[0, :, at], slots[n].at[slot], sems[n].at[slot]
+        )
 
     def down_copy(i, slot):
         at = pl.ds(pl.multiple_of(i * columns, 128), columns)
         return pltpu.make_async_copy(down.at[0, :, at], down_slots.at[slot], down_sems.at[slot])
 
-    for i in range(ahead):
-        for copy in up_copies(first + i, i):
-            copy.start()
+    for n in range(2):
+        for i in range(aheads[n]):
+            up_copy(n, firsts[n] + i, i).start()
 
     def read(g, s, at):
         parts = [
-            packed[side * groups + g][pl.ds(s * chips, chips), :, :, at] for side in range(2)
+            packed[side * groups + g][s * chips + p, ctx ^ (t * groups + h), :, at]
+            for side in range(2)
+            for h in range(groups)
+            for t in range(2)
+            for p in range(chips)
         ]
-        parts = [part.astype(F32).reshape(half_rows, part.shape[-1]) for part in parts]
-        return jnp.concatenate(parts, axis=0)
+        return jnp.concatenate([part.astype(F32) for part in parts], axis=0)
 
     tails = [read(k % groups, k // groups, slice(cols, cols + EXTRA)) for k in range(C)]
     lane = lax.broadcasted_iota(jnp.int32, tails[0].shape, 1)
@@ -319,8 +324,7 @@
                 value = (read(g, s, at) + shift[k, 1]) * spread[...]
                 block[...] = (value * gain[:, pl.ds(place, width)]).astype(BF16)
                 own = packed[g][s * chips, ctx, :, at].astype(F32)
-                rows = pl.ds(pl.multiple_of(ctx * token_rows, token_rows), token_rows)
-                hidden[:, pl.ds(place, width)] = own + shift[k, 0, rows]
+                hidden[:, pl.ds(place, width)] = own + shift[k, 0, :token_rows]
 
     turned_dot = functools.partial(
         lax.dot_general,
@@ -328,38 +332,42 @@
         preferred_element_type=F32,
     )
     if held == 0:
-        gate_sum[...] = jnp.zeros_like(gate_sum)
-        up_sum[...] = jnp.zeros_like(up_sum)
+        for total in sums:
+            total[...] = jnp.zeros_like(total)
         for i in range(down_ahead):
             down_copy(i, i).start()
     for i in range(first):
         j, part = i // per_block, i % per_block
         normalise(j, part)
-        at = slice(part * width, (part + 1) * width)
-        gate_part = turned_dot(block[...], gate_held[j][:, at])
-        gate_sum[...] = gate_part if i == 0 else gate_sum[...] + gate_part
-        up_part = turned_dot(block[...], up_held[j][:, at])
-        up_sum[...] = up_part if i == 0 else up_sum[...] + up_part
+        for n, total in enumerate(sums):
+            slot = (i - firsts[n]) % aheads[n]
+            if i < firsts[n]:
+                weight = helds[n][j][:, part * width : (part + 1) * width]
+            else:
+                up_copy(n, i, slot).wait()
+                weight = slots[n][slot]
+            product = turned_dot(block[...], weight)
+            total[...] = product if i == 0 else total[...] + product
+            if i >= firsts[n] and i + aheads[n] < up_steps:
+                up_copy(n, i + aheads[n], slot).start()
         if i == first // 2:
             for d in range(down_ahead):
                 down_copy(d, d).start()
 
     @pl.loop(first, up_steps)
     def _(i):
-        slot = (i - first) % ahead
         normalise(i // per_block, i % per_block)
-        for copy in up_copies(i, slot):
-            copy.wait()
-        gate_sum[...] += turned_dot(block[...], gate_slots[slot])
-        up_sum[...] += turned_dot(block[...], up_slots[slot])
-
-        @pl.when(i + ahead < up_steps)
-        def _():
-            for copy in up_copies(i + ahead, slot):
-                copy.start()
-
-    value = gate_sum[...]
-    value = value / (1.0 + jnp.exp(-value)) * up_sum[...]
+        for n, total in enumerate(sums):
+            slot = (i - firsts[n]) % aheads[n]
+            up_copy(n, i, slot).wait()
+            total[...] += turned_dot(block[...], slots[n][slot])
+
+            @pl.when(i + aheads[n] < up_steps)
+            def _():
+                up_copy(n, i + aheads[n], slot).start()
+
+    value = sums[0][...]
+    value = value / (1.0 + jnp.exp(-value)) * sums[1][...]
     activated[...] = value.astype(BF16)
 
     @pl.loop(0, down_steps)
@@ -367,44 +375,39 @@
         slot = i % down_ahead
         down_copy(i, slot).wait()
         value = jnp.dot(activated[...], down_slots[slot], preferred_element_type=F32)
-        piece[...] = value * scale[...]
+        value = value * scale[...]
 
         @pl.when(i + down_ahead < down_steps)
         def _():
             down_copy(i + down_ahead, slot).start()
 
         place = pl.ds(pl.multiple_of(i * columns, 128), columns)
-        for g in range(groups):
-            for side in range(2):
-                for s in range(2):
-                    for p in range(chips):
-                        k = s * groups + g
-                        row = ((side * chips + p) * C + (ctx ^ k)) * token_rows
-                        at = pl.ds(pl.multiple_of(row, token_rows), token_rows)
-                        out = outs[side * groups + g]
-                        out[s * chips + p, :, place] = piece[at, :].astype(BF16)
+        for n, out in enumerate(outs):
+            part = value[n * group_rows : (n + 1) * group_rows]
+            out[:, :, place] = part.reshape(2 * chips, token_rows, columns).astype(BF16)
 
 
 def largest_part(size, most, unit):
     return max(c for c in range(unit, most + 1, unit) if size % c == 0)
 
 
-def run_experts(packed, gate_held, up_held, gain, weights, down_weight, C, E):
+def run_experts(packed, helds, gain, weights, down_weight, C, E):
     count = len(packed)
     pieces, _, token_rows, wide = packed[0].shape
     cols = wide - EXTRA
     features = cols * C
     units = weights[0].shape[1]
     total = C * E * token_rows
-    held = len(gate_held)
+    held_counts = [len(blocks) for blocks in helds]
+    held = sum(held_counts)
     width = largest_part(cols, 768 if held else 384, 128)
     columns = largest_part(features, 768 if held else 384, 128)
     per_block = cols // width
-    ahead = 3 if held else 2
+    ahead, up_ahead = 2, 3 if held else 2
     down_ahead = 3 if held else 2
-    operands = [*packed, *gate_held, *up_held, gain]
+    operands = [*packed, *helds[0], *helds[1], gain]
     *outs, hidden = pl.pallas_call(
-        functools.partial(expert_kernel, C, E, per_block, width, columns, held),
+        functools.partial(expert_kernel, C, E, per_block, width, columns, held_counts),
         out_shape=[shape((pieces, token_rows, features), BF16) for _ in packed]
         + [shape((token_rows, features), F32)],
         in_specs=[WHOLE] * len(operands) + [IN_HBM] * 3,
@@ -413,18 +416,18 @@
             pltpu.VMEM((total, units), F32),
             pltpu.VMEM((total, units), F32),
             pltpu.VMEM((total, units), BF16),
-            pltpu.VMEM((total, columns), F32),
             pltpu.VMEM((total, width), BF16),
             pltpu.VMEM((C, 2, total, 1), F32),
             pltpu.VMEM((total, 1), F32),
             pltpu.VMEM((total, 1), F32),
             pltpu.VMEM((ahead, units, width), BF16),
-            pltpu.VMEM((ahead, units, width), BF16),
+            pltpu.VMEM((up_ahead, units, width), BF16),
             pltpu.VMEM((down_ahead, units, columns), BF16),
-            pltpu.SemaphoreType.DMA((2, ahead)),
+            pltpu.SemaphoreType.DMA((ahead,)),
+            pltpu.SemaphoreType.DMA((up_ahead,)),
             pltpu.SemaphoreType.DMA((down_ahead,)),
         ],
-        compiler_params=pltpu.CompilerParams(vmem_limit_bytes=(35 if held else 58) * MIB),
+        compiler_params=pltpu.CompilerParams(vmem_limit_bytes=(33 if held else 58) * MIB),
         cost_estimate=pl.CostEstimate(
             flops=6 * total * features * units,
             bytes_accessed=6 * features * units + 4 * total * features,
@@ -567,10 +570,10 @@
     hold = C * E * token_rows <= 256 and C == 4 and len(chip_bits) == 2
     loaded = []
 
-    def load(which, after):
+    def load(which, j, after, limit):
         if not hold:
             return []
-        blocks, token = load_blocks(weights, [(which, 0)], cols, after, 44)
+        blocks, token = load_blocks(weights, [(which, j)], cols, after, limit)
         loaded.extend(blocks)
         return [token]
 
@@ -583,10 +586,10 @@
     afters = [[]] * len(chip_bits)
     group, sends = spread_over_plane(near, [(0, None), (1, None)], orders, chips, afters)
     packed = [group]
-    token = load(0, sends[0])
+    token = load(0, 0, sends[0], 44)
     for value in pairs[1:]:
         afters = [sends] + [token] * (len(chip_bits) - 1)
-        last = (lambda sent: load(1, sent[0])) if hold else (lambda sent: [])
+        last = lambda sent: load(1, 0, sent[0], 44) + load(0, 1, packed[0], 40)
         group, sends = spread_over_plane(
             [value], [(0, 0), (0, 1)], orders, chips, afters, last
         )
@@ -594,7 +597,7 @@
     packed += [swap(group, "exp", 1) for group in packed]
 
     outs, hidden = run_experts(
-        packed, loaded[0::2], loaded[1::2], gain, weights, down_weight, C, E
+        packed, (loaded[0::2], loaded[1::2]), gain, weights, down_weight, C, E
     )
 
     count = C // 2

time: 112 us -> 114 us (1.018)
  Pallas kernels: 29.6 us -> 32.8 us
  starting transfers between devices: 33.8 us -> 32.3 us
    pallas_call x2 -> x3, Pallas kernels: 4.35 us -> 6.54 us  [load_blocks(): pl.pallas_call(functools.partial(load_kernel, blocks), out_shape=[shape((...]
    ppermute x32, starting transfers between devices: 33.8 us -> 32.3 us  [swap(): lax.ppermute(value, axis, [(i, i ^ mask) for i in range(lax.axis_size(axi...]
  transfers between devices with their start and end apart: 32 -> 32, of which waited for: 20 -> 21; matrix products, arithmetic and copies ran while one was open for 0% -> 0% of each run, Pallas kernels for 5% -> 7%
where the time goes in v2:
time: 114 us; the launch traced here: 113 us
  waiting for transfers between devices  44.4 us (39%)
  Pallas kernels  32.8 us (29%)
  starting transfers between devices  32.3 us (28%)
  local copies, waits for them, and re-layouts  2.9 us (3%)
    ppermute x32, waiting for transfers between devices, swap(): lax.ppermute(value, axis, [(i, i ^ mask) for i in range(lax.axis_size(axi...  44.4 us
    ppermute x32, starting transfers between devices, swap(): lax.ppermute(value, axis, [(i, i ^ mask) for i in range(lax.axis_size(axi...  32.3 us
    pallas_call x1, Pallas kernels, run_experts(): pl.pallas_call(functools.partial(expert_kernel, C, E, per_block, width, c...  21.7 us
    pallas_call x3, Pallas kernels, load_blocks(): pl.pallas_call(functools.partial(load_kernel, blocks), out_shape=[shape((...  6.54 us
    pallas_call x18, Pallas kernels, call(): pl.pallas_call(kernel, out_shape=out_shape, in_specs=in_specs, out_specs=...  4.49 us
    unnamed x10, local copies, waits for them, and re-layouts  2.9 us
  transfers between devices with their start and end apart: 32, of which 21 were waited for; matrix products, arithmetic and copies ran while one was open for 0% of the time, Pallas kernels for 7%

profile of v2, /device:TPU:0, one launch (start us, length us, event | category | flops | bytes accessed | tf_op | source)
XLA Modules:
  0.0 113.4 jit_solution(10557948377318021925)
XLA Ops:
  0.0 1.8 %shard_map.100 = (bf16[11,8,512]{2,1,0:T(8,128)(2,1)}, bf16[11,8,512]{2,1,0:T(8,128)(2,1)}, bf16[11,8,512]{2,1,0:T(8,128)(2,1)}, bf16[11,8,512]{2,1,0:T(8,128)(2,1)}) custom-call(bf16[64,384]{1,0:T(8,128)(2,1)} %queries_in.1, bf16[2,64,64]{2,1,0:T(8,128)(2,1)} %own_in.1, bf16[8,6144]{1,0:T(8,128)(2,1)} %residual_in.1), custom_call_target="tpu_custom_call" | custom-call | tf_op jit(solution)/shard_map/pallas_call | solution.py:27
  1.8 3.1 %collective-permute-start = (bf16[11,8,512]{2,1,0:T(8,128)(2,1)}, bf16[11,8,512]{2,1,0:T(8,128)(2,1)S(1)}, u32[]{:S(2)}, u32[]{:S(2)}) collective-permute-start(bf16[11,8,512]{2,1,0:T(8,128)(2,1)} %get-tuple-element.55), channel_id=1, source_target_pairs={{0,8},{8,0},{16,24},{24,16},{1,9},{9,1},{17,25},{25,17},{2,10},{10... | collective-permute-start | bytes 270344 | tf_op jit(solution)/shard_map/ppermute | solution.py:23
  4.9 2.6 %collective-permute-start.1 = (bf16[11,8,512]{2,1,0:T(8,128)(2,1)}, bf16[11,8,512]{2,1,0:T(8,128)(2,1)S(1)}, u32[]{:S(2)}, u32[]{:S(2)}) collective-permute-start(bf16[11,8,512]{2,1,0:T(8,128)(2,1)} %get-tuple-element.56), channel_id=1, source_target_pairs={{0,16},{8,24},{16,0},{24,8},{1,17},{9,25},{17,1},{25,9},{2,18},{10... | collective-permute-start | bytes 270344 | tf_op jit(solution)/shard_map/ppermute | solution.py:23
  10.5 4.4 %collective-permute-done.1.refs_2_.refs_6_ = bf16[11,8,512]{2,1,0:T(8,128)(2,1)S(1)} collective-permute-done((bf16[11,8,512]{2,1,0:T(8,128)(2,1)}, bf16[11,8,512]{2,1,0:T(8,128)(2,1)S(1)}, u32[]{:S(2)}, u32[]{:S(2)}) %collective-permute-start.1) | collective-permute-done | bytes 90144 | tf_op jit(solution)/shard_map/ppermute | solution.py:23
  16.3 1.4 %shard_map.103 = (bf16[4,4,8,1536]{3,2,1,0:T(8,128)(2,1)S(1)}, f32[4,4,8,1536]{3,2,1,0:T(8,128)S(1)}) custom-call(bf16[11,8,512]{2,1,0:T(8,128)(2,1)S(1)} %copy-done.1, bf16[11,8,512]{2,1,0:T(8,128)(2,1)S(1)} %collective-permute-done.refs_1_.refs_5_, bf16[11,8,512]{2,1,0:T(8,128)(2,1)S(1)} %collective-permute-done.1.refs_2_.refs_6_, ...), custom_call_target="tpu_custom_call" | custom-call | tf_op jit(solution)/shard_map/pallas_call | solution.py:27
  18.0 1.5 %collective-permute-done.4.received = bf16[4,4,8,1536]{3,2,1,0:T(8,128)(2,1)S(1)} collective-permute-done((bf16[4,4,8,1536]{3,2,1,0:T(8,128)(2,1)S(1)}, bf16[4,4,8,1536]{3,2,1,0:T(8,128)(2,1)S(1)}, u32[]{:S(2)}, u32[]{:S(2)}) %collective-permute-start.4) | collective-permute-done | bytes 393248 | tf_op jit(solution)/shard_map/ppermute | solution.py:23
  19.5 1.6 %collective-permute-start.5 = (bf16[4,8,1536]{2,1,0:T(8,128)(2,1)S(1)}, bf16[4,8,1536]{2,1,0:T(8,128)(2,1)S(1)}, u32[]{:S(2)}, u32[]{:S(2)}) collective-permute-start(bf16[4,8,1536]{2,1,0:T(8,128)(2,1)S(1)} %get-tuple-element.64), channel_id=1, source_target_pairs={{0,2},{1,3},{2,0},{3,1},{4,6},{5,7},{6,4},{7,5},{8,10},{9,11},{10,... | collective-permute-start | bytes 294920 | tf_op jit(solution)/shard_map/ppermute | solution.py:23
  21.1 1.5 %collective-permute-start.6 = (bf16[4,8,1536]{2,1,0:T(8,128)(2,1)S(1)}, bf16[4,8,1536]{2,1,0:T(8,128)(2,1)S(1)}, u32[]{:S(2)}, u32[]{:S(2)}) collective-permute-start(bf16[4,8,1536]{2,1,0:T(8,128)(2,1)S(1)} %get-tuple-element.65), channel_id=1, source_target_pairs={{0,4},{1,5},{2,6},{3,7},{4,0},{5,1},{6,2},{7,3},{8,12},{9,13},{10,... | collective-permute-start | bytes 294920 | tf_op jit(solution)/shard_map/ppermute | solution.py:23
  23.2 1.3 %collective-permute-done.5.refs_1_ = bf16[4,8,1536]{2,1,0:T(8,128)(2,1)S(1)} collective-permute-done((bf16[4,8,1536]{2,1,0:T(8,128)(2,1)S(1)}, bf16[4,8,1536]{2,1,0:T(8,128)(2,1)S(1)}, u32[]{:S(2)}, u32[]{:S(2)}) %collective-permute-start.5) | collective-permute-done | bytes 98336 | tf_op jit(solution)/shard_map/ppermute | solution.py:23
  24.5 2.4 %collective-permute-done.6.refs_2_ = bf16[4,8,1536]{2,1,0:T(8,128)(2,1)S(1)} collective-permute-done((bf16[4,8,1536]{2,1,0:T(8,128)(2,1)S(1)}, bf16[4,8,1536]{2,1,0:T(8,128)(2,1)S(1)}, u32[]{:S(2)}, u32[]{:S(2)}) %collective-permute-start.6) | collective-permute-done | bytes 98336 | tf_op jit(solution)/shard_map/ppermute | solution.py:23
  26.9 1.3 %collective-permute-done.7.refs_3_ = bf16[4,8,1536]{2,1,0:T(8,128)(2,1)S(1)} collective-permute-done((bf16[4,8,1536]{2,1,0:T(8,128)(2,1)S(1)}, bf16[4,8,1536]{2,1,0:T(8,128)(2,1)S(1)}, u32[]{:S(2)}, u32[]{:S(2)}) %collective-permute-start.7) | collective-permute-done | bytes 98336 | tf_op jit(solution)/shard_map/ppermute | solution.py:23
  28.4 2.6 %collective-permute-start.8 = (bf16[4,8,1664]{2,1,0:T(8,128)(2,1)S(1)}, bf16[4,8,1664]{2,1,0:T(8,128)(2,1)S(1)}, u32[]{:S(2)}, u32[]{:S(2)}) collective-permute-start(bf16[4,8,1664]{2,1,0:T(8,128)(2,1)S(1)} %shard_map.105.refs_0_), channel_id=1, source_target_pairs={{0,16},{8,24},{16,0},{24,8},{1,17},{9,25},{17,1},{25,9},{2,18},{10... | collective-permute-start | bytes 319496 | tf_op jit(solution)/shard_map/ppermute | solution.py:23
  31.0 4.2 %collective-permute-done.8.refs_1_ = bf16[4,8,1664]{2,1,0:T(8,128)(2,1)S(1)} collective-permute-done((bf16[4,8,1664]{2,1,0:T(8,128)(2,1)S(1)}, bf16[4,8,1664]{2,1,0:T(8,128)(2,1)S(1)}, u32[]{:S(2)}, u32[]{:S(2)}) %collective-permute-start.8) | collective-permute-done | bytes 106528 | tf_op jit(solution)/shard_map/ppermute | solution.py:23
  37.5 3.5 %collective-permute-done.9.refs_2_ = bf16[4,8,1664]{2,1,0:T(8,128)(2,1)S(1)} collective-permute-done((bf16[4,8,1664]{2,1,0:T(8,128)(2,1)S(1)}, bf16[4,8,1664]{2,1,0:T(8,128)(2,1)S(1)}, u32[]{:S(2)}, u32[]{:S(2)}) %collective-permute-start.9) | collective-permute-done | bytes 106528 | tf_op jit(solution)/shard_map/ppermute | solution.py:23
  41.0 1.6 %collective-permute-done.10.refs_3_ = bf16[4,8,1664]{2,1,0:T(8,128)(2,1)S(1)} collective-permute-done((bf16[4,8,1664]{2,1,0:T(8,128)(2,1)S(1)}, bf16[4,8,1664]{2,1,0:T(8,128)(2,1)S(1)}, u32[]{:S(2)}, u32[]{:S(2)}) %collective-permute-start.10) | collective-permute-done | bytes 106528 | tf_op jit(solution)/shard_map/ppermute | solution.py:23
  44.8 1.9 %collective-permute-start.11 = (bf16[2,4,8,1664]{3,2,1,0:T(8,128)(2,1)S(1)}, bf16[2,4,8,1664]{3,2,1,0:T(8,128)(2,1)S(1)}, u32[]{:S(2)}, u32[]{:S(2)}) collective-permute-start(bf16[2,4,8,1664]{3,2,1,0:T(8,128)(2,1)S(1)} %get-tuple-element.68.refs_1_.refs_2_), channel_id=1, source_target_pairs={{0,2},{1,3},{2,0},{3,1},{4,6},{5,7},{6,4},{7,5},{8,10},{9,11},{10,... | collective-permute-start | bytes 638984 | tf_op jit(solution)/shard_map/ppermute | solution.py:23
  46.7 2.2 %shard_map.110 = (bf16[1344,1536]{1,0:T(8,128)(2,1)S(1)}, f32[8,128]{1,0:T(8,128)S(1)}) custom-call(bf16[1,1344,6144]{2,1,0:T(8,128)(2,1)} %bitcast.10, bf16[1,1344,6144]{2,1,0:T(8,128)(2,1)} %bitcast.14, bf16[2,4,8,1664]{3,2,1,0:T(8,128)(2,1)S(1)} %get-tuple-element.68.refs_1_.refs_2_), custom_call_target="tpu_custom_call" | custom-call | bytes 8257536 | tf_op jit(solution)/shard_map/pallas_call | solution.py:237
  49.0 1.7 %collective-permute-start.17 = (bf16[2,4,8,1664]{3,2,1,0:T(8,128)(2,1)S(1)}, bf16[2,4,8,1664]{3,2,1,0:T(8,128)(2,1)S(1)}, u32[]{:S(2)}, u32[]{:S(2)}) collective-permute-start(bf16[2,4,8,1664]{3,2,1,0:T(8,128)(2,1)S(1)} %get-tuple-element.74), channel_id=1, source_target_pairs={{0,4},{1,5},{2,6},{3,7},{4,0},{5,1},{6,2},{7,3},{8,12},{9,13},{10,... | collective-permute-start | bytes 638984 | tf_op jit(solution)/shard_map/ppermute | solution.py:23
  51.9 2.2 %shard_map.113 = (bf16[1344,1536]{1,0:T(8,128)(2,1)S(1)}, f32[8,128]{1,0:T(8,128)S(1)}) custom-call(bf16[1,1344,6144]{2,1,0:T(8,128)(2,1)} %bitcast.11, bf16[1,1344,6144]{2,1,0:T(8,128)(2,1)} %bitcast.15, bf16[8,4,8,1664]{3,2,1,0:T(8,128)(2,1)S(1)} %shard_map.107.refs_2_.refs_0_), custom_call_target="tpu_custom_call" | custom-call | bytes 8257536 | tf_op jit(solution)/shard_map/pallas_call | solution.py:237
  54.1 2.2 %shard_map.112 = (bf16[1344,1536]{1,0:T(8,128)(2,1)S(1)}, f32[8,128]{1,0:T(8,128)S(1)}) custom-call(bf16[1,1344,6144]{2,1,0:T(8,128)(2,1)} %bitcast.12, bf16[1,1344,6144]{2,1,0:T(8,128)(2,1)} %bitcast.16, bf16[2,4,8,1664]{3,2,1,0:T(8,128)(2,1)S(1)} %get-tuple-element.73.refs_2_), custom_call_target="tpu_custom_call" | custom-call | bytes 8257536 | tf_op jit(solution)/shard_map/pallas_call | solution.py:237
  56.9 2.1 %collective-permute-done.19.refs_3_ = bf16[8,4,8,1664]{3,2,1,0:T(8,128)(2,1)S(1)} collective-permute-done((bf16[8,4,8,1664]{3,2,1,0:T(8,128)(2,1)S(1)}, bf16[8,4,8,1664]{3,2,1,0:T(8,128)(2,1)S(1)}, u32[]{:S(2)}, u32[]{:S(2)}) %collective-permute-start.19) | collective-permute-done | bytes 852000 | tf_op jit(solution)/shard_map/ppermute | solution.py:23
  59.0 21.7 %shard_map.115 = (bf16[8,8,6144]{2,1,0:T(8,128)(2,1)S(1)}, bf16[8,8,6144]{2,1,0:T(8,128)(2,1)S(1)}, bf16[8,8,6144]{2,1,0:T(8,128)(2,1)S(1)}, bf16[8,8,6144]{2,1,0:T(8,128)(2,1)S(1)}, f32[8,6144]{1,0:T(8,128)S(1)}) custom-call(bf16[8,4,8,1664]{3,2,1,0:T(8,128)(2,1)S(1)} %shard_map.107.refs_2_.refs_0_, bf16[8,4,8,1664]{3,2,1,0:T(8,128)(2,1)S(1)} %shard_map.114.refs_1_, ...), custom_call_target="tpu_custom_call" | custom-call | flops 12683575296 | bytes 55836672 | tf_op jit(solution)/shard_map/pallas_call | solution.py:409
  81.3 1.8 %collective-permute-done.25.refs_1_ = bf16[8,8,6144]{2,1,0:T(8,128)(2,1)S(1)} collective-permute-done((bf16[8,8,6144]{2,1,0:T(8,128)(2,1)S(1)}, bf16[8,8,6144]{2,1,0:T(8,128)(2,1)S(1)}, u32[]{:S(2)}, u32[]{:S(2)}) %collective-permute-start.25) | collective-permute-done | bytes 786464 | tf_op jit(solution)/shard_map/ppermute | solution.py:23
  83.3 1.3 %collective-permute-start.26 = (bf16[2,8,6144]{2,1,0:T(8,128)(2,1)S(1)}, bf16[2,8,6144]{2,1,0:T(8,128)(2,1)S(1)}, u32[]{:S(2)}, u32[]{:S(2)}) collective-permute-start(bf16[2,8,6144]{2,1,0:T(8,128)(2,1)S(1)} %get-tuple-element.94), channel_id=1, source_target_pairs={{0,2},{1,3},{2,0},{3,1},{4,6},{5,7},{6,4},{7,5},{8,10},{9,11},{10,... | collective-permute-start | bytes 589832 | tf_op jit(solution)/shard_map/ppermute | solution.py:23
  87.6 3.4 %collective-permute-done.26.refs_1_ = bf16[2,8,6144]{2,1,0:T(8,128)(2,1)S(1)} collective-permute-done((bf16[2,8,6144]{2,1,0:T(8,128)(2,1)S(1)}, bf16[2,8,6144]{2,1,0:T(8,128)(2,1)S(1)}, u32[]{:S(2)}, u32[]{:S(2)}) %collective-permute-start.26) | collective-permute-done | bytes 196640 | tf_op jit(solution)/shard_map/ppermute | solution.py:23
  91.1 1.3 %collective-permute-done.27.refs_3_ = bf16[2,8,6144]{2,1,0:T(8,128)(2,1)S(1)} collective-permute-done((bf16[2,8,6144]{2,1,0:T(8,128)(2,1)S(1)}, bf16[2,8,6144]{2,1,0:T(8,128)(2,1)S(1)}, u32[]{:S(2)}, u32[]{:S(2)}) %collective-permute-start.27) | collective-permute-done | bytes 196640 | tf_op jit(solution)/shard_map/ppermute | solution.py:23
  94.5 3.3 %collective-permute-done.28.refs_1_ = bf16[1,8,6144]{2,1,0:T(8,128)(2,1)S(1)} collective-permute-done((bf16[1,8,6144]{2,1,0:T(8,128)(2,1)S(1)}, bf16[1,8,6144]{2,1,0:T(8,128)(2,1)S(1)}, u32[]{:S(2)}, u32[]{:S(2)}) %collective-permute-start.28) | collective-permute-done | bytes 98336 | tf_op jit(solution)/shard_map/ppermute | solution.py:23
  98.2 2.1 %collective-permute-start.30 = (bf16[2,8,6144]{2,1,0:T(8,128)(2,1)S(1)}, bf16[2,8,6144]{2,1,0:T(8,128)(2,1)S(1)}, u32[]{:S(2)}, u32[]{:S(2)}) collective-permute-start(bf16[2,8,6144]{2,1,0:T(8,128)(2,1)S(1)} %shard_map.120), channel_id=1, source_target_pairs={{0,8},{8,0},{16,24},{24,16},{1,9},{9,1},{17,25},{25,17},{2,10},{10... | collective-permute-start | bytes 589832 | tf_op jit(solution)/shard_map/ppermute | solution.py:23
  100.4 1.4 %collective-permute-start.23 = (bf16[1,8,6144]{2,1,0:T(8,128)(2,1)S(1)}, bf16[1,8,6144]{2,1,0:T(8,128)(2,1)S(1)}, u32[]{:S(2)}, u32[]{:S(2)}) collective-permute-start(bf16[1,8,6144]{2,1,0:T(8,128)(2,1)S(1)} %get-tuple-element.88), channel_id=1, source_target_pairs={{0,4},{1,5},{2,6},{3,7},{4,0},{5,1},{6,2},{7,3},{8,12},{9,13},{10,... | collective-permute-start | bytes 294920 | tf_op jit(solution)/shard_map/ppermute | solution.py:23
  102.1 3.0 %collective-permute-done.23.refs_1_ = bf16[1,8,6144]{2,1,0:T(8,128)(2,1)S(1)} collective-permute-done((bf16[1,8,6144]{2,1,0:T(8,128)(2,1)S(1)}, bf16[1,8,6144]{2,1,0:T(8,128)(2,1)S(1)}, u32[]{:S(2)}, u32[]{:S(2)}) %collective-permute-start.23) | collective-permute-done | bytes 98336 | tf_op jit(solution)/shard_map/ppermute | solution.py:23
  105.1 1.4 %collective-permute-done.24.refs_3_ = bf16[1,8,6144]{2,1,0:T(8,128)(2,1)S(1)} collective-permute-done((bf16[1,8,6144]{2,1,0:T(8,128)(2,1)S(1)}, bf16[1,8,6144]{2,1,0:T(8,128)(2,1)S(1)}, u32[]{:S(2)}, u32[]{:S(2)}) %collective-permute-start.24) | collective-permute-done | bytes 98336 | tf_op jit(solution)/shard_map/ppermute | solution.py:23
  107.6 5.1 %collective-permute-done.31 = bf16[1,8,6144]{2,1,0:T(8,128)(2,1)S(1)} collective-permute-done((bf16[1,8,6144]{2,1,0:T(8,128)(2,1)S(1)}, bf16[1,8,6144]{2,1,0:T(8,128)(2,1)S(1)}, u32[]{:S(2)}, u32[]{:S(2)}) %collective-permute-start.31) | collective-permute-done | bytes 98336 | tf_op jit(solution)/shard_map/ppermute | solution.py:23
  (68 shorter events, 20.5 us)
Async XLA Ops:
  1.8 8.7 %collective-permute-start = (bf16[11,8,512]{2,1,0:T(8,128)(2,1)}, bf16[11,8,512]{2,1,0:T(8,128)(2,1)S(1)}, u32[]{:S(2)}, u32[]{:S(2)}) collective-permute-start(bf16[11,8,512]{2,1,0:T(8,128)(2,1)} %get-tuple-element.55), channel_id=1, source_target_pairs={{0,8},{8,0},{16,24},{24,16},{1,9},{9,1},{17,25},{25,17},{2,10},{10... | collective-permute-start | bytes 270344 | tf_op jit(solution)/shard_map/ppermute | solution.py:23
  4.9 10.0 %collective-permute-start.1 = (bf16[11,8,512]{2,1,0:T(8,128)(2,1)}, bf16[11,8,512]{2,1,0:T(8,128)(2,1)S(1)}, u32[]{:S(2)}, u32[]{:S(2)}) collective-permute-start(bf16[11,8,512]{2,1,0:T(8,128)(2,1)} %get-tuple-element.56), channel_id=1, source_target_pairs={{0,16},{8,24},{16,0},{24,8},{1,17},{9,25},{17,1},{25,9},{2,18},{10... | collective-permute-start | bytes 270344 | tf_op jit(solution)/shard_map/ppermute | solution.py:23
  7.5 7.4 %collective-permute-start.2 = (bf16[11,8,512]{2,1,0:T(8,128)(2,1)}, bf16[11,8,512]{2,1,0:T(8,128)(2,1)S(1)}, u32[]{:S(2)}, u32[]{:S(2)}) collective-permute-start(bf16[11,8,512]{2,1,0:T(8,128)(2,1)} %get-tuple-element.57), channel_id=1, source_target_pairs={{0,24},{8,16},{16,8},{24,0},{1,25},{9,17},{17,9},{25,1},{2,26},{10... | collective-permute-start | bytes 270344 | tf_op jit(solution)/shard_map/ppermute | solution.py:23
  14.9 1.3 %collective-permute-start.3 = (bf16[4,8,8,128]{3,2,1,0:T(8,128)(2,1)S(1)}, bf16[4,8,8,128]{3,2,1,0:T(8,128)(2,1)S(1)}, u32[]{:S(2)}, u32[]{:S(2)}) collective-permute-start(bf16[4,8,8,128]{3,2,1,0:T(8,128)(2,1)S(1)} %get-tuple-element.60), channel_id=1, source_target_pairs={{0,1},{1,0},{2,3},{3,2},{4,5},{5,4},{6,7},{7,6},{8,9},{9,8},{10,11... | collective-permute-start | bytes 196616 | tf_op jit(solution)/shard_map/ppermute | solution.py:23
  17.7 1.8 %collective-permute-start.4 = (bf16[4,4,8,1536]{3,2,1,0:T(8,128)(2,1)S(1)}, bf16[4,4,8,1536]{3,2,1,0:T(8,128)(2,1)S(1)}, u32[]{:S(2)}, u32[]{:S(2)}) collective-permute-start(bf16[4,4,8,1536]{3,2,1,0:T(8,128)(2,1)S(1)} %get-tuple-element.62), channel_id=1, source_target_pairs={{0,1},{1,0},{2,3},{3,2},{4,5},{5,4},{6,7},{7,6},{8,9},{9,8},{10,11... | collective-permute-start | bytes 1179656 | tf_op jit(solution)/shard_map/ppermute | solution.py:23
  19.5 4.9 %collective-permute-start.5 = (bf16[4,8,1536]{2,1,0:T(8,128)(2,1)S(1)}, bf16[4,8,1536]{2,1,0:T(8,128)(2,1)S(1)}, u32[]{:S(2)}, u32[]{:S(2)}) collective-permute-start(bf16[4,8,1536]{2,1,0:T(8,128)(2,1)S(1)} %get-tuple-element.64), channel_id=1, source_target_pairs={{0,2},{1,3},{2,0},{3,1},{4,6},{5,7},{6,4},{7,5},{8,10},{9,11},{10,... | collective-permute-start | bytes 294920 | tf_op jit(solution)/shard_map/ppermute | solution.py:23
  21.1 5.8 %collective-permute-start.6 = (bf16[4,8,1536]{2,1,0:T(8,128)(2,1)S(1)}, bf16[4,8,1536]{2,1,0:T(8,128)(2,1)S(1)}, u32[]{:S(2)}, u32[]{:S(2)}) collective-permute-start(bf16[4,8,1536]{2,1,0:T(8,128)(2,1)S(1)} %get-tuple-element.65), channel_id=1, source_target_pairs={{0,4},{1,5},{2,6},{3,7},{4,0},{5,1},{6,2},{7,3},{8,12},{9,13},{10,... | collective-permute-start | bytes 294920 | tf_op jit(solution)/shard_map/ppermute | solution.py:23
  22.6 5.5 %collective-permute-start.7 = (bf16[4,8,1536]{2,1,0:T(8,128)(2,1)S(1)}, bf16[4,8,1536]{2,1,0:T(8,128)(2,1)S(1)}, u32[]{:S(2)}, u32[]{:S(2)}) collective-permute-start(bf16[4,8,1536]{2,1,0:T(8,128)(2,1)S(1)} %get-tuple-element.66), channel_id=1, source_target_pairs={{0,6},{1,7},{2,4},{3,5},{4,2},{5,3},{6,0},{7,1},{8,14},{9,15},{10,... | collective-permute-start | bytes 294920 | tf_op jit(solution)/shard_map/ppermute | solution.py:23
  28.4 6.8 %collective-permute-start.8 = (bf16[4,8,1664]{2,1,0:T(8,128)(2,1)S(1)}, bf16[4,8,1664]{2,1,0:T(8,128)(2,1)S(1)}, u32[]{:S(2)}, u32[]{:S(2)}) collective-permute-start(bf16[4,8,1664]{2,1,0:T(8,128)(2,1)S(1)} %shard_map.105.refs_0_), channel_id=1, source_target_pairs={{0,16},{8,24},{16,0},{24,8},{1,17},{9,25},{17,1},{25,9},{2,18},{10... | collective-permute-start | bytes 319496 | tf_op jit(solution)/shard_map/ppermute | solution.py:23
  35.2 7.4 %collective-permute-start.13 = (bf16[2,4,8,1664]{3,2,1,0:T(8,128)(2,1)S(1)}, bf16[2,4,8,1664]{3,2,1,0:T(8,128)(2,1)S(1)}, u32[]{:S(2)}, u32[]{:S(2)}) collective-permute-start(bf16[2,4,8,1664]{3,2,1,0:T(8,128)(2,1)S(1)} %shard_map.108), channel_id=1, source_target_pairs={{0,8},{8,0},{16,24},{24,16},{1,9},{9,1},{17,25},{25,17},{2,10},{10... | collective-permute-start | bytes 638984 | tf_op jit(solution)/shard_map/ppermute | solution.py:23
  35.8 5.2 %collective-permute-start.9 = (bf16[4,8,1664]{2,1,0:T(8,128)(2,1)S(1)}, bf16[4,8,1664]{2,1,0:T(8,128)(2,1)S(1)}, u32[]{:S(2)}, u32[]{:S(2)}) collective-permute-start(bf16[4,8,1664]{2,1,0:T(8,128)(2,1)S(1)} %shard_map.105.refs_0_), channel_id=1, source_target_pairs={{0,4},{1,5},{2,6},{3,7},{4,0},{5,1},{6,2},{7,3},{8,12},{9,13},{10,... | collective-permute-start | bytes 319496 | tf_op jit(solution)/shard_map/ppermute | solution.py:23
  37.0 5.6 %collective-permute-start.10 = (bf16[4,8,1664]{2,1,0:T(8,128)(2,1)S(1)}, bf16[4,8,1664]{2,1,0:T(8,128)(2,1)S(1)}, u32[]{:S(2)}, u32[]{:S(2)}) collective-permute-start(bf16[4,8,1664]{2,1,0:T(8,128)(2,1)S(1)} %collective-permute-done.8.refs_1_), channel_id=1, source_target_pairs={{0,2},{1,3},{2,0},{3,1},{4,6},{5,7},{6,4},{7,5},{8,10},{9,11},{10,... | collective-permute-start | bytes 319496 | tf_op jit(solution)/shard_map/ppermute | solution.py:23
  42.6 6.3 %collective-permute-start.14 = (bf16[4,8,1664]{2,1,0:T(8,128)(2,1)S(1)}, bf16[4,8,1664]{2,1,0:T(8,128)(2,1)S(1)}, u32[]{:S(2)}, u32[]{:S(2)}) collective-permute-start(bf16[4,8,1664]{2,1,0:T(8,128)(2,1)S(1)} %get-tuple-element.70), channel_id=1, source_target_pairs={{0,4},{1,5},{2,6},{3,7},{4,0},{5,1},{6,2},{7,3},{8,12},{9,13},{10,... | collective-permute-start | bytes 319496 | tf_op jit(solution)/shard_map/ppermute | solution.py:23
  43.1 5.9 %collective-permute-start.15 = (bf16[4,8,1664]{2,1,0:T(8,128)(2,1)S(1)}, bf16[4,8,1664]{2,1,0:T(8,128)(2,1)S(1)}, u32[]{:S(2)}, u32[]{:S(2)}) collective-permute-start(bf16[4,8,1664]{2,1,0:T(8,128)(2,1)S(1)} %get-tuple-element.71), channel_id=1, source_target_pairs={{0,2},{1,3},{2,0},{3,1},{4,6},{5,7},{6,4},{7,5},{8,10},{9,11},{10,... | collective-permute-start | bytes 319496 | tf_op jit(solution)/shard_map/ppermute | solution.py:23
  43.8 7.5 %collective-permute-start.12 = (bf16[2,4,8,1664]{3,2,1,0:T(8,128)(2,1)S(1)}, bf16[2,4,8,1664]{3,2,1,0:T(8,128)(2,1)S(1)}, u32[]{:S(2)}, u32[]{:S(2)}) collective-permute-start(bf16[2,4,8,1664]{3,2,1,0:T(8,128)(2,1)S(1)} %get-tuple-element.69.refs_2_), channel_id=1, source_target_pairs={{0,4},{1,5},{2,6},{3,7},{4,0},{5,1},{6,2},{7,3},{8,12},{9,13},{10,... | collective-permute-start | bytes 638984 | tf_op jit(solution)/shard_map/ppermute | solution.py:23
  44.8 6.9 %collective-permute-start.11 = (bf16[2,4,8,1664]{3,2,1,0:T(8,128)(2,1)S(1)}, bf16[2,4,8,1664]{3,2,1,0:T(8,128)(2,1)S(1)}, u32[]{:S(2)}, u32[]{:S(2)}) collective-permute-start(bf16[2,4,8,1664]{3,2,1,0:T(8,128)(2,1)S(1)} %get-tuple-element.68.refs_1_.refs_2_), channel_id=1, source_target_pairs={{0,2},{1,3},{2,0},{3,1},{4,6},{5,7},{6,4},{7,5},{8,10},{9,11},{10,... | collective-permute-start | bytes 638984 | tf_op jit(solution)/shard_map/ppermute | solution.py:23
  49.0 7.3 %collective-permute-start.17 = (bf16[2,4,8,1664]{3,2,1,0:T(8,128)(2,1)S(1)}, bf16[2,4,8,1664]{3,2,1,0:T(8,128)(2,1)S(1)}, u32[]{:S(2)}, u32[]{:S(2)}) collective-permute-start(bf16[2,4,8,1664]{3,2,1,0:T(8,128)(2,1)S(1)} %get-tuple-element.74), channel_id=1, source_target_pairs={{0,4},{1,5},{2,6},{3,7},{4,0},{5,1},{6,2},{7,3},{8,12},{9,13},{10,... | collective-permute-start | bytes 638984 | tf_op jit(solution)/shard_map/ppermute | solution.py:23
  50.6 5.8 %collective-permute-start.16 = (bf16[2,4,8,1664]{3,2,1,0:T(8,128)(2,1)S(1)}, bf16[2,4,8,1664]{3,2,1,0:T(8,128)(2,1)S(1)}, u32[]{:S(2)}, u32[]{:S(2)}) collective-permute-start(bf16[2,4,8,1664]{3,2,1,0:T(8,128)(2,1)S(1)} %get-tuple-element.73.refs_2_), channel_id=1, source_target_pairs={{0,2},{1,3},{2,0},{3,1},{4,6},{5,7},{6,4},{7,5},{8,10},{9,11},{10,... | collective-permute-start | bytes 638984 | tf_op jit(solution)/shard_map/ppermute | solution.py:23
  51.8 5.1 %collective-permute-start.18 = (bf16[8,4,8,1664]{3,2,1,0:T(8,128)(2,1)S(1)}, bf16[8,4,8,1664]{3,2,1,0:T(8,128)(2,1)S(1)}, u32[]{:S(2)}, u32[]{:S(2)}) collective-permute-start(bf16[8,4,8,1664]{3,2,1,0:T(8,128)(2,1)S(1)} %shard_map.107.refs_2_.refs_0_), channel_id=1, source_target_pairs={{0,1},{1,0},{2,3},{3,2},{4,5},{5,4},{6,7},{7,6},{8,9},{9,8},{10,11... | collective-permute-start | bytes 2555912 | tf_op jit(solution)/shard_map/ppermute | solution.py:23
  56.6 2.4 %collective-permute-start.19 = (bf16[8,4,8,1664]{3,2,1,0:T(8,128)(2,1)S(1)}, bf16[8,4,8,1664]{3,2,1,0:T(8,128)(2,1)S(1)}, u32[]{:S(2)}, u32[]{:S(2)}) collective-permute-start(bf16[8,4,8,1664]{3,2,1,0:T(8,128)(2,1)S(1)} %shard_map.114.refs_1_), channel_id=1, source_target_pairs={{0,1},{1,0},{2,3},{3,2},{4,5},{5,4},{6,7},{7,6},{8,9},{9,8},{10,11... | collective-permute-start | bytes 2555912 | tf_op jit(solution)/shard_map/ppermute | solution.py:23
  80.7 2.4 %collective-permute-start.25 = (bf16[8,8,6144]{2,1,0:T(8,128)(2,1)S(1)}, bf16[8,8,6144]{2,1,0:T(8,128)(2,1)S(1)}, u32[]{:S(2)}, u32[]{:S(2)}) collective-permute-start(bf16[8,8,6144]{2,1,0:T(8,128)(2,1)S(1)} %get-tuple-element.92), channel_id=1, source_target_pairs={{0,1},{1,0},{2,3},{3,2},{4,5},{5,4},{6,7},{7,6},{8,9},{9,8},{10,11... | collective-permute-start | bytes 2359304 | tf_op jit(solution)/shard_map/ppermute | solution.py:23
  81.1 4.5 %collective-permute-start.20 = (bf16[8,8,6144]{2,1,0:T(8,128)(2,1)S(1)}, bf16[8,8,6144]{2,1,0:T(8,128)(2,1)S(1)}, u32[]{:S(2)}, u32[]{:S(2)}) collective-permute-start(bf16[8,8,6144]{2,1,0:T(8,128)(2,1)S(1)} %get-tuple-element.82), channel_id=1, source_target_pairs={{0,1},{1,0},{2,3},{3,2},{4,5},{5,4},{6,7},{7,6},{8,9},{9,8},{10,11... | collective-permute-start | bytes 2359304 | tf_op jit(solution)/shard_map/ppermute | solution.py:23
  83.3 7.8 %collective-permute-start.26 = (bf16[2,8,6144]{2,1,0:T(8,128)(2,1)S(1)}, bf16[2,8,6144]{2,1,0:T(8,128)(2,1)S(1)}, u32[]{:S(2)}, u32[]{:S(2)}) collective-permute-start(bf16[2,8,6144]{2,1,0:T(8,128)(2,1)S(1)} %get-tuple-element.94), channel_id=1, source_target_pairs={{0,2},{1,3},{2,0},{3,1},{4,6},{5,7},{6,4},{7,5},{8,10},{9,11},{10,... | collective-permute-start | bytes 589832 | tf_op jit(solution)/shard_map/ppermute | solution.py:23
  84.6 7.8 %collective-permute-start.27 = (bf16[2,8,6144]{2,1,0:T(8,128)(2,1)S(1)}, bf16[2,8,6144]{2,1,0:T(8,128)(2,1)S(1)}, u32[]{:S(2)}, u32[]{:S(2)}) collective-permute-start(bf16[2,8,6144]{2,1,0:T(8,128)(2,1)S(1)} %get-tuple-element.96), channel_id=1, source_target_pairs={{0,4},{1,5},{2,6},{3,7},{4,0},{5,1},{6,2},{7,3},{8,12},{9,13},{10,... | collective-permute-start | bytes 589832 | tf_op jit(solution)/shard_map/ppermute | solution.py:23
  85.8 14.5 %collective-permute-start.21 = (bf16[2,8,6144]{2,1,0:T(8,128)(2,1)S(1)}, bf16[2,8,6144]{2,1,0:T(8,128)(2,1)S(1)}, u32[]{:S(2)}, u32[]{:S(2)}) collective-permute-start(bf16[2,8,6144]{2,1,0:T(8,128)(2,1)S(1)} %get-tuple-element.84), channel_id=1, source_target_pairs={{0,2},{1,3},{2,0},{3,1},{4,6},{5,7},{6,4},{7,5},{8,10},{9,11},{10,... | collective-permute-start | bytes 589832 | tf_op jit(solution)/shard_map/ppermute | solution.py:23
  86.8 13.5 %collective-permute-start.22 = (bf16[2,8,6144]{2,1,0:T(8,128)(2,1)S(1)}, bf16[2,8,6144]{2,1,0:T(8,128)(2,1)S(1)}, u32[]{:S(2)}, u32[]{:S(2)}) collective-permute-start(bf16[2,8,6144]{2,1,0:T(8,128)(2,1)S(1)} %get-tuple-element.86), channel_id=1, source_target_pairs={{0,4},{1,5},{2,6},{3,7},{4,0},{5,1},{6,2},{7,3},{8,12},{9,13},{10,... | collective-permute-start | bytes 589832 | tf_op jit(solution)/shard_map/ppermute | solution.py:23
  92.5 5.3 %collective-permute-start.28 = (bf16[1,8,6144]{2,1,0:T(8,128)(2,1)S(1)}, bf16[1,8,6144]{2,1,0:T(8,128)(2,1)S(1)}, u32[]{:S(2)}, u32[]{:S(2)}) collective-permute-start(bf16[1,8,6144]{2,1,0:T(8,128)(2,1)S(1)} %get-tuple-element.98), channel_id=1, source_target_pairs={{0,4},{1,5},{2,6},{3,7},{4,0},{5,1},{6,2},{7,3},{8,12},{9,13},{10,... | collective-permute-start | bytes 294920 | tf_op jit(solution)/shard_map/ppermute | solution.py:23
  93.5 4.6 %collective-permute-start.29 = (bf16[1,8,6144]{2,1,0:T(8,128)(2,1)S(1)}, bf16[1,8,6144]{2,1,0:T(8,128)(2,1)S(1)}, u32[]{:S(2)}, u32[]{:S(2)}) collective-permute-start(bf16[1,8,6144]{2,1,0:T(8,128)(2,1)S(1)} %get-tuple-element.100), channel_id=1, source_target_pairs={{0,2},{1,3},{2,0},{3,1},{4,6},{5,7},{6,4},{7,5},{8,10},{9,11},{10,... | collective-permute-start | bytes 294920 | tf_op jit(solution)/shard_map/ppermute | solution.py:23
  98.2 8.2 %collective-permute-start.30 = (bf16[2,8,6144]{2,1,0:T(8,128)(2,1)S(1)}, bf16[2,8,6144]{2,1,0:T(8,128)(2,1)S(1)}, u32[]{:S(2)}, u32[]{:S(2)}) collective-permute-start(bf16[2,8,6144]{2,1,0:T(8,128)(2,1)S(1)} %shard_map.120), channel_id=1, source_target_pairs={{0,8},{8,0},{16,24},{24,16},{1,9},{9,1},{17,25},{25,17},{2,10},{10... | collective-permute-start | bytes 589832 | tf_op jit(solution)/shard_map/ppermute | solution.py:23
  100.4 4.7 %collective-permute-start.23 = (bf16[1,8,6144]{2,1,0:T(8,128)(2,1)S(1)}, bf16[1,8,6144]{2,1,0:T(8,128)(2,1)S(1)}, u32[]{:S(2)}, u32[]{:S(2)}) collective-permute-start(bf16[1,8,6144]{2,1,0:T(8,128)(2,1)S(1)} %get-tuple-element.88), channel_id=1, source_target_pairs={{0,4},{1,5},{2,6},{3,7},{4,0},{5,1},{6,2},{7,3},{8,12},{9,13},{10,... | collective-permute-start | bytes 294920 | tf_op jit(solution)/shard_map/ppermute | solution.py:23
  101.8 4.6 %collective-permute-start.24 = (bf16[1,8,6144]{2,1,0:T(8,128)(2,1)S(1)}, bf16[1,8,6144]{2,1,0:T(8,128)(2,1)S(1)}, u32[]{:S(2)}, u32[]{:S(2)}) collective-permute-start(bf16[1,8,6144]{2,1,0:T(8,128)(2,1)S(1)} %get-tuple-element.90), channel_id=1, source_target_pairs={{0,2},{1,3},{2,0},{3,1},{4,6},{5,7},{6,4},{7,5},{8,10},{9,11},{10,... | collective-permute-start | bytes 294920 | tf_op jit(solution)/shard_map/ppermute | solution.py:23
  106.5 6.2 %collective-permute-start.31 = (bf16[1,8,6144]{2,1,0:T(8,128)(2,1)S(1)}, bf16[1,8,6144]{2,1,0:T(8,128)(2,1)S(1)}, u32[]{:S(2)}, u32[]{:S(2)}) collective-permute-start(bf16[1,8,6144]{2,1,0:T(8,128)(2,1)S(1)} %get-tuple-element.102), channel_id=1, source_target_pairs={{0,16},{8,24},{16,0},{24,8},{1,17},{9,25},{17,1},{25,9},{2,18},{10... | collective-permute-start | bytes 294920 | tf_op jit(solution)/shard_map/ppermute | solution.py:23
  (5 other events, 38.7 us)

commit v3 on v2

--- a/solution.py
+++ b/solution.py
@@ -255,8 +255,8 @@
     helds, refs = (refs[:gate_count], refs[gate_count:held]), refs[held:]
     gain, *streamed, down = refs[:4]
     outs, hidden, refs = refs[4 : 2 * groups + 4], refs[2 * groups + 4], refs[2 * groups + 5 :]
-    *sums, activated, block, shift, spread, scale = refs[:7]
-    *slots, down_slots, gate_sems, up_sems, down_sems = refs[7:]
+    *sums, activated, block, next_block, shift, spread, scale = refs[:8]
+    *slots, down_slots, gate_sems, up_sems, down_sems = refs[8:]
     sems = (gate_sems, up_sems)
     ctx, exp = lax.axis_index("ctx"), lax.axis_index("exp")
     chips = E // 2
@@ -266,7 +266,6 @@
     features = hidden.shape[1]
     up_steps = C * per_block
     firsts = [count * per_block for count in held_counts]
-    first = max(firsts)
     down_steps = features // columns
     aheads, down_ahead = [ref.shape[0] for ref in slots], down_slots.shape[0]
 
@@ -326,6 +325,18 @@
                 own = packed[g][s * chips, ctx, :, at].astype(F32)
                 hidden[:, pl.ds(place, width)] = own + shift[k, 0, :token_rows]
 
+    def normalise_any(j, part, target):
+        k = j ^ ctx
+        s = k // groups
+        at = slice(part * width, (part + 1) * width)
+        place = slice(j * cols + part * width, j * cols + (part + 1) * width)
+        centered = read(groups - 1, s, at)
+        for g in range(groups - 1):
+            centered = jnp.where(k % groups == g, read(g, s, at), centered)
+        value = (centered + shift[k, 1]) * spread[...]
+        target[...] = (value * gain[:, place]).astype(BF16)
+        hidden[:, place] = centered[:token_rows] + shift[k, 0, :token_rows]
+
     turned_dot = functools.partial(
         lax.dot_general,
         dimension_numbers=(((1,), (1,)), ((), ())),
@@ -336,35 +347,45 @@
             total[...] = jnp.zeros_like(total)
         for i in range(down_ahead):
             down_copy(i, i).start()
-    for i in range(first):
-        j, part = i // per_block, i % per_block
-        normalise(j, part)
+    static_steps = up_steps if held else 0
+    blocks = (block, next_block)
+    for i in range(static_steps):
+        if i == 0:
+            normalise_any(0, 0, blocks[0])
+        for n in range(2):
+            if i >= firsts[n]:
+                up_copy(n, i, (i - firsts[n]) % aheads[n]).wait()
+        if i + 1 < up_steps:
+            normalise_any((i + 1) // per_block, (i + 1) % per_block, blocks[(i + 1) % 2])
         for n, total in enumerate(sums):
-            slot = (i - firsts[n]) % aheads[n]
             if i < firsts[n]:
-                weight = helds[n][j][:, part * width : (part + 1) * width]
+                weight = helds[n][i // per_block]
+                part = i % per_block
+                weight = weight[:, part * width : (part + 1) * width]
             else:
-                up_copy(n, i, slot).wait()
-                weight = slots[n][slot]
-            product = turned_dot(block[...], weight)
+                weight = slots[n][(i - firsts[n]) % aheads[n]]
+            product = turned_dot(blocks[i % 2][...], weight)
             total[...] = product if i == 0 else total[...] + product
+        for n in range(2):
             if i >= firsts[n] and i + aheads[n] < up_steps:
-                up_copy(n, i + aheads[n], slot).start()
-        if i == first // 2:
+                up_copy(n, i + aheads[n], (i - firsts[n]) % aheads[n]).start()
+        if i == 1:
             for d in range(down_ahead):
                 down_copy(d, d).start()
 
-    @pl.loop(first, up_steps)
-    def _(i):
-        normalise(i // per_block, i % per_block)
-        for n, total in enumerate(sums):
-            slot = (i - firsts[n]) % aheads[n]
-            up_copy(n, i, slot).wait()
-            total[...] += turned_dot(block[...], slots[n][slot])
-
-            @pl.when(i + aheads[n] < up_steps)
-            def _():
-                up_copy(n, i + aheads[n], slot).start()
+    if static_steps < up_steps:
+
+        @pl.loop(static_steps, up_steps)
+        def _(i):
+            normalise(i // per_block, i % per_block)
+            for n, total in enumerate(sums):
+                slot = (i - firsts[n]) % aheads[n]
+                up_copy(n, i, slot).wait()
+                total[...] += turned_dot(block[...], slots[n][slot])
+
+                @pl.when(i + aheads[n] < up_steps)
+                def _():
+                    up_copy(n, i + aheads[n], slot).start()
 
     value = sums[0][...]
     value = value / (1.0 + jnp.exp(-value)) * sums[1][...]
@@ -403,7 +424,7 @@
     width = largest_part(cols, 768 if held else 384, 128)
     columns = largest_part(features, 768 if held else 384, 128)
     per_block = cols // width
-    ahead, up_ahead = 2, 3 if held else 2
+    ahead = 3 if held else 2
     down_ahead = 3 if held else 2
     operands = [*packed, *helds[0], *helds[1], gain]
     *outs, hidden = pl.pallas_call(
@@ -417,17 +438,18 @@
             pltpu.VMEM((total, units), F32),
             pltpu.VMEM((total, units), BF16),
             pltpu.VMEM((total, width), BF16),
+            pltpu.VMEM((total, width), BF16),
             pltpu.VMEM((C, 2, total, 1), F32),
             pltpu.VMEM((total, 1), F32),
             pltpu.VMEM((total, 1), F32),
             pltpu.VMEM((ahead, units, width), BF16),
-            pltpu.VMEM((up_ahead, units, width), BF16),
+            pltpu.VMEM((ahead, units, width), BF16),
             pltpu.VMEM((down_ahead, units, columns), BF16),
             pltpu.SemaphoreType.DMA((ahead,)),
-            pltpu.SemaphoreType.DMA((up_ahead,)),
+            pltpu.SemaphoreType.DMA((ahead,)),
             pltpu.SemaphoreType.DMA((down_ahead,)),
         ],
-        compiler_params=pltpu.CompilerParams(vmem_limit_bytes=(33 if held else 58) * MIB),
+        compiler_params=pltpu.CompilerParams(vmem_limit_bytes=(35 if held else 58) * MIB),
         cost_estimate=pl.CostEstimate(
             flops=6 * total * features * units,
             bytes_accessed=6 * features * units + 4 * total * features,
@@ -589,7 +611,7 @@
     token = load(0, 0, sends[0], 44)
     for value in pairs[1:]:
         afters = [sends] + [token] * (len(chip_bits) - 1)
-        last = lambda sent: load(1, 0, sent[0], 44) + load(0, 1, packed[0], 40)
+        last = lambda sent: load(1, 0, sent[0], 44)
         group, sends = spread_over_plane(
             [value], [(0, 0), (0, 1)], orders, chips, afters, last
         )

time: 114 us -> 113 us (level)
  Pallas kernels: 32.8 us -> 30.8 us
  starting transfers between devices: 32.3 us -> 33.7 us
    pallas_call x3 -> x2, Pallas kernels: 6.54 us -> 4.35 us  [load_blocks(): pl.pallas_call(functools.partial(load_kernel, blocks), out_shape=[shape((...]
    ppermute x32, starting transfers between devices: 32.3 us -> 33.7 us  [swap(): lax.ppermute(value, axis, [(i, i ^ mask) for i in range(lax.axis_size(axi...]
  transfers between devices with their start and end apart: 32 -> 32, of which waited for: 21 -> 20; matrix products, arithmetic and copies ran while one was open for 0% -> 0% of each run, Pallas kernels for 7% -> 5%
where the time goes in v3:
time: 113 us
  waiting for transfers between devices  44.1 us (39%)
  starting transfers between devices  33.7 us (30%)
  Pallas kernels  30.8 us (27%)
  local copies, waits for them, and re-layouts  2.9 us (3%)
    ppermute x32, waiting for transfers between devices, swap(): lax.ppermute(value, axis, [(i, i ^ mask) for i in range(lax.axis_size(axi...  44.1 us
    ppermute x32, starting transfers between devices, swap(): lax.ppermute(value, axis, [(i, i ^ mask) for i in range(lax.axis_size(axi...  33.7 us
    pallas_call x1, Pallas kernels, run_experts(): pl.pallas_call(functools.partial(expert_kernel, C, E, per_block, width, c...  21.9 us
    pallas_call x18, Pallas kernels, call(): pl.pallas_call(kernel, out_shape=out_shape, in_specs=in_specs, out_specs=...  4.51 us
    pallas_call x2, Pallas kernels, load_blocks(): pl.pallas_call(functools.partial(load_kernel, blocks), out_shape=[shape((...  4.35 us
    unnamed x10, local copies, waits for them, and re-layouts  2.9 us
  transfers between devices with their start and end apart: 32, of which 20 were waited for; matrix products, arithmetic and copies ran while one was open for 0% of the time, Pallas kernels for 5%

profile of v3, /device:TPU:0, one launch (start us, length us, event | category | flops | bytes accessed | tf_op | source)
XLA Modules:
  0.0 112.6 jit_solution(1465977739714044650)
XLA Ops:
  0.0 1.8 %shard_map.100 = (bf16[11,8,512]{2,1,0:T(8,128)(2,1)}, bf16[11,8,512]{2,1,0:T(8,128)(2,1)}, bf16[11,8,512]{2,1,0:T(8,128)(2,1)}, bf16[11,8,512]{2,1,0:T(8,128)(2,1)}) custom-call(bf16[64,384]{1,0:T(8,128)(2,1)} %queries_in.1, bf16[2,64,64]{2,1,0:T(8,128)(2,1)} %own_in.1, bf16[8,6144]{1,0:T(8,128)(2,1)} %residual_in.1), custom_call_target="tpu_custom_call" | custom-call | tf_op jit(solution)/shard_map/pallas_call | solution.py:27
  1.8 3.1 %collective-permute-start = (bf16[11,8,512]{2,1,0:T(8,128)(2,1)}, bf16[11,8,512]{2,1,0:T(8,128)(2,1)S(1)}, u32[]{:S(2)}, u32[]{:S(2)}) collective-permute-start(bf16[11,8,512]{2,1,0:T(8,128)(2,1)} %get-tuple-element.53), channel_id=1, source_target_pairs={{0,8},{8,0},{16,24},{24,16},{1,9},{9,1},{17,25},{25,17},{2,10},{10... | collective-permute-start | bytes 270344 | tf_op jit(solution)/shard_map/ppermute | solution.py:23
  4.9 2.6 %collective-permute-start.1 = (bf16[11,8,512]{2,1,0:T(8,128)(2,1)}, bf16[11,8,512]{2,1,0:T(8,128)(2,1)S(1)}, u32[]{:S(2)}, u32[]{:S(2)}) collective-permute-start(bf16[11,8,512]{2,1,0:T(8,128)(2,1)} %get-tuple-element.54), channel_id=1, source_target_pairs={{0,16},{8,24},{16,0},{24,8},{1,17},{9,25},{17,1},{25,9},{2,18},{10... | collective-permute-start | bytes 270344 | tf_op jit(solution)/shard_map/ppermute | solution.py:23
  10.5 4.4 %collective-permute-done.1.refs_2_.refs_6_ = bf16[11,8,512]{2,1,0:T(8,128)(2,1)S(1)} collective-permute-done((bf16[11,8,512]{2,1,0:T(8,128)(2,1)}, bf16[11,8,512]{2,1,0:T(8,128)(2,1)S(1)}, u32[]{:S(2)}, u32[]{:S(2)}) %collective-permute-start.1) | collective-permute-done | bytes 90144 | tf_op jit(solution)/shard_map/ppermute | solution.py:23
  16.3 1.4 %shard_map.103 = (bf16[4,4,8,1536]{3,2,1,0:T(8,128)(2,1)S(1)}, f32[4,4,8,1536]{3,2,1,0:T(8,128)S(1)}) custom-call(bf16[11,8,512]{2,1,0:T(8,128)(2,1)S(1)} %copy-done.1, bf16[11,8,512]{2,1,0:T(8,128)(2,1)S(1)} %collective-permute-done.refs_1_.refs_5_, bf16[11,8,512]{2,1,0:T(8,128)(2,1)S(1)} %collective-permute-done.1.refs_2_.refs_6_, ...), custom_call_target="tpu_custom_call" | custom-call | tf_op jit(solution)/shard_map/pallas_call | solution.py:27
  18.0 1.5 %collective-permute-done.4.received = bf16[4,4,8,1536]{3,2,1,0:T(8,128)(2,1)S(1)} collective-permute-done((bf16[4,4,8,1536]{3,2,1,0:T(8,128)(2,1)S(1)}, bf16[4,4,8,1536]{3,2,1,0:T(8,128)(2,1)S(1)}, u32[]{:S(2)}, u32[]{:S(2)}) %collective-permute-start.4) | collective-permute-done | bytes 393248 | tf_op jit(solution)/shard_map/ppermute | solution.py:23
  19.5 1.6 %collective-permute-start.5 = (bf16[4,8,1536]{2,1,0:T(8,128)(2,1)S(1)}, bf16[4,8,1536]{2,1,0:T(8,128)(2,1)S(1)}, u32[]{:S(2)}, u32[]{:S(2)}) collective-permute-start(bf16[4,8,1536]{2,1,0:T(8,128)(2,1)S(1)} %get-tuple-element.62), channel_id=1, source_target_pairs={{0,2},{1,3},{2,0},{3,1},{4,6},{5,7},{6,4},{7,5},{8,10},{9,11},{10,... | collective-permute-start | bytes 294920 | tf_op jit(solution)/shard_map/ppermute | solution.py:23
  21.1 1.5 %collective-permute-start.6 = (bf16[4,8,1536]{2,1,0:T(8,128)(2,1)S(1)}, bf16[4,8,1536]{2,1,0:T(8,128)(2,1)S(1)}, u32[]{:S(2)}, u32[]{:S(2)}) collective-permute-start(bf16[4,8,1536]{2,1,0:T(8,128)(2,1)S(1)} %get-tuple-element.63), channel_id=1, source_target_pairs={{0,4},{1,5},{2,6},{3,7},{4,0},{5,1},{6,2},{7,3},{8,12},{9,13},{10,... | collective-permute-start | bytes 294920 | tf_op jit(solution)/shard_map/ppermute | solution.py:23
  23.2 1.3 %collective-permute-done.5.refs_1_ = bf16[4,8,1536]{2,1,0:T(8,128)(2,1)S(1)} collective-permute-done((bf16[4,8,1536]{2,1,0:T(8,128)(2,1)S(1)}, bf16[4,8,1536]{2,1,0:T(8,128)(2,1)S(1)}, u32[]{:S(2)}, u32[]{:S(2)}) %collective-permute-start.5) | collective-permute-done | bytes 98336 | tf_op jit(solution)/shard_map/ppermute | solution.py:23
  24.5 2.4 %collective-permute-done.6.refs_2_ = bf16[4,8,1536]{2,1,0:T(8,128)(2,1)S(1)} collective-permute-done((bf16[4,8,1536]{2,1,0:T(8,128)(2,1)S(1)}, bf16[4,8,1536]{2,1,0:T(8,128)(2,1)S(1)}, u32[]{:S(2)}, u32[]{:S(2)}) %collective-permute-start.6) | collective-permute-done | bytes 98336 | tf_op jit(solution)/shard_map/ppermute | solution.py:23
  28.4 2.6 %collective-permute-start.8 = (bf16[4,8,1664]{2,1,0:T(8,128)(2,1)S(1)}, bf16[4,8,1664]{2,1,0:T(8,128)(2,1)S(1)}, u32[]{:S(2)}, u32[]{:S(2)}) collective-permute-start(bf16[4,8,1664]{2,1,0:T(8,128)(2,1)S(1)} %shard_map.105.refs_0_), channel_id=1, source_target_pairs={{0,16},{8,24},{16,0},{24,8},{1,17},{9,25},{17,1},{25,9},{2,18},{10... | collective-permute-start | bytes 319496 | tf_op jit(solution)/shard_map/ppermute | solution.py:23
  31.0 4.2 %collective-permute-done.8.refs_1_ = bf16[4,8,1664]{2,1,0:T(8,128)(2,1)S(1)} collective-permute-done((bf16[4,8,1664]{2,1,0:T(8,128)(2,1)S(1)}, bf16[4,8,1664]{2,1,0:T(8,128)(2,1)S(1)}, u32[]{:S(2)}, u32[]{:S(2)}) %collective-permute-start.8) | collective-permute-done | bytes 106528 | tf_op jit(solution)/shard_map/ppermute | solution.py:23
  37.5 3.5 %collective-permute-done.9.refs_2_ = bf16[4,8,1664]{2,1,0:T(8,128)(2,1)S(1)} collective-permute-done((bf16[4,8,1664]{2,1,0:T(8,128)(2,1)S(1)}, bf16[4,8,1664]{2,1,0:T(8,128)(2,1)S(1)}, u32[]{:S(2)}, u32[]{:S(2)}) %collective-permute-start.9) | collective-permute-done | bytes 106528 | tf_op jit(solution)/shard_map/ppermute | solution.py:23
  41.0 1.6 %collective-permute-done.10.refs_3_ = bf16[4,8,1664]{2,1,0:T(8,128)(2,1)S(1)} collective-permute-done((bf16[4,8,1664]{2,1,0:T(8,128)(2,1)S(1)}, bf16[4,8,1664]{2,1,0:T(8,128)(2,1)S(1)}, u32[]{:S(2)}, u32[]{:S(2)}) %collective-permute-start.10) | collective-permute-done | bytes 106528 | tf_op jit(solution)/shard_map/ppermute | solution.py:23
  44.8 1.9 %collective-permute-start.11 = (bf16[2,4,8,1664]{3,2,1,0:T(8,128)(2,1)S(1)}, bf16[2,4,8,1664]{3,2,1,0:T(8,128)(2,1)S(1)}, u32[]{:S(2)}, u32[]{:S(2)}) collective-permute-start(bf16[2,4,8,1664]{3,2,1,0:T(8,128)(2,1)S(1)} %get-tuple-element.66.refs_1_.refs_2_), channel_id=1, source_target_pairs={{0,2},{1,3},{2,0},{3,1},{4,6},{5,7},{6,4},{7,5},{8,10},{9,11},{10,... | collective-permute-start | bytes 638984 | tf_op jit(solution)/shard_map/ppermute | solution.py:23
  46.7 2.2 %shard_map.110 = (bf16[1344,1536]{1,0:T(8,128)(2,1)S(1)}, f32[8,128]{1,0:T(8,128)S(1)}) custom-call(bf16[1,1344,6144]{2,1,0:T(8,128)(2,1)} %bitcast.10, bf16[1,1344,6144]{2,1,0:T(8,128)(2,1)} %bitcast.13, bf16[2,4,8,1664]{3,2,1,0:T(8,128)(2,1)S(1)} %get-tuple-element.66.refs_1_.refs_2_), custom_call_target="tpu_custom_call" | custom-call | bytes 8257536 | tf_op jit(solution)/shard_map/pallas_call | solution.py:237
  49.0 1.7 %collective-permute-start.17 = (bf16[2,4,8,1664]{3,2,1,0:T(8,128)(2,1)S(1)}, bf16[2,4,8,1664]{3,2,1,0:T(8,128)(2,1)S(1)}, u32[]{:S(2)}, u32[]{:S(2)}) collective-permute-start(bf16[2,4,8,1664]{3,2,1,0:T(8,128)(2,1)S(1)} %get-tuple-element.72), channel_id=1, source_target_pairs={{0,4},{1,5},{2,6},{3,7},{4,0},{5,1},{6,2},{7,3},{8,12},{9,13},{10,... | collective-permute-start | bytes 638984 | tf_op jit(solution)/shard_map/ppermute | solution.py:23
  50.7 2.2 %shard_map.112 = (bf16[1344,1536]{1,0:T(8,128)(2,1)S(1)}, f32[8,128]{1,0:T(8,128)S(1)}) custom-call(bf16[1,1344,6144]{2,1,0:T(8,128)(2,1)} %bitcast.11, bf16[1,1344,6144]{2,1,0:T(8,128)(2,1)} %bitcast.14, bf16[2,4,8,1664]{3,2,1,0:T(8,128)(2,1)S(1)} %get-tuple-element.71.refs_2_), custom_call_target="tpu_custom_call" | custom-call | bytes 8257536 | tf_op jit(solution)/shard_map/pallas_call | solution.py:237
  53.0 1.9 %collective-permute-done.17.refs_4_ = bf16[2,4,8,1664]{3,2,1,0:T(8,128)(2,1)S(1)} collective-permute-done((bf16[2,4,8,1664]{3,2,1,0:T(8,128)(2,1)S(1)}, bf16[2,4,8,1664]{3,2,1,0:T(8,128)(2,1)S(1)}, u32[]{:S(2)}, u32[]{:S(2)}) %collective-permute-start.17) | collective-permute-done | bytes 213024 | tf_op jit(solution)/shard_map/ppermute | solution.py:23
  54.9 1.6 %collective-permute-done.16.refs_3_ = bf16[2,4,8,1664]{3,2,1,0:T(8,128)(2,1)S(1)} collective-permute-done((bf16[2,4,8,1664]{3,2,1,0:T(8,128)(2,1)S(1)}, bf16[2,4,8,1664]{3,2,1,0:T(8,128)(2,1)S(1)}, u32[]{:S(2)}, u32[]{:S(2)}) %collective-permute-start.16) | collective-permute-done | bytes 213024 | tf_op jit(solution)/shard_map/ppermute | solution.py:23
  56.7 2.4 %collective-permute-done.19.refs_3_ = bf16[8,4,8,1664]{3,2,1,0:T(8,128)(2,1)S(1)} collective-permute-done((bf16[8,4,8,1664]{3,2,1,0:T(8,128)(2,1)S(1)}, bf16[8,4,8,1664]{3,2,1,0:T(8,128)(2,1)S(1)}, u32[]{:S(2)}, u32[]{:S(2)}) %collective-permute-start.19) | collective-permute-done | bytes 852000 | tf_op jit(solution)/shard_map/ppermute | solution.py:23
  59.0 21.9 %shard_map.114 = (bf16[8,8,6144]{2,1,0:T(8,128)(2,1)S(1)}, bf16[8,8,6144]{2,1,0:T(8,128)(2,1)S(1)}, bf16[8,8,6144]{2,1,0:T(8,128)(2,1)S(1)}, bf16[8,8,6144]{2,1,0:T(8,128)(2,1)S(1)}, f32[8,6144]{1,0:T(8,128)S(1)}) custom-call(bf16[8,4,8,1664]{3,2,1,0:T(8,128)(2,1)S(1)} %shard_map.107.refs_0_, bf16[8,4,8,1664]{3,2,1,0:T(8,128)(2,1)S(1)} %shard_map.113.refs_1_, ...), custom_call_target="tpu_custom_call" | custom-call | flops 12683575296 | bytes 55836672 | tf_op jit(solution)/shard_map/pallas_call | solution.py:430
  81.5 1.8 %collective-permute-done.25.refs_1_ = bf16[8,8,6144]{2,1,0:T(8,128)(2,1)S(1)} collective-permute-done((bf16[8,8,6144]{2,1,0:T(8,128)(2,1)S(1)}, bf16[8,8,6144]{2,1,0:T(8,128)(2,1)S(1)}, u32[]{:S(2)}, u32[]{:S(2)}) %collective-permute-start.25) | collective-permute-done | bytes 786464 | tf_op jit(solution)/shard_map/ppermute | solution.py:23
  84.6 1.7 %collective-permute-start.21 = (bf16[2,8,6144]{2,1,0:T(8,128)(2,1)S(1)}, bf16[2,8,6144]{2,1,0:T(8,128)(2,1)S(1)}, u32[]{:S(2)}, u32[]{:S(2)}) collective-permute-start(bf16[2,8,6144]{2,1,0:T(8,128)(2,1)S(1)} %get-tuple-element.80), channel_id=1, source_target_pairs={{0,2},{1,3},{2,0},{3,1},{4,6},{5,7},{6,4},{7,5},{8,10},{9,11},{10,... | collective-permute-start | bytes 589832 | tf_op jit(solution)/shard_map/ppermute | solution.py:23
  86.3 1.6 %collective-permute-start.22 = (bf16[2,8,6144]{2,1,0:T(8,128)(2,1)S(1)}, bf16[2,8,6144]{2,1,0:T(8,128)(2,1)S(1)}, u32[]{:S(2)}, u32[]{:S(2)}) collective-permute-start(bf16[2,8,6144]{2,1,0:T(8,128)(2,1)S(1)} %get-tuple-element.82), channel_id=1, source_target_pairs={{0,4},{1,5},{2,6},{3,7},{4,0},{5,1},{6,2},{7,3},{8,12},{9,13},{10,... | collective-permute-start | bytes 589832 | tf_op jit(solution)/shard_map/ppermute | solution.py:23
  87.9 3.4 %collective-permute-done.26.refs_1_ = bf16[2,8,6144]{2,1,0:T(8,128)(2,1)S(1)} collective-permute-done((bf16[2,8,6144]{2,1,0:T(8,128)(2,1)S(1)}, bf16[2,8,6144]{2,1,0:T(8,128)(2,1)S(1)}, u32[]{:S(2)}, u32[]{:S(2)}) %collective-permute-start.26) | collective-permute-done | bytes 196640 | tf_op jit(solution)/shard_map/ppermute | solution.py:23
  92.3 1.7 %collective-permute-start.29 = (bf16[1,8,6144]{2,1,0:T(8,128)(2,1)S(1)}, bf16[1,8,6144]{2,1,0:T(8,128)(2,1)S(1)}, u32[]{:S(2)}, u32[]{:S(2)}) collective-permute-start(bf16[1,8,6144]{2,1,0:T(8,128)(2,1)S(1)} %get-tuple-element.96), channel_id=1, source_target_pairs={{0,2},{1,3},{2,0},{3,1},{4,6},{5,7},{6,4},{7,5},{8,10},{9,11},{10,... | collective-permute-start | bytes 294920 | tf_op jit(solution)/shard_map/ppermute | solution.py:23
  94.0 2.9 %collective-permute-done.28.refs_1_ = bf16[1,8,6144]{2,1,0:T(8,128)(2,1)S(1)} collective-permute-done((bf16[1,8,6144]{2,1,0:T(8,128)(2,1)S(1)}, bf16[1,8,6144]{2,1,0:T(8,128)(2,1)S(1)}, u32[]{:S(2)}, u32[]{:S(2)}) %collective-permute-start.28) | collective-permute-done | bytes 98336 | tf_op jit(solution)/shard_map/ppermute | solution.py:23
  97.0 3.1 %collective-permute-start.30 = (bf16[2,8,6144]{2,1,0:T(8,128)(2,1)S(1)}, bf16[2,8,6144]{2,1,0:T(8,128)(2,1)S(1)}, u32[]{:S(2)}, u32[]{:S(2)}) collective-permute-start(bf16[2,8,6144]{2,1,0:T(8,128)(2,1)S(1)} %shard_map.119), channel_id=1, source_target_pairs={{0,8},{8,0},{16,24},{24,16},{1,9},{9,1},{17,25},{25,17},{2,10},{10... | collective-permute-start | bytes 589832 | tf_op jit(solution)/shard_map/ppermute | solution.py:23
  101.8 3.0 %collective-permute-done.23.refs_1_ = bf16[1,8,6144]{2,1,0:T(8,128)(2,1)S(1)} collective-permute-done((bf16[1,8,6144]{2,1,0:T(8,128)(2,1)S(1)}, bf16[1,8,6144]{2,1,0:T(8,128)(2,1)S(1)}, u32[]{:S(2)}, u32[]{:S(2)}) %collective-permute-start.23) | collective-permute-done | bytes 98336 | tf_op jit(solution)/shard_map/ppermute | solution.py:23
  105.4 1.4 %collective-permute-start.31 = (bf16[1,8,6144]{2,1,0:T(8,128)(2,1)S(1)}, bf16[1,8,6144]{2,1,0:T(8,128)(2,1)S(1)}, u32[]{:S(2)}, u32[]{:S(2)}) collective-permute-start(bf16[1,8,6144]{2,1,0:T(8,128)(2,1)S(1)} %get-tuple-element.98), channel_id=1, source_target_pairs={{0,16},{8,24},{16,0},{24,8},{1,17},{9,25},{17,1},{25,9},{2,18},{10... | collective-permute-start | bytes 294920 | tf_op jit(solution)/shard_map/ppermute | solution.py:23
  106.9 5.0 %collective-permute-done.31 = bf16[1,8,6144]{2,1,0:T(8,128)(2,1)S(1)} collective-permute-done((bf16[1,8,6144]{2,1,0:T(8,128)(2,1)S(1)}, bf16[1,8,6144]{2,1,0:T(8,128)(2,1)S(1)}, u32[]{:S(2)}, u32[]{:S(2)}) %collective-permute-start.31) | collective-permute-done | bytes 98336 | tf_op jit(solution)/shard_map/ppermute | solution.py:23
  (67 shorter events, 17.6 us)
Async XLA Ops:
  1.8 8.7 %collective-permute-start = (bf16[11,8,512]{2,1,0:T(8,128)(2,1)}, bf16[11,8,512]{2,1,0:T(8,128)(2,1)S(1)}, u32[]{:S(2)}, u32[]{:S(2)}) collective-permute-start(bf16[11,8,512]{2,1,0:T(8,128)(2,1)} %get-tuple-element.53), channel_id=1, source_target_pairs={{0,8},{8,0},{16,24},{24,16},{1,9},{9,1},{17,25},{25,17},{2,10},{10... | collective-permute-start | bytes 270344 | tf_op jit(solution)/shard_map/ppermute | solution.py:23
  4.9 10.0 %collective-permute-start.1 = (bf16[11,8,512]{2,1,0:T(8,128)(2,1)}, bf16[11,8,512]{2,1,0:T(8,128)(2,1)S(1)}, u32[]{:S(2)}, u32[]{:S(2)}) collective-permute-start(bf16[11,8,512]{2,1,0:T(8,128)(2,1)} %get-tuple-element.54), channel_id=1, source_target_pairs={{0,16},{8,24},{16,0},{24,8},{1,17},{9,25},{17,1},{25,9},{2,18},{10... | collective-permute-start | bytes 270344 | tf_op jit(solution)/shard_map/ppermute | solution.py:23
  7.5 7.4 %collective-permute-start.2 = (bf16[11,8,512]{2,1,0:T(8,128)(2,1)}, bf16[11,8,512]{2,1,0:T(8,128)(2,1)S(1)}, u32[]{:S(2)}, u32[]{:S(2)}) collective-permute-start(bf16[11,8,512]{2,1,0:T(8,128)(2,1)} %get-tuple-element.55), channel_id=1, source_target_pairs={{0,24},{8,16},{16,8},{24,0},{1,25},{9,17},{17,9},{25,1},{2,26},{10... | collective-permute-start | bytes 270344 | tf_op jit(solution)/shard_map/ppermute | solution.py:23
  14.9 1.3 %collective-permute-start.3 = (bf16[4,8,8,128]{3,2,1,0:T(8,128)(2,1)S(1)}, bf16[4,8,8,128]{3,2,1,0:T(8,128)(2,1)S(1)}, u32[]{:S(2)}, u32[]{:S(2)}) collective-permute-start(bf16[4,8,8,128]{3,2,1,0:T(8,128)(2,1)S(1)} %get-tuple-element.58), channel_id=1, source_target_pairs={{0,1},{1,0},{2,3},{3,2},{4,5},{5,4},{6,7},{7,6},{8,9},{9,8},{10,11... | collective-permute-start | bytes 196616 | tf_op jit(solution)/shard_map/ppermute | solution.py:23
  17.7 1.8 %collective-permute-start.4 = (bf16[4,4,8,1536]{3,2,1,0:T(8,128)(2,1)S(1)}, bf16[4,4,8,1536]{3,2,1,0:T(8,128)(2,1)S(1)}, u32[]{:S(2)}, u32[]{:S(2)}) collective-permute-start(bf16[4,4,8,1536]{3,2,1,0:T(8,128)(2,1)S(1)} %get-tuple-element.60), channel_id=1, source_target_pairs={{0,1},{1,0},{2,3},{3,2},{4,5},{5,4},{6,7},{7,6},{8,9},{9,8},{10,11... | collective-permute-start | bytes 1179656 | tf_op jit(solution)/shard_map/ppermute | solution.py:23
  19.5 4.9 %collective-permute-start.5 = (bf16[4,8,1536]{2,1,0:T(8,128)(2,1)S(1)}, bf16[4,8,1536]{2,1,0:T(8,128)(2,1)S(1)}, u32[]{:S(2)}, u32[]{:S(2)}) collective-permute-start(bf16[4,8,1536]{2,1,0:T(8,128)(2,1)S(1)} %get-tuple-element.62), channel_id=1, source_target_pairs={{0,2},{1,3},{2,0},{3,1},{4,6},{5,7},{6,4},{7,5},{8,10},{9,11},{10,... | collective-permute-start | bytes 294920 | tf_op jit(solution)/shard_map/ppermute | solution.py:23
  21.1 5.8 %collective-permute-start.6 = (bf16[4,8,1536]{2,1,0:T(8,128)(2,1)S(1)}, bf16[4,8,1536]{2,1,0:T(8,128)(2,1)S(1)}, u32[]{:S(2)}, u32[]{:S(2)}) collective-permute-start(bf16[4,8,1536]{2,1,0:T(8,128)(2,1)S(1)} %get-tuple-element.63), channel_id=1, source_target_pairs={{0,4},{1,5},{2,6},{3,7},{4,0},{5,1},{6,2},{7,3},{8,12},{9,13},{10,... | collective-permute-start | bytes 294920 | tf_op jit(solution)/shard_map/ppermute | solution.py:23
  22.6 5.5 %collective-permute-start.7 = (bf16[4,8,1536]{2,1,0:T(8,128)(2,1)S(1)}, bf16[4,8,1536]{2,1,0:T(8,128)(2,1)S(1)}, u32[]{:S(2)}, u32[]{:S(2)}) collective-permute-start(bf16[4,8,1536]{2,1,0:T(8,128)(2,1)S(1)} %get-tuple-element.64), channel_id=1, source_target_pairs={{0,6},{1,7},{2,4},{3,5},{4,2},{5,3},{6,0},{7,1},{8,14},{9,15},{10,... | collective-permute-start | bytes 294920 | tf_op jit(solution)/shard_map/ppermute | solution.py:23
  28.4 6.8 %collective-permute-start.8 = (bf16[4,8,1664]{2,1,0:T(8,128)(2,1)S(1)}, bf16[4,8,1664]{2,1,0:T(8,128)(2,1)S(1)}, u32[]{:S(2)}, u32[]{:S(2)}) collective-permute-start(bf16[4,8,1664]{2,1,0:T(8,128)(2,1)S(1)} %shard_map.105.refs_0_), channel_id=1, source_target_pairs={{0,16},{8,24},{16,0},{24,8},{1,17},{9,25},{17,1},{25,9},{2,18},{10... | collective-permute-start | bytes 319496 | tf_op jit(solution)/shard_map/ppermute | solution.py:23
  35.2 7.4 %collective-permute-start.13 = (bf16[2,4,8,1664]{3,2,1,0:T(8,128)(2,1)S(1)}, bf16[2,4,8,1664]{3,2,1,0:T(8,128)(2,1)S(1)}, u32[]{:S(2)}, u32[]{:S(2)}) collective-permute-start(bf16[2,4,8,1664]{3,2,1,0:T(8,128)(2,1)S(1)} %shard_map.108), channel_id=1, source_target_pairs={{0,8},{8,0},{16,24},{24,16},{1,9},{9,1},{17,25},{25,17},{2,10},{10... | collective-permute-start | bytes 638984 | tf_op jit(solution)/shard_map/ppermute | solution.py:23
  35.8 5.2 %collective-permute-start.9 = (bf16[4,8,1664]{2,1,0:T(8,128)(2,1)S(1)}, bf16[4,8,1664]{2,1,0:T(8,128)(2,1)S(1)}, u32[]{:S(2)}, u32[]{:S(2)}) collective-permute-start(bf16[4,8,1664]{2,1,0:T(8,128)(2,1)S(1)} %shard_map.105.refs_0_), channel_id=1, source_target_pairs={{0,4},{1,5},{2,6},{3,7},{4,0},{5,1},{6,2},{7,3},{8,12},{9,13},{10,... | collective-permute-start | bytes 319496 | tf_op jit(solution)/shard_map/ppermute | solution.py:23
  37.0 5.6 %collective-permute-start.10 = (bf16[4,8,1664]{2,1,0:T(8,128)(2,1)S(1)}, bf16[4,8,1664]{2,1,0:T(8,128)(2,1)S(1)}, u32[]{:S(2)}, u32[]{:S(2)}) collective-permute-start(bf16[4,8,1664]{2,1,0:T(8,128)(2,1)S(1)} %collective-permute-done.8.refs_1_), channel_id=1, source_target_pairs={{0,2},{1,3},{2,0},{3,1},{4,6},{5,7},{6,4},{7,5},{8,10},{9,11},{10,... | collective-permute-start | bytes 319496 | tf_op jit(solution)/shard_map/ppermute | solution.py:23
  42.6 6.3 %collective-permute-start.14 = (bf16[4,8,1664]{2,1,0:T(8,128)(2,1)S(1)}, bf16[4,8,1664]{2,1,0:T(8,128)(2,1)S(1)}, u32[]{:S(2)}, u32[]{:S(2)}) collective-permute-start(bf16[4,8,1664]{2,1,0:T(8,128)(2,1)S(1)} %get-tuple-element.68), channel_id=1, source_target_pairs={{0,4},{1,5},{2,6},{3,7},{4,0},{5,1},{6,2},{7,3},{8,12},{9,13},{10,... | collective-permute-start | bytes 319496 | tf_op jit(solution)/shard_map/ppermute | solution.py:23
  43.1 5.9 %collective-permute-start.15 = (bf16[4,8,1664]{2,1,0:T(8,128)(2,1)S(1)}, bf16[4,8,1664]{2,1,0:T(8,128)(2,1)S(1)}, u32[]{:S(2)}, u32[]{:S(2)}) collective-permute-start(bf16[4,8,1664]{2,1,0:T(8,128)(2,1)S(1)} %get-tuple-element.69), channel_id=1, source_target_pairs={{0,2},{1,3},{2,0},{3,1},{4,6},{5,7},{6,4},{7,5},{8,10},{9,11},{10,... | collective-permute-start | bytes 319496 | tf_op jit(solution)/shard_map/ppermute | solution.py:23
  43.8 9.0 %collective-permute-start.12 = (bf16[2,4,8,1664]{3,2,1,0:T(8,128)(2,1)S(1)}, bf16[2,4,8,1664]{3,2,1,0:T(8,128)(2,1)S(1)}, u32[]{:S(2)}, u32[]{:S(2)}) collective-permute-start(bf16[2,4,8,1664]{3,2,1,0:T(8,128)(2,1)S(1)} %get-tuple-element.67.refs_2_), channel_id=1, source_target_pairs={{0,4},{1,5},{2,6},{3,7},{4,0},{5,1},{6,2},{7,3},{8,12},{9,13},{10,... | collective-permute-start | bytes 638984 | tf_op jit(solution)/shard_map/ppermute | solution.py:23
  44.8 8.0 %collective-permute-start.11 = (bf16[2,4,8,1664]{3,2,1,0:T(8,128)(2,1)S(1)}, bf16[2,4,8,1664]{3,2,1,0:T(8,128)(2,1)S(1)}, u32[]{:S(2)}, u32[]{:S(2)}) collective-permute-start(bf16[2,4,8,1664]{3,2,1,0:T(8,128)(2,1)S(1)} %get-tuple-element.66.refs_1_.refs_2_), channel_id=1, source_target_pairs={{0,2},{1,3},{2,0},{3,1},{4,6},{5,7},{6,4},{7,5},{8,10},{9,11},{10,... | collective-permute-start | bytes 638984 | tf_op jit(solution)/shard_map/ppermute | solution.py:23
  49.0 5.9 %collective-permute-start.17 = (bf16[2,4,8,1664]{3,2,1,0:T(8,128)(2,1)S(1)}, bf16[2,4,8,1664]{3,2,1,0:T(8,128)(2,1)S(1)}, u32[]{:S(2)}, u32[]{:S(2)}) collective-permute-start(bf16[2,4,8,1664]{3,2,1,0:T(8,128)(2,1)S(1)} %get-tuple-element.72), channel_id=1, source_target_pairs={{0,4},{1,5},{2,6},{3,7},{4,0},{5,1},{6,2},{7,3},{8,12},{9,13},{10,... | collective-permute-start | bytes 638984 | tf_op jit(solution)/shard_map/ppermute | solution.py:23
  50.7 5.8 %collective-permute-start.16 = (bf16[2,4,8,1664]{3,2,1,0:T(8,128)(2,1)S(1)}, bf16[2,4,8,1664]{3,2,1,0:T(8,128)(2,1)S(1)}, u32[]{:S(2)}, u32[]{:S(2)}) collective-permute-start(bf16[2,4,8,1664]{3,2,1,0:T(8,128)(2,1)S(1)} %get-tuple-element.71.refs_2_), channel_id=1, source_target_pairs={{0,2},{1,3},{2,0},{3,1},{4,6},{5,7},{6,4},{7,5},{8,10},{9,11},{10,... | collective-permute-start | bytes 638984 | tf_op jit(solution)/shard_map/ppermute | solution.py:23
  52.9 3.7 %collective-permute-start.18 = (bf16[8,4,8,1664]{3,2,1,0:T(8,128)(2,1)S(1)}, bf16[8,4,8,1664]{3,2,1,0:T(8,128)(2,1)S(1)}, u32[]{:S(2)}, u32[]{:S(2)}) collective-permute-start(bf16[8,4,8,1664]{3,2,1,0:T(8,128)(2,1)S(1)} %shard_map.107.refs_0_), channel_id=1, source_target_pairs={{0,1},{1,0},{2,3},{3,2},{4,5},{5,4},{6,7},{7,6},{8,9},{9,8},{10,11... | collective-permute-start | bytes 2555912 | tf_op jit(solution)/shard_map/ppermute | solution.py:23
  56.6 2.4 %collective-permute-start.19 = (bf16[8,4,8,1664]{3,2,1,0:T(8,128)(2,1)S(1)}, bf16[8,4,8,1664]{3,2,1,0:T(8,128)(2,1)S(1)}, u32[]{:S(2)}, u32[]{:S(2)}) collective-permute-start(bf16[8,4,8,1664]{3,2,1,0:T(8,128)(2,1)S(1)} %shard_map.113.refs_1_), channel_id=1, source_target_pairs={{0,1},{1,0},{2,3},{3,2},{4,5},{5,4},{6,7},{7,6},{8,9},{9,8},{10,11... | collective-permute-start | bytes 2555912 | tf_op jit(solution)/shard_map/ppermute | solution.py:23
  81.0 2.4 %collective-permute-start.25 = (bf16[8,8,6144]{2,1,0:T(8,128)(2,1)S(1)}, bf16[8,8,6144]{2,1,0:T(8,128)(2,1)S(1)}, u32[]{:S(2)}, u32[]{:S(2)}) collective-permute-start(bf16[8,8,6144]{2,1,0:T(8,128)(2,1)S(1)} %get-tuple-element.88), channel_id=1, source_target_pairs={{0,1},{1,0},{2,3},{3,2},{4,5},{5,4},{6,7},{7,6},{8,9},{9,8},{10,11... | collective-permute-start | bytes 2359304 | tf_op jit(solution)/shard_map/ppermute | solution.py:23
  81.2 3.3 %collective-permute-start.20 = (bf16[8,8,6144]{2,1,0:T(8,128)(2,1)S(1)}, bf16[8,8,6144]{2,1,0:T(8,128)(2,1)S(1)}, u32[]{:S(2)}, u32[]{:S(2)}) collective-permute-start(bf16[8,8,6144]{2,1,0:T(8,128)(2,1)S(1)} %get-tuple-element.78), channel_id=1, source_target_pairs={{0,1},{1,0},{2,3},{3,2},{4,5},{5,4},{6,7},{7,6},{8,9},{9,8},{10,11... | collective-permute-start | bytes 2359304 | tf_op jit(solution)/shard_map/ppermute | solution.py:23
  83.5 7.8 %collective-permute-start.26 = (bf16[2,8,6144]{2,1,0:T(8,128)(2,1)S(1)}, bf16[2,8,6144]{2,1,0:T(8,128)(2,1)S(1)}, u32[]{:S(2)}, u32[]{:S(2)}) collective-permute-start(bf16[2,8,6144]{2,1,0:T(8,128)(2,1)S(1)} %get-tuple-element.90), channel_id=1, source_target_pairs={{0,2},{1,3},{2,0},{3,1},{4,6},{5,7},{6,4},{7,5},{8,10},{9,11},{10,... | collective-permute-start | bytes 589832 | tf_op jit(solution)/shard_map/ppermute | solution.py:23
  83.6 7.8 %collective-permute-start.27 = (bf16[2,8,6144]{2,1,0:T(8,128)(2,1)S(1)}, bf16[2,8,6144]{2,1,0:T(8,128)(2,1)S(1)}, u32[]{:S(2)}, u32[]{:S(2)}) collective-permute-start(bf16[2,8,6144]{2,1,0:T(8,128)(2,1)S(1)} %get-tuple-element.92), channel_id=1, source_target_pairs={{0,4},{1,5},{2,6},{3,7},{4,0},{5,1},{6,2},{7,3},{8,12},{9,13},{10,... | collective-permute-start | bytes 589832 | tf_op jit(solution)/shard_map/ppermute | solution.py:23
  84.6 15.4 %collective-permute-start.21 = (bf16[2,8,6144]{2,1,0:T(8,128)(2,1)S(1)}, bf16[2,8,6144]{2,1,0:T(8,128)(2,1)S(1)}, u32[]{:S(2)}, u32[]{:S(2)}) collective-permute-start(bf16[2,8,6144]{2,1,0:T(8,128)(2,1)S(1)} %get-tuple-element.80), channel_id=1, source_target_pairs={{0,2},{1,3},{2,0},{3,1},{4,6},{5,7},{6,4},{7,5},{8,10},{9,11},{10,... | collective-permute-start | bytes 589832 | tf_op jit(solution)/shard_map/ppermute | solution.py:23
  86.3 13.8 %collective-permute-start.22 = (bf16[2,8,6144]{2,1,0:T(8,128)(2,1)S(1)}, bf16[2,8,6144]{2,1,0:T(8,128)(2,1)S(1)}, u32[]{:S(2)}, u32[]{:S(2)}) collective-permute-start(bf16[2,8,6144]{2,1,0:T(8,128)(2,1)S(1)} %get-tuple-element.82), channel_id=1, source_target_pairs={{0,4},{1,5},{2,6},{3,7},{4,0},{5,1},{6,2},{7,3},{8,12},{9,13},{10,... | collective-permute-start | bytes 589832 | tf_op jit(solution)/shard_map/ppermute | solution.py:23
  91.5 5.4 %collective-permute-start.28 = (bf16[1,8,6144]{2,1,0:T(8,128)(2,1)S(1)}, bf16[1,8,6144]{2,1,0:T(8,128)(2,1)S(1)}, u32[]{:S(2)}, u32[]{:S(2)}) collective-permute-start(bf16[1,8,6144]{2,1,0:T(8,128)(2,1)S(1)} %get-tuple-element.94), channel_id=1, source_target_pairs={{0,4},{1,5},{2,6},{3,7},{4,0},{5,1},{6,2},{7,3},{8,12},{9,13},{10,... | collective-permute-start | bytes 294920 | tf_op jit(solution)/shard_map/ppermute | solution.py:23
  92.3 4.6 %collective-permute-start.29 = (bf16[1,8,6144]{2,1,0:T(8,128)(2,1)S(1)}, bf16[1,8,6144]{2,1,0:T(8,128)(2,1)S(1)}, u32[]{:S(2)}, u32[]{:S(2)}) collective-permute-start(bf16[1,8,6144]{2,1,0:T(8,128)(2,1)S(1)} %get-tuple-element.96), channel_id=1, source_target_pairs={{0,2},{1,3},{2,0},{3,1},{4,6},{5,7},{6,4},{7,5},{8,10},{9,11},{10,... | collective-permute-start | bytes 294920 | tf_op jit(solution)/shard_map/ppermute | solution.py:23
  97.0 8.4 %collective-permute-start.30 = (bf16[2,8,6144]{2,1,0:T(8,128)(2,1)S(1)}, bf16[2,8,6144]{2,1,0:T(8,128)(2,1)S(1)}, u32[]{:S(2)}, u32[]{:S(2)}) collective-permute-start(bf16[2,8,6144]{2,1,0:T(8,128)(2,1)S(1)} %shard_map.119), channel_id=1, source_target_pairs={{0,8},{8,0},{16,24},{24,16},{1,9},{9,1},{17,25},{25,17},{2,10},{10... | collective-permute-start | bytes 589832 | tf_op jit(solution)/shard_map/ppermute | solution.py:23
  100.2 4.7 %collective-permute-start.23 = (bf16[1,8,6144]{2,1,0:T(8,128)(2,1)S(1)}, bf16[1,8,6144]{2,1,0:T(8,128)(2,1)S(1)}, u32[]{:S(2)}, u32[]{:S(2)}) collective-permute-start(bf16[1,8,6144]{2,1,0:T(8,128)(2,1)S(1)} %get-tuple-element.84), channel_id=1, source_target_pairs={{0,4},{1,5},{2,6},{3,7},{4,0},{5,1},{6,2},{7,3},{8,12},{9,13},{10,... | collective-permute-start | bytes 294920 | tf_op jit(solution)/shard_map/ppermute | solution.py:23
  100.7 4.6 %collective-permute-start.24 = (bf16[1,8,6144]{2,1,0:T(8,128)(2,1)S(1)}, bf16[1,8,6144]{2,1,0:T(8,128)(2,1)S(1)}, u32[]{:S(2)}, u32[]{:S(2)}) collective-permute-start(bf16[1,8,6144]{2,1,0:T(8,128)(2,1)S(1)} %get-tuple-element.86), channel_id=1, source_target_pairs={{0,2},{1,3},{2,0},{3,1},{4,6},{5,7},{6,4},{7,5},{8,10},{9,11},{10,... | collective-permute-start | bytes 294920 | tf_op jit(solution)/shard_map/ppermute | solution.py:23
  105.4 6.4 %collective-permute-start.31 = (bf16[1,8,6144]{2,1,0:T(8,128)(2,1)S(1)}, bf16[1,8,6144]{2,1,0:T(8,128)(2,1)S(1)}, u32[]{:S(2)}, u32[]{:S(2)}) collective-permute-start(bf16[1,8,6144]{2,1,0:T(8,128)(2,1)S(1)} %get-tuple-element.98), channel_id=1, source_target_pairs={{0,16},{8,24},{16,0},{24,8},{1,17},{9,25},{17,1},{25,9},{2,18},{10... | collective-permute-start | bytes 294920 | tf_op jit(solution)/shard_map/ppermute | solution.py:23
  (5 other events, 38.7 us)

commit v4 on v1

--- a/solution.py
+++ b/solution.py
@@ -398,10 +398,10 @@
     total = C * E * token_rows
     held = len(gate_held)
     width = largest_part(cols, 768 if held else 384, 128)
-    columns = largest_part(features, 768 if held else 384, 128)
+    columns = largest_part(features, 512 if held else 384, 128)
     per_block = cols // width
     ahead = 3 if held else 2
-    down_ahead = 3 if held else 2
+    down_ahead = 4 if held else 2
     operands = [*packed, *gate_held, *up_held, gain]
     *outs, hidden = pl.pallas_call(
         functools.partial(expert_kernel, C, E, per_block, width, columns, held),

time: 112 us -> 112 us (level)
  no operation moved by 1% of the time
where the time goes in v4:
time: 112 us
  waiting for transfers between devices  44 us (39%)
  starting transfers between devices  33.8 us (30%)
  Pallas kernels  30.2 us (27%)
  local copies, waits for them, and re-layouts  2.9 us (3%)
    ppermute x32, waiting for transfers between devices, swap(): lax.ppermute(value, axis, [(i, i ^ mask) for i in range(lax.axis_size(axi...  44 us
    ppermute x32, starting transfers between devices, swap(): lax.ppermute(value, axis, [(i, i ^ mask) for i in range(lax.axis_size(axi...  33.8 us
    pallas_call x1, Pallas kernels, run_experts(): pl.pallas_call(functools.partial(expert_kernel, C, E, per_block, width, c...  21.3 us
    pallas_call x18, Pallas kernels, call(): pl.pallas_call(kernel, out_shape=out_shape, in_specs=in_specs, out_specs=...  4.5 us
    pallas_call x2, Pallas kernels, load_blocks(): pl.pallas_call(functools.partial(load_kernel, blocks), out_shape=[shape((...  4.35 us
    unnamed x10, local copies, waits for them, and re-layouts  2.9 us
  transfers between devices with their start and end apart: 32, of which 20 were waited for; matrix products, arithmetic and copies ran while one was open for 0% of the time, Pallas kernels for 5%

profile of v4, /device:TPU:0, one launch (start us, length us, event | category | flops | bytes accessed | tf_op | source)
XLA Modules:
  0.0 112.0 jit_solution(6566376983914279722)
XLA Ops:
  0.0 1.8 %shard_map.100 = (bf16[11,8,512]{2,1,0:T(8,128)(2,1)}, bf16[11,8,512]{2,1,0:T(8,128)(2,1)}, bf16[11,8,512]{2,1,0:T(8,128)(2,1)}, bf16[11,8,512]{2,1,0:T(8,128)(2,1)}) custom-call(bf16[64,384]{1,0:T(8,128)(2,1)} %queries_in.1, bf16[2,64,64]{2,1,0:T(8,128)(2,1)} %own_in.1, bf16[8,6144]{1,0:T(8,128)(2,1)} %residual_in.1), custom_call_target="tpu_custom_call" | custom-call | tf_op jit(solution)/shard_map/pallas_call | solution.py:27
  1.8 3.1 %collective-permute-start = (bf16[11,8,512]{2,1,0:T(8,128)(2,1)}, bf16[11,8,512]{2,1,0:T(8,128)(2,1)S(1)}, u32[]{:S(2)}, u32[]{:S(2)}) collective-permute-start(bf16[11,8,512]{2,1,0:T(8,128)(2,1)} %get-tuple-element.53), channel_id=1, source_target_pairs={{0,8},{8,0},{16,24},{24,16},{1,9},{9,1},{17,25},{25,17},{2,10},{10... | collective-permute-start | bytes 270344 | tf_op jit(solution)/shard_map/ppermute | solution.py:23
  4.9 2.6 %collective-permute-start.1 = (bf16[11,8,512]{2,1,0:T(8,128)(2,1)}, bf16[11,8,512]{2,1,0:T(8,128)(2,1)S(1)}, u32[]{:S(2)}, u32[]{:S(2)}) collective-permute-start(bf16[11,8,512]{2,1,0:T(8,128)(2,1)} %get-tuple-element.54), channel_id=1, source_target_pairs={{0,16},{8,24},{16,0},{24,8},{1,17},{9,25},{17,1},{25,9},{2,18},{10... | collective-permute-start | bytes 270344 | tf_op jit(solution)/shard_map/ppermute | solution.py:23
  10.5 4.4 %collective-permute-done.1.refs_2_.refs_6_ = bf16[11,8,512]{2,1,0:T(8,128)(2,1)S(1)} collective-permute-done((bf16[11,8,512]{2,1,0:T(8,128)(2,1)}, bf16[11,8,512]{2,1,0:T(8,128)(2,1)S(1)}, u32[]{:S(2)}, u32[]{:S(2)}) %collective-permute-start.1) | collective-permute-done | bytes 90144 | tf_op jit(solution)/shard_map/ppermute | solution.py:23
  16.3 1.4 %shard_map.103 = (bf16[4,4,8,1536]{3,2,1,0:T(8,128)(2,1)S(1)}, f32[4,4,8,1536]{3,2,1,0:T(8,128)S(1)}) custom-call(bf16[11,8,512]{2,1,0:T(8,128)(2,1)S(1)} %copy-done.1, bf16[11,8,512]{2,1,0:T(8,128)(2,1)S(1)} %collective-permute-done.refs_1_.refs_5_, bf16[11,8,512]{2,1,0:T(8,128)(2,1)S(1)} %collective-permute-done.1.refs_2_.refs_6_, ...), custom_call_target="tpu_custom_call" | custom-call | tf_op jit(solution)/shard_map/pallas_call | solution.py:27
  18.0 1.5 %collective-permute-done.4.received = bf16[4,4,8,1536]{3,2,1,0:T(8,128)(2,1)S(1)} collective-permute-done((bf16[4,4,8,1536]{3,2,1,0:T(8,128)(2,1)S(1)}, bf16[4,4,8,1536]{3,2,1,0:T(8,128)(2,1)S(1)}, u32[]{:S(2)}, u32[]{:S(2)}) %collective-permute-start.4) | collective-permute-done | bytes 393248 | tf_op jit(solution)/shard_map/ppermute | solution.py:23
  19.5 1.6 %collective-permute-start.5 = (bf16[4,8,1536]{2,1,0:T(8,128)(2,1)S(1)}, bf16[4,8,1536]{2,1,0:T(8,128)(2,1)S(1)}, u32[]{:S(2)}, u32[]{:S(2)}) collective-permute-start(bf16[4,8,1536]{2,1,0:T(8,128)(2,1)S(1)} %get-tuple-element.62), channel_id=1, source_target_pairs={{0,2},{1,3},{2,0},{3,1},{4,6},{5,7},{6,4},{7,5},{8,10},{9,11},{10,... | collective-permute-start | bytes 294920 | tf_op jit(solution)/shard_map/ppermute | solution.py:23
  21.1 1.5 %collective-permute-start.6 = (bf16[4,8,1536]{2,1,0:T(8,128)(2,1)S(1)}, bf16[4,8,1536]{2,1,0:T(8,128)(2,1)S(1)}, u32[]{:S(2)}, u32[]{:S(2)}) collective-permute-start(bf16[4,8,1536]{2,1,0:T(8,128)(2,1)S(1)} %get-tuple-element.63), channel_id=1, source_target_pairs={{0,4},{1,5},{2,6},{3,7},{4,0},{5,1},{6,2},{7,3},{8,12},{9,13},{10,... | collective-permute-start | bytes 294920 | tf_op jit(solution)/shard_map/ppermute | solution.py:23
  23.2 1.3 %collective-permute-done.5.refs_1_ = bf16[4,8,1536]{2,1,0:T(8,128)(2,1)S(1)} collective-permute-done((bf16[4,8,1536]{2,1,0:T(8,128)(2,1)S(1)}, bf16[4,8,1536]{2,1,0:T(8,128)(2,1)S(1)}, u32[]{:S(2)}, u32[]{:S(2)}) %collective-permute-start.5) | collective-permute-done | bytes 98336 | tf_op jit(solution)/shard_map/ppermute | solution.py:23
  24.5 2.4 %collective-permute-done.6.refs_2_ = bf16[4,8,1536]{2,1,0:T(8,128)(2,1)S(1)} collective-permute-done((bf16[4,8,1536]{2,1,0:T(8,128)(2,1)S(1)}, bf16[4,8,1536]{2,1,0:T(8,128)(2,1)S(1)}, u32[]{:S(2)}, u32[]{:S(2)}) %collective-permute-start.6) | collective-permute-done | bytes 98336 | tf_op jit(solution)/shard_map/ppermute | solution.py:23
  28.4 2.6 %collective-permute-start.8 = (bf16[4,8,1664]{2,1,0:T(8,128)(2,1)S(1)}, bf16[4,8,1664]{2,1,0:T(8,128)(2,1)S(1)}, u32[]{:S(2)}, u32[]{:S(2)}) collective-permute-start(bf16[4,8,1664]{2,1,0:T(8,128)(2,1)S(1)} %shard_map.105.refs_0_), channel_id=1, source_target_pairs={{0,16},{8,24},{16,0},{24,8},{1,17},{9,25},{17,1},{25,9},{2,18},{10... | collective-permute-start | bytes 319496 | tf_op jit(solution)/shard_map/ppermute | solution.py:23
  31.0 4.2 %collective-permute-done.8.refs_1_ = bf16[4,8,1664]{2,1,0:T(8,128)(2,1)S(1)} collective-permute-done((bf16[4,8,1664]{2,1,0:T(8,128)(2,1)S(1)}, bf16[4,8,1664]{2,1,0:T(8,128)(2,1)S(1)}, u32[]{:S(2)}, u32[]{:S(2)}) %collective-permute-start.8) | collective-permute-done | bytes 106528 | tf_op jit(solution)/shard_map/ppermute | solution.py:23
  37.5 3.5 %collective-permute-done.9.refs_2_ = bf16[4,8,1664]{2,1,0:T(8,128)(2,1)S(1)} collective-permute-done((bf16[4,8,1664]{2,1,0:T(8,128)(2,1)S(1)}, bf16[4,8,1664]{2,1,0:T(8,128)(2,1)S(1)}, u32[]{:S(2)}, u32[]{:S(2)}) %collective-permute-start.9) | collective-permute-done | bytes 106528 | tf_op jit(solution)/shard_map/ppermute | solution.py:23
  41.0 1.5 %collective-permute-done.10.refs_3_ = bf16[4,8,1664]{2,1,0:T(8,128)(2,1)S(1)} collective-permute-done((bf16[4,8,1664]{2,1,0:T(8,128)(2,1)S(1)}, bf16[4,8,1664]{2,1,0:T(8,128)(2,1)S(1)}, u32[]{:S(2)}, u32[]{:S(2)}) %collective-permute-start.10) | collective-permute-done | bytes 106528 | tf_op jit(solution)/shard_map/ppermute | solution.py:23
  44.8 1.9 %collective-permute-start.11 = (bf16[2,4,8,1664]{3,2,1,0:T(8,128)(2,1)S(1)}, bf16[2,4,8,1664]{3,2,1,0:T(8,128)(2,1)S(1)}, u32[]{:S(2)}, u32[]{:S(2)}) collective-permute-start(bf16[2,4,8,1664]{3,2,1,0:T(8,128)(2,1)S(1)} %get-tuple-element.66.refs_1_.refs_2_), channel_id=1, source_target_pairs={{0,2},{1,3},{2,0},{3,1},{4,6},{5,7},{6,4},{7,5},{8,10},{9,11},{10,... | collective-permute-start | bytes 638984 | tf_op jit(solution)/shard_map/ppermute | solution.py:23
  46.7 2.2 %shard_map.110 = (bf16[1344,1536]{1,0:T(8,128)(2,1)S(1)}, f32[8,128]{1,0:T(8,128)S(1)}) custom-call(bf16[1,1344,6144]{2,1,0:T(8,128)(2,1)} %bitcast.10, bf16[1,1344,6144]{2,1,0:T(8,128)(2,1)} %bitcast.13, bf16[2,4,8,1664]{3,2,1,0:T(8,128)(2,1)S(1)} %get-tuple-element.66.refs_1_.refs_2_), custom_call_target="tpu_custom_call" | custom-call | bytes 8257536 | tf_op jit(solution)/shard_map/pallas_call | solution.py:237
  49.0 1.7 %collective-permute-start.17 = (bf16[2,4,8,1664]{3,2,1,0:T(8,128)(2,1)S(1)}, bf16[2,4,8,1664]{3,2,1,0:T(8,128)(2,1)S(1)}, u32[]{:S(2)}, u32[]{:S(2)}) collective-permute-start(bf16[2,4,8,1664]{3,2,1,0:T(8,128)(2,1)S(1)} %get-tuple-element.72), channel_id=1, source_target_pairs={{0,4},{1,5},{2,6},{3,7},{4,0},{5,1},{6,2},{7,3},{8,12},{9,13},{10,... | collective-permute-start | bytes 638984 | tf_op jit(solution)/shard_map/ppermute | solution.py:23
  50.6 2.2 %shard_map.112 = (bf16[1344,1536]{1,0:T(8,128)(2,1)S(1)}, f32[8,128]{1,0:T(8,128)S(1)}) custom-call(bf16[1,1344,6144]{2,1,0:T(8,128)(2,1)} %bitcast.11, bf16[1,1344,6144]{2,1,0:T(8,128)(2,1)} %bitcast.14, bf16[2,4,8,1664]{3,2,1,0:T(8,128)(2,1)S(1)} %get-tuple-element.71.refs_2_), custom_call_target="tpu_custom_call" | custom-call | bytes 8257536 | tf_op jit(solution)/shard_map/pallas_call | solution.py:237
  53.0 1.9 %collective-permute-done.17.refs_4_ = bf16[2,4,8,1664]{3,2,1,0:T(8,128)(2,1)S(1)} collective-permute-done((bf16[2,4,8,1664]{3,2,1,0:T(8,128)(2,1)S(1)}, bf16[2,4,8,1664]{3,2,1,0:T(8,128)(2,1)S(1)}, u32[]{:S(2)}, u32[]{:S(2)}) %collective-permute-start.17) | collective-permute-done | bytes 213024 | tf_op jit(solution)/shard_map/ppermute | solution.py:23
  54.9 1.6 %collective-permute-done.16.refs_3_ = bf16[2,4,8,1664]{3,2,1,0:T(8,128)(2,1)S(1)} collective-permute-done((bf16[2,4,8,1664]{3,2,1,0:T(8,128)(2,1)S(1)}, bf16[2,4,8,1664]{3,2,1,0:T(8,128)(2,1)S(1)}, u32[]{:S(2)}, u32[]{:S(2)}) %collective-permute-start.16) | collective-permute-done | bytes 213024 | tf_op jit(solution)/shard_map/ppermute | solution.py:23
  56.6 2.4 %collective-permute-done.19.refs_3_ = bf16[8,4,8,1664]{3,2,1,0:T(8,128)(2,1)S(1)} collective-permute-done((bf16[8,4,8,1664]{3,2,1,0:T(8,128)(2,1)S(1)}, bf16[8,4,8,1664]{3,2,1,0:T(8,128)(2,1)S(1)}, u32[]{:S(2)}, u32[]{:S(2)}) %collective-permute-start.19) | collective-permute-done | bytes 852000 | tf_op jit(solution)/shard_map/ppermute | solution.py:23
  59.0 21.3 %shard_map.114 = (bf16[8,8,6144]{2,1,0:T(8,128)(2,1)S(1)}, bf16[8,8,6144]{2,1,0:T(8,128)(2,1)S(1)}, bf16[8,8,6144]{2,1,0:T(8,128)(2,1)S(1)}, bf16[8,8,6144]{2,1,0:T(8,128)(2,1)S(1)}, f32[8,6144]{1,0:T(8,128)S(1)}) custom-call(bf16[8,4,8,1664]{3,2,1,0:T(8,128)(2,1)S(1)} %shard_map.107.refs_0_, bf16[8,4,8,1664]{3,2,1,0:T(8,128)(2,1)S(1)} %shard_map.113.refs_1_, ...), custom_call_target="tpu_custom_call" | custom-call | flops 12683575296 | bytes 55836672 | tf_op jit(solution)/shard_map/pallas_call | solution.py:406
  80.9 1.8 %collective-permute-done.25.refs_1_ = bf16[8,8,6144]{2,1,0:T(8,128)(2,1)S(1)} collective-permute-done((bf16[8,8,6144]{2,1,0:T(8,128)(2,1)S(1)}, bf16[8,8,6144]{2,1,0:T(8,128)(2,1)S(1)}, u32[]{:S(2)}, u32[]{:S(2)}) %collective-permute-start.25) | collective-permute-done | bytes 786464 | tf_op jit(solution)/shard_map/ppermute | solution.py:23
  84.0 1.7 %collective-permute-start.21 = (bf16[2,8,6144]{2,1,0:T(8,128)(2,1)S(1)}, bf16[2,8,6144]{2,1,0:T(8,128)(2,1)S(1)}, u32[]{:S(2)}, u32[]{:S(2)}) collective-permute-start(bf16[2,8,6144]{2,1,0:T(8,128)(2,1)S(1)} %get-tuple-element.80), channel_id=1, source_target_pairs={{0,2},{1,3},{2,0},{3,1},{4,6},{5,7},{6,4},{7,5},{8,10},{9,11},{10,... | collective-permute-start | bytes 589832 | tf_op jit(solution)/shard_map/ppermute | solution.py:23
  85.6 1.6 %collective-permute-start.22 = (bf16[2,8,6144]{2,1,0:T(8,128)(2,1)S(1)}, bf16[2,8,6144]{2,1,0:T(8,128)(2,1)S(1)}, u32[]{:S(2)}, u32[]{:S(2)}) collective-permute-start(bf16[2,8,6144]{2,1,0:T(8,128)(2,1)S(1)} %get-tuple-element.82), channel_id=1, source_target_pairs={{0,4},{1,5},{2,6},{3,7},{4,0},{5,1},{6,2},{7,3},{8,12},{9,13},{10,... | collective-permute-start | bytes 589832 | tf_op jit(solution)/shard_map/ppermute | solution.py:23
  87.2 3.4 %collective-permute-done.26.refs_1_ = bf16[2,8,6144]{2,1,0:T(8,128)(2,1)S(1)} collective-permute-done((bf16[2,8,6144]{2,1,0:T(8,128)(2,1)S(1)}, bf16[2,8,6144]{2,1,0:T(8,128)(2,1)S(1)}, u32[]{:S(2)}, u32[]{:S(2)}) %collective-permute-start.26) | collective-permute-done | bytes 196640 | tf_op jit(solution)/shard_map/ppermute | solution.py:23
  91.7 1.6 %collective-permute-start.29 = (bf16[1,8,6144]{2,1,0:T(8,128)(2,1)S(1)}, bf16[1,8,6144]{2,1,0:T(8,128)(2,1)S(1)}, u32[]{:S(2)}, u32[]{:S(2)}) collective-permute-start(bf16[1,8,6144]{2,1,0:T(8,128)(2,1)S(1)} %get-tuple-element.96), channel_id=1, source_target_pairs={{0,2},{1,3},{2,0},{3,1},{4,6},{5,7},{6,4},{7,5},{8,10},{9,11},{10,... | collective-permute-start | bytes 294920 | tf_op jit(solution)/shard_map/ppermute | solution.py:23
  93.3 2.9 %collective-permute-done.28.refs_1_ = bf16[1,8,6144]{2,1,0:T(8,128)(2,1)S(1)} collective-permute-done((bf16[1,8,6144]{2,1,0:T(8,128)(2,1)S(1)}, bf16[1,8,6144]{2,1,0:T(8,128)(2,1)S(1)}, u32[]{:S(2)}, u32[]{:S(2)}) %collective-permute-start.28) | collective-permute-done | bytes 98336 | tf_op jit(solution)/shard_map/ppermute | solution.py:23
  96.4 3.1 %collective-permute-start.30 = (bf16[2,8,6144]{2,1,0:T(8,128)(2,1)S(1)}, bf16[2,8,6144]{2,1,0:T(8,128)(2,1)S(1)}, u32[]{:S(2)}, u32[]{:S(2)}) collective-permute-start(bf16[2,8,6144]{2,1,0:T(8,128)(2,1)S(1)} %shard_map.119), channel_id=1, source_target_pairs={{0,8},{8,0},{16,24},{24,16},{1,9},{9,1},{17,25},{25,17},{2,10},{10... | collective-permute-start | bytes 589832 | tf_op jit(solution)/shard_map/ppermute | solution.py:23
  101.3 3.0 %collective-permute-done.23.refs_1_ = bf16[1,8,6144]{2,1,0:T(8,128)(2,1)S(1)} collective-permute-done((bf16[1,8,6144]{2,1,0:T(8,128)(2,1)S(1)}, bf16[1,8,6144]{2,1,0:T(8,128)(2,1)S(1)}, u32[]{:S(2)}, u32[]{:S(2)}) %collective-permute-start.23) | collective-permute-done | bytes 98336 | tf_op jit(solution)/shard_map/ppermute | solution.py:23
  104.9 1.5 %collective-permute-start.31 = (bf16[1,8,6144]{2,1,0:T(8,128)(2,1)S(1)}, bf16[1,8,6144]{2,1,0:T(8,128)(2,1)S(1)}, u32[]{:S(2)}, u32[]{:S(2)}) collective-permute-start(bf16[1,8,6144]{2,1,0:T(8,128)(2,1)S(1)} %get-tuple-element.98), channel_id=1, source_target_pairs={{0,16},{8,24},{16,0},{24,8},{1,17},{9,25},{17,1},{25,9},{2,18},{10... | collective-permute-start | bytes 294920 | tf_op jit(solution)/shard_map/ppermute | solution.py:23
  106.4 4.9 %collective-permute-done.31 = bf16[1,8,6144]{2,1,0:T(8,128)(2,1)S(1)} collective-permute-done((bf16[1,8,6144]{2,1,0:T(8,128)(2,1)S(1)}, bf16[1,8,6144]{2,1,0:T(8,128)(2,1)S(1)}, u32[]{:S(2)}, u32[]{:S(2)}) %collective-permute-start.31) | collective-permute-done | bytes 98336 | tf_op jit(solution)/shard_map/ppermute | solution.py:23
  (67 shorter events, 17.7 us)
Async XLA Ops:
  1.8 8.7 %collective-permute-start = (bf16[11,8,512]{2,1,0:T(8,128)(2,1)}, bf16[11,8,512]{2,1,0:T(8,128)(2,1)S(1)}, u32[]{:S(2)}, u32[]{:S(2)}) collective-permute-start(bf16[11,8,512]{2,1,0:T(8,128)(2,1)} %get-tuple-element.53), channel_id=1, source_target_pairs={{0,8},{8,0},{16,24},{24,16},{1,9},{9,1},{17,25},{25,17},{2,10},{10... | collective-permute-start | bytes 270344 | tf_op jit(solution)/shard_map/ppermute | solution.py:23
  4.9 10.0 %collective-permute-start.1 = (bf16[11,8,512]{2,1,0:T(8,128)(2,1)}, bf16[11,8,512]{2,1,0:T(8,128)(2,1)S(1)}, u32[]{:S(2)}, u32[]{:S(2)}) collective-permute-start(bf16[11,8,512]{2,1,0:T(8,128)(2,1)} %get-tuple-element.54), channel_id=1, source_target_pairs={{0,16},{8,24},{16,0},{24,8},{1,17},{9,25},{17,1},{25,9},{2,18},{10... | collective-permute-start | bytes 270344 | tf_op jit(solution)/shard_map/ppermute | solution.py:23
  7.5 7.4 %collective-permute-start.2 = (bf16[11,8,512]{2,1,0:T(8,128)(2,1)}, bf16[11,8,512]{2,1,0:T(8,128)(2,1)S(1)}, u32[]{:S(2)}, u32[]{:S(2)}) collective-permute-start(bf16[11,8,512]{2,1,0:T(8,128)(2,1)} %get-tuple-element.55), channel_id=1, source_target_pairs={{0,24},{8,16},{16,8},{24,0},{1,25},{9,17},{17,9},{25,1},{2,26},{10... | collective-permute-start | bytes 270344 | tf_op jit(solution)/shard_map/ppermute | solution.py:23
  14.9 1.3 %collective-permute-start.3 = (bf16[4,8,8,128]{3,2,1,0:T(8,128)(2,1)S(1)}, bf16[4,8,8,128]{3,2,1,0:T(8,128)(2,1)S(1)}, u32[]{:S(2)}, u32[]{:S(2)}) collective-permute-start(bf16[4,8,8,128]{3,2,1,0:T(8,128)(2,1)S(1)} %get-tuple-element.58), channel_id=1, source_target_pairs={{0,1},{1,0},{2,3},{3,2},{4,5},{5,4},{6,7},{7,6},{8,9},{9,8},{10,11... | collective-permute-start | bytes 196616 | tf_op jit(solution)/shard_map/ppermute | solution.py:23
  17.7 1.8 %collective-permute-start.4 = (bf16[4,4,8,1536]{3,2,1,0:T(8,128)(2,1)S(1)}, bf16[4,4,8,1536]{3,2,1,0:T(8,128)(2,1)S(1)}, u32[]{:S(2)}, u32[]{:S(2)}) collective-permute-start(bf16[4,4,8,1536]{3,2,1,0:T(8,128)(2,1)S(1)} %get-tuple-element.60), channel_id=1, source_target_pairs={{0,1},{1,0},{2,3},{3,2},{4,5},{5,4},{6,7},{7,6},{8,9},{9,8},{10,11... | collective-permute-start | bytes 1179656 | tf_op jit(solution)/shard_map/ppermute | solution.py:23
  19.5 4.9 %collective-permute-start.5 = (bf16[4,8,1536]{2,1,0:T(8,128)(2,1)S(1)}, bf16[4,8,1536]{2,1,0:T(8,128)(2,1)S(1)}, u32[]{:S(2)}, u32[]{:S(2)}) collective-permute-start(bf16[4,8,1536]{2,1,0:T(8,128)(2,1)S(1)} %get-tuple-element.62), channel_id=1, source_target_pairs={{0,2},{1,3},{2,0},{3,1},{4,6},{5,7},{6,4},{7,5},{8,10},{9,11},{10,... | collective-permute-start | bytes 294920 | tf_op jit(solution)/shard_map/ppermute | solution.py:23
  21.1 5.8 %collective-permute-start.6 = (bf16[4,8,1536]{2,1,0:T(8,128)(2,1)S(1)}, bf16[4,8,1536]{2,1,0:T(8,128)(2,1)S(1)}, u32[]{:S(2)}, u32[]{:S(2)}) collective-permute-start(bf16[4,8,1536]{2,1,0:T(8,128)(2,1)S(1)} %get-tuple-element.63), channel_id=1, source_target_pairs={{0,4},{1,5},{2,6},{3,7},{4,0},{5,1},{6,2},{7,3},{8,12},{9,13},{10,... | collective-permute-start | bytes 294920 | tf_op jit(solution)/shard_map/ppermute | solution.py:23
  22.6 5.5 %collective-permute-start.7 = (bf16[4,8,1536]{2,1,0:T(8,128)(2,1)S(1)}, bf16[4,8,1536]{2,1,0:T(8,128)(2,1)S(1)}, u32[]{:S(2)}, u32[]{:S(2)}) collective-permute-start(bf16[4,8,1536]{2,1,0:T(8,128)(2,1)S(1)} %get-tuple-element.64), channel_id=1, source_target_pairs={{0,6},{1,7},{2,4},{3,5},{4,2},{5,3},{6,0},{7,1},{8,14},{9,15},{10,... | collective-permute-start | bytes 294920 | tf_op jit(solution)/shard_map/ppermute | solution.py:23
  28.4 6.8 %collective-permute-start.8 = (bf16[4,8,1664]{2,1,0:T(8,128)(2,1)S(1)}, bf16[4,8,1664]{2,1,0:T(8,128)(2,1)S(1)}, u32[]{:S(2)}, u32[]{:S(2)}) collective-permute-start(bf16[4,8,1664]{2,1,0:T(8,128)(2,1)S(1)} %shard_map.105.refs_0_), channel_id=1, source_target_pairs={{0,16},{8,24},{16,0},{24,8},{1,17},{9,25},{17,1},{25,9},{2,18},{10... | collective-permute-start | bytes 319496 | tf_op jit(solution)/shard_map/ppermute | solution.py:23
  35.2 7.4 %collective-permute-start.13 = (bf16[2,4,8,1664]{3,2,1,0:T(8,128)(2,1)S(1)}, bf16[2,4,8,1664]{3,2,1,0:T(8,128)(2,1)S(1)}, u32[]{:S(2)}, u32[]{:S(2)}) collective-permute-start(bf16[2,4,8,1664]{3,2,1,0:T(8,128)(2,1)S(1)} %shard_map.108), channel_id=1, source_target_pairs={{0,8},{8,0},{16,24},{24,16},{1,9},{9,1},{17,25},{25,17},{2,10},{10... | collective-permute-start | bytes 638984 | tf_op jit(solution)/shard_map/ppermute | solution.py:23
  35.8 5.2 %collective-permute-start.9 = (bf16[4,8,1664]{2,1,0:T(8,128)(2,1)S(1)}, bf16[4,8,1664]{2,1,0:T(8,128)(2,1)S(1)}, u32[]{:S(2)}, u32[]{:S(2)}) collective-permute-start(bf16[4,8,1664]{2,1,0:T(8,128)(2,1)S(1)} %shard_map.105.refs_0_), channel_id=1, source_target_pairs={{0,4},{1,5},{2,6},{3,7},{4,0},{5,1},{6,2},{7,3},{8,12},{9,13},{10,... | collective-permute-start | bytes 319496 | tf_op jit(solution)/shard_map/ppermute | solution.py:23
  37.0 5.6 %collective-permute-start.10 = (bf16[4,8,1664]{2,1,0:T(8,128)(2,1)S(1)}, bf16[4,8,1664]{2,1,0:T(8,128)(2,1)S(1)}, u32[]{:S(2)}, u32[]{:S(2)}) collective-permute-start(bf16[4,8,1664]{2,1,0:T(8,128)(2,1)S(1)} %collective-permute-done.8.refs_1_), channel_id=1, source_target_pairs={{0,2},{1,3},{2,0},{3,1},{4,6},{5,7},{6,4},{7,5},{8,10},{9,11},{10,... | collective-permute-start | bytes 319496 | tf_op jit(solution)/shard_map/ppermute | solution.py:23
  42.6 6.3 %collective-permute-start.14 = (bf16[4,8,1664]{2,1,0:T(8,128)(2,1)S(1)}, bf16[4,8,1664]{2,1,0:T(8,128)(2,1)S(1)}, u32[]{:S(2)}, u32[]{:S(2)}) collective-permute-start(bf16[4,8,1664]{2,1,0:T(8,128)(2,1)S(1)} %get-tuple-element.68), channel_id=1, source_target_pairs={{0,4},{1,5},{2,6},{3,7},{4,0},{5,1},{6,2},{7,3},{8,12},{9,13},{10,... | collective-permute-start | bytes 319496 | tf_op jit(solution)/shard_map/ppermute | solution.py:23
  43.0 5.9 %collective-permute-start.15 = (bf16[4,8,1664]{2,1,0:T(8,128)(2,1)S(1)}, bf16[4,8,1664]{2,1,0:T(8,128)(2,1)S(1)}, u32[]{:S(2)}, u32[]{:S(2)}) collective-permute-start(bf16[4,8,1664]{2,1,0:T(8,128)(2,1)S(1)} %get-tuple-element.69), channel_id=1, source_target_pairs={{0,2},{1,3},{2,0},{3,1},{4,6},{5,7},{6,4},{7,5},{8,10},{9,11},{10,... | collective-permute-start | bytes 319496 | tf_op jit(solution)/shard_map/ppermute | solution.py:23
  43.8 9.0 %collective-permute-start.12 = (bf16[2,4,8,1664]{3,2,1,0:T(8,128)(2,1)S(1)}, bf16[2,4,8,1664]{3,2,1,0:T(8,128)(2,1)S(1)}, u32[]{:S(2)}, u32[]{:S(2)}) collective-permute-start(bf16[2,4,8,1664]{3,2,1,0:T(8,128)(2,1)S(1)} %get-tuple-element.67.refs_2_), channel_id=1, source_target_pairs={{0,4},{1,5},{2,6},{3,7},{4,0},{5,1},{6,2},{7,3},{8,12},{9,13},{10,... | collective-permute-start | bytes 638984 | tf_op jit(solution)/shard_map/ppermute | solution.py:23
  44.8 8.0 %collective-permute-start.11 = (bf16[2,4,8,1664]{3,2,1,0:T(8,128)(2,1)S(1)}, bf16[2,4,8,1664]{3,2,1,0:T(8,128)(2,1)S(1)}, u32[]{:S(2)}, u32[]{:S(2)}) collective-permute-start(bf16[2,4,8,1664]{3,2,1,0:T(8,128)(2,1)S(1)} %get-tuple-element.66.refs_1_.refs_2_), channel_id=1, source_target_pairs={{0,2},{1,3},{2,0},{3,1},{4,6},{5,7},{6,4},{7,5},{8,10},{9,11},{10,... | collective-permute-start | bytes 638984 | tf_op jit(solution)/shard_map/ppermute | solution.py:23
  49.0 5.9 %collective-permute-start.17 = (bf16[2,4,8,1664]{3,2,1,0:T(8,128)(2,1)S(1)}, bf16[2,4,8,1664]{3,2,1,0:T(8,128)(2,1)S(1)}, u32[]{:S(2)}, u32[]{:S(2)}) collective-permute-start(bf16[2,4,8,1664]{3,2,1,0:T(8,128)(2,1)S(1)} %get-tuple-element.72), channel_id=1, source_target_pairs={{0,4},{1,5},{2,6},{3,7},{4,0},{5,1},{6,2},{7,3},{8,12},{9,13},{10,... | collective-permute-start | bytes 638984 | tf_op jit(solution)/shard_map/ppermute | solution.py:23
  50.6 5.8 %collective-permute-start.16 = (bf16[2,4,8,1664]{3,2,1,0:T(8,128)(2,1)S(1)}, bf16[2,4,8,1664]{3,2,1,0:T(8,128)(2,1)S(1)}, u32[]{:S(2)}, u32[]{:S(2)}) collective-permute-start(bf16[2,4,8,1664]{3,2,1,0:T(8,128)(2,1)S(1)} %get-tuple-element.71.refs_2_), channel_id=1, source_target_pairs={{0,2},{1,3},{2,0},{3,1},{4,6},{5,7},{6,4},{7,5},{8,10},{9,11},{10,... | collective-permute-start | bytes 638984 | tf_op jit(solution)/shard_map/ppermute | solution.py:23
  52.9 3.7 %collective-permute-start.18 = (bf16[8,4,8,1664]{3,2,1,0:T(8,128)(2,1)S(1)}, bf16[8,4,8,1664]{3,2,1,0:T(8,128)(2,1)S(1)}, u32[]{:S(2)}, u32[]{:S(2)}) collective-permute-start(bf16[8,4,8,1664]{3,2,1,0:T(8,128)(2,1)S(1)} %shard_map.107.refs_0_), channel_id=1, source_target_pairs={{0,1},{1,0},{2,3},{3,2},{4,5},{5,4},{6,7},{7,6},{8,9},{9,8},{10,11... | collective-permute-start | bytes 2555912 | tf_op jit(solution)/shard_map/ppermute | solution.py:23
  56.5 2.4 %collective-permute-start.19 = (bf16[8,4,8,1664]{3,2,1,0:T(8,128)(2,1)S(1)}, bf16[8,4,8,1664]{3,2,1,0:T(8,128)(2,1)S(1)}, u32[]{:S(2)}, u32[]{:S(2)}) collective-permute-start(bf16[8,4,8,1664]{3,2,1,0:T(8,128)(2,1)S(1)} %shard_map.113.refs_1_), channel_id=1, source_target_pairs={{0,1},{1,0},{2,3},{3,2},{4,5},{5,4},{6,7},{7,6},{8,9},{9,8},{10,11... | collective-permute-start | bytes 2555912 | tf_op jit(solution)/shard_map/ppermute | solution.py:23
  80.3 2.4 %collective-permute-start.25 = (bf16[8,8,6144]{2,1,0:T(8,128)(2,1)S(1)}, bf16[8,8,6144]{2,1,0:T(8,128)(2,1)S(1)}, u32[]{:S(2)}, u32[]{:S(2)}) collective-permute-start(bf16[8,8,6144]{2,1,0:T(8,128)(2,1)S(1)} %get-tuple-element.88), channel_id=1, source_target_pairs={{0,1},{1,0},{2,3},{3,2},{4,5},{5,4},{6,7},{7,6},{8,9},{9,8},{10,11... | collective-permute-start | bytes 2359304 | tf_op jit(solution)/shard_map/ppermute | solution.py:23
  80.5 3.3 %collective-permute-start.20 = (bf16[8,8,6144]{2,1,0:T(8,128)(2,1)S(1)}, bf16[8,8,6144]{2,1,0:T(8,128)(2,1)S(1)}, u32[]{:S(2)}, u32[]{:S(2)}) collective-permute-start(bf16[8,8,6144]{2,1,0:T(8,128)(2,1)S(1)} %get-tuple-element.78), channel_id=1, source_target_pairs={{0,1},{1,0},{2,3},{3,2},{4,5},{5,4},{6,7},{7,6},{8,9},{9,8},{10,11... | collective-permute-start | bytes 2359304 | tf_op jit(solution)/shard_map/ppermute | solution.py:23
  82.9 7.8 %collective-permute-start.26 = (bf16[2,8,6144]{2,1,0:T(8,128)(2,1)S(1)}, bf16[2,8,6144]{2,1,0:T(8,128)(2,1)S(1)}, u32[]{:S(2)}, u32[]{:S(2)}) collective-permute-start(bf16[2,8,6144]{2,1,0:T(8,128)(2,1)S(1)} %get-tuple-element.90), channel_id=1, source_target_pairs={{0,2},{1,3},{2,0},{3,1},{4,6},{5,7},{6,4},{7,5},{8,10},{9,11},{10,... | collective-permute-start | bytes 589832 | tf_op jit(solution)/shard_map/ppermute | solution.py:23
  83.0 7.8 %collective-permute-start.27 = (bf16[2,8,6144]{2,1,0:T(8,128)(2,1)S(1)}, bf16[2,8,6144]{2,1,0:T(8,128)(2,1)S(1)}, u32[]{:S(2)}, u32[]{:S(2)}) collective-permute-start(bf16[2,8,6144]{2,1,0:T(8,128)(2,1)S(1)} %get-tuple-element.92), channel_id=1, source_target_pairs={{0,4},{1,5},{2,6},{3,7},{4,0},{5,1},{6,2},{7,3},{8,12},{9,13},{10,... | collective-permute-start | bytes 589832 | tf_op jit(solution)/shard_map/ppermute | solution.py:23
  84.0 15.5 %collective-permute-start.21 = (bf16[2,8,6144]{2,1,0:T(8,128)(2,1)S(1)}, bf16[2,8,6144]{2,1,0:T(8,128)(2,1)S(1)}, u32[]{:S(2)}, u32[]{:S(2)}) collective-permute-start(bf16[2,8,6144]{2,1,0:T(8,128)(2,1)S(1)} %get-tuple-element.80), channel_id=1, source_target_pairs={{0,2},{1,3},{2,0},{3,1},{4,6},{5,7},{6,4},{7,5},{8,10},{9,11},{10,... | collective-permute-start | bytes 589832 | tf_op jit(solution)/shard_map/ppermute | solution.py:23
  85.6 13.8 %collective-permute-start.22 = (bf16[2,8,6144]{2,1,0:T(8,128)(2,1)S(1)}, bf16[2,8,6144]{2,1,0:T(8,128)(2,1)S(1)}, u32[]{:S(2)}, u32[]{:S(2)}) collective-permute-start(bf16[2,8,6144]{2,1,0:T(8,128)(2,1)S(1)} %get-tuple-element.82), channel_id=1, source_target_pairs={{0,4},{1,5},{2,6},{3,7},{4,0},{5,1},{6,2},{7,3},{8,12},{9,13},{10,... | collective-permute-start | bytes 589832 | tf_op jit(solution)/shard_map/ppermute | solution.py:23
  90.9 5.4 %collective-permute-start.28 = (bf16[1,8,6144]{2,1,0:T(8,128)(2,1)S(1)}, bf16[1,8,6144]{2,1,0:T(8,128)(2,1)S(1)}, u32[]{:S(2)}, u32[]{:S(2)}) collective-permute-start(bf16[1,8,6144]{2,1,0:T(8,128)(2,1)S(1)} %get-tuple-element.94), channel_id=1, source_target_pairs={{0,4},{1,5},{2,6},{3,7},{4,0},{5,1},{6,2},{7,3},{8,12},{9,13},{10,... | collective-permute-start | bytes 294920 | tf_op jit(solution)/shard_map/ppermute | solution.py:23
  91.7 4.6 %collective-permute-start.29 = (bf16[1,8,6144]{2,1,0:T(8,128)(2,1)S(1)}, bf16[1,8,6144]{2,1,0:T(8,128)(2,1)S(1)}, u32[]{:S(2)}, u32[]{:S(2)}) collective-permute-start(bf16[1,8,6144]{2,1,0:T(8,128)(2,1)S(1)} %get-tuple-element.96), channel_id=1, source_target_pairs={{0,2},{1,3},{2,0},{3,1},{4,6},{5,7},{6,4},{7,5},{8,10},{9,11},{10,... | collective-permute-start | bytes 294920 | tf_op jit(solution)/shard_map/ppermute | solution.py:23
  96.4 8.4 %collective-permute-start.30 = (bf16[2,8,6144]{2,1,0:T(8,128)(2,1)S(1)}, bf16[2,8,6144]{2,1,0:T(8,128)(2,1)S(1)}, u32[]{:S(2)}, u32[]{:S(2)}) collective-permute-start(bf16[2,8,6144]{2,1,0:T(8,128)(2,1)S(1)} %shard_map.119), channel_id=1, source_target_pairs={{0,8},{8,0},{16,24},{24,16},{1,9},{9,1},{17,25},{25,17},{2,10},{10... | collective-permute-start | bytes 589832 | tf_op jit(solution)/shard_map/ppermute | solution.py:23
  99.6 4.7 %collective-permute-start.23 = (bf16[1,8,6144]{2,1,0:T(8,128)(2,1)S(1)}, bf16[1,8,6144]{2,1,0:T(8,128)(2,1)S(1)}, u32[]{:S(2)}, u32[]{:S(2)}) collective-permute-start(bf16[1,8,6144]{2,1,0:T(8,128)(2,1)S(1)} %get-tuple-element.84), channel_id=1, source_target_pairs={{0,4},{1,5},{2,6},{3,7},{4,0},{5,1},{6,2},{7,3},{8,12},{9,13},{10,... | collective-permute-start | bytes 294920 | tf_op jit(solution)/shard_map/ppermute | solution.py:23
  100.2 4.6 %collective-permute-start.24 = (bf16[1,8,6144]{2,1,0:T(8,128)(2,1)S(1)}, bf16[1,8,6144]{2,1,0:T(8,128)(2,1)S(1)}, u32[]{:S(2)}, u32[]{:S(2)}) collective-permute-start(bf16[1,8,6144]{2,1,0:T(8,128)(2,1)S(1)} %get-tuple-element.86), channel_id=1, source_target_pairs={{0,2},{1,3},{2,0},{3,1},{4,6},{5,7},{6,4},{7,5},{8,10},{9,11},{10,... | collective-permute-start | bytes 294920 | tf_op jit(solution)/shard_map/ppermute | solution.py:23
  104.9 6.4 %collective-permute-start.31 = (bf16[1,8,6144]{2,1,0:T(8,128)(2,1)S(1)}, bf16[1,8,6144]{2,1,0:T(8,128)(2,1)S(1)}, u32[]{:S(2)}, u32[]{:S(2)}) collective-permute-start(bf16[1,8,6144]{2,1,0:T(8,128)(2,1)S(1)} %get-tuple-element.98), channel_id=1, source_target_pairs={{0,16},{8,24},{16,0},{24,8},{1,17},{9,25},{17,1},{25,9},{2,18},{10... | collective-permute-start | bytes 294920 | tf_op jit(solution)/shard_map/ppermute | solution.py:23
  (5 other events, 38.7 us)
